TPU v7x, 128 devices: a whole 4x4x4 slice. The times are simulated.
128 devices in a mesh: dp: 16 (over y_hi, x, core), seq: 8 (over z, y_lo).
Axes of the slice: x: 4, y: 4 (y_hi: 2, y_lo: 2; y = y_hi * 2 + y_lo), z: 4, core: 2. Of those that a mesh axis runs over, the one named last changes fastest.
Arguments:
- residual_in: bfloat16 [16, 1024, 768], P('dp', 'seq'), may hold values from -6 to 6
- cotangent: bfloat16 [16, 1024, 768], P('dp', 'seq'), may hold values from -6 to 6
- segments: int32 [16, 1024], P('dp'), may hold values from 0 to 2, as said below
- first_gain: bfloat16 [768], P('seq'), may hold values from 0.5 to 1.5
- first_shift: bfloat16 [768], P('seq'), may hold values from -1 to 1
- mixer_weight: bfloat16 [768, 2304], P('dp', 'seq'), may hold values from -0.21875 to 0.21875
- mixer_bias: bfloat16 [1536], P('seq'), may hold values from -1 to 1
- merge_weight: bfloat16 [768, 768], P('dp', 'seq'), may hold values from -1.25 to 1.25
- merge_bias: bfloat16 [768], P('seq'), may hold values from -1 to 1
- second_gain: bfloat16 [768], P('seq'), may hold values from 0.5 to 1.5
- second_shift: bfloat16 [768], P('seq'), may hold values from -1 to 1
- expand_weight: bfloat16 [768, 3072], P('dp', 'seq'), may hold values from -0.21875 to 0.21875
- expand_bias: bfloat16 [3072], P('seq'), may hold values from -1 to 1
- shrink_weight: bfloat16 [3072, 768], P('seq', 'dp'), may hold values from -0.109375 to 0.109375
- shrink_bias: bfloat16 [768], P('seq'), may hold values from -1 to 1
Outputs:
- hidden_out: bfloat16 [16, 1024, 768], P('dp', 'seq')
- grad_input: float32 [16, 1024, 768], P('dp', 'seq')
- grad_first_gain: float32 [768], P('seq')
- grad_first_shift: float32 [768], P('seq')
- grad_mixer_weight: float32 [768, 2304], P('dp', 'seq')
- grad_mixer_bias: float32 [1536], P('seq')
- grad_merge_weight: float32 [768, 768], P('dp', 'seq')
- grad_merge_bias: float32 [768], P('seq')
- grad_second_gain: float32 [768], P('seq')
- grad_second_shift: float32 [768], P('seq')
- grad_expand_weight: float32 [768, 3072], P('dp', 'seq')
- grad_expand_bias: float32 [3072], P('seq')
- grad_shrink_weight: float32 [3072, 768], P('seq', 'dp')
- grad_shrink_bias: float32 [768], P('seq')
Inputs may be any that keep to these rules, and one draw needn't show every extreme that they name: `segments`: each sequence holds exactly three documents numbered 0, 1, 2 in order; document 1 begins within the first 128 tokens and ends within the last 128 tokens.
All inputs are finite; a program needn't handle non-finite values.
Results may differ from a plain program's by a relative error of at most 0.019.
Values may be sent and summed in bfloat16 or wider, within the bound.
A program may use at most 128 MiB of HBM per device.

v0:
```python
import jax
import jax.numpy as jnp
from jax import lax
from jax.sharding import PartitionSpec as P

HEADS = 12
HEAD_DIM = 64


EPS = 1e-05
NEG = -1e30


def layer_norm(value, gain, shift):
    centre = jnp.mean(value, axis=-1, keepdims=True)
    centred = value - centre
    spread = jnp.mean(centred * centred, axis=-1, keepdims=True)
    return centred * lax.rsqrt(spread + EPS) * gain + shift


def gelu_tanh(value):
    inner = 0.7978845608028654 * (value + 0.044715 * value * value * value)
    return 0.5 * value * (1.0 + jnp.tanh(inner))


def col_sums(value):
    return jnp.sum(value.astype(jnp.float32), axis=0)


def own_slice(vector, seq_index, count):
    piece = vector.shape[0] // count
    return lax.dynamic_slice_in_dim(vector, seq_index * piece, piece, 0)


def body(
    residual_in,
    cotangent,
    segments,
    first_gain,
    first_shift,
    mixer_weight,
    mixer_bias,
    merge_weight,
    merge_bias,
    second_gain,
    second_shift,
    expand_weight,
    expand_bias,
    shrink_weight,
    shrink_bias,
):
    wide = (
        lax.all_gather(mixer_weight, "seq", axis=1, tiled=True),
        lax.all_gather(merge_weight, "seq", axis=1, tiled=True),
        lax.all_gather(expand_weight, "seq", axis=1, tiled=True),
        lax.all_gather(shrink_weight, "seq", axis=0, tiled=True),
        lax.all_gather(first_gain, "seq", axis=0, tiled=True),
        lax.all_gather(first_shift, "seq", axis=0, tiled=True),
        lax.all_gather(mixer_bias, "seq", axis=0, tiled=True),
        lax.all_gather(merge_bias, "seq", axis=0, tiled=True),
        lax.all_gather(second_gain, "seq", axis=0, tiled=True),
        lax.all_gather(second_shift, "seq", axis=0, tiled=True),
        lax.all_gather(expand_bias, "seq", axis=0, tiled=True),
        lax.all_gather(shrink_bias, "seq", axis=0, tiled=True),
    )
    mix_part, merge_part, expand_part, shrink_part = (wide[0], wide[1], wide[2], wide[3])
    vector_list = wide[4:]
    w_mix, merge_matrix, w_expand, w_shrink = (
        lax.all_gather(mix_part, "dp", axis=0, tiled=True),
        lax.all_gather(merge_part, "dp", axis=0, tiled=True),
        lax.all_gather(expand_part, "dp", axis=0, tiled=True),
        lax.all_gather(shrink_part, "dp", axis=1, tiled=True),
    )
    gain_a, shift_a, b_mix, b_merge, gain_b, shift_b, b_expand, b_shrink = [
        v.astype(jnp.float32) for v in vector_list
    ]
    rows = residual_in.shape[1]
    width = residual_in.shape[2]
    scale = HEAD_DIM ** (-0.5)
    seq_index = lax.axis_index("seq")
    seq_count = lax.axis_size("seq")
    x_rows = residual_in[0].astype(jnp.float32)
    normed_a, norm_a_back = jax.vjp(layer_norm, x_rows, gain_a, shift_a)
    first = normed_a.astype(jnp.bfloat16)
    full_bias = jnp.concatenate([b_mix[:width], jnp.zeros((width,), jnp.float32), b_mix[width:]])
    mixed = (jnp.dot(first, w_mix, preferred_element_type=jnp.float32) + full_bias).astype(
        jnp.bfloat16
    )
    query = mixed[:, :width]
    keys = mixed[:, width : 2 * width]
    values = mixed[:, 2 * width :]
    keys_all, values_all = (
        lax.all_gather(keys, "seq", axis=0, tiled=True),
        lax.all_gather(values, "seq", axis=0, tiled=True),
    )
    length = keys_all.shape[0]
    query_h = query.reshape(rows, HEADS, HEAD_DIM)
    keys_h = keys_all.reshape(length, HEADS, HEAD_DIM)
    values_h = values_all.reshape(length, HEADS, HEAD_DIM)
    start = seq_index * rows
    seg_all = segments[0]
    seg_rows = lax.dynamic_slice_in_dim(seg_all, start, rows, 0)
    query_pos = start + jnp.arange(rows, dtype=jnp.int32)
    key_pos = jnp.arange(length, dtype=jnp.int32)
    allowed = (query_pos[:, None] >= key_pos[None, :]) & (seg_rows[:, None] == seg_all[None, :])

    def masked_scores():
        raw = (
            jnp.einsum("qhd,khd->hqk", query_h, keys_h, preferred_element_type=jnp.float32) * scale
        )
        return jnp.where(allowed[None], raw, NEG)

    masked = masked_scores()
    top = jnp.max(masked, axis=-1, keepdims=True)
    log_total = top + jnp.log(jnp.sum(jnp.exp(masked - top), axis=-1, keepdims=True))
    probs = jnp.exp(masked - log_total)
    weights = probs.astype(jnp.bfloat16)
    attended = jnp.einsum("hqk,khd->qhd", weights, values_h, preferred_element_type=jnp.float32)
    attended = attended.reshape(rows, width).astype(jnp.bfloat16)
    middle = x_rows + jnp.dot(attended, merge_matrix, preferred_element_type=jnp.float32) + b_merge
    normed_b, norm_b_back = jax.vjp(layer_norm, middle, gain_b, shift_b)
    second = normed_b.astype(jnp.bfloat16)
    pre = jnp.dot(second, w_expand, preferred_element_type=jnp.float32) + b_expand
    activated, gelu_back = jax.vjp(gelu_tanh, pre)
    active = activated.astype(jnp.bfloat16)
    perceptron_output = jnp.dot(active, w_shrink, preferred_element_type=jnp.float32)
    result = middle + perceptron_output + b_shrink
    hidden_out = result.astype(jnp.bfloat16)[None]
    again = (
        lax.all_gather(mixer_weight, "seq", axis=1, tiled=True),
        lax.all_gather(merge_weight, "seq", axis=1, tiled=True),
        lax.all_gather(expand_weight, "seq", axis=1, tiled=True),
        lax.all_gather(shrink_weight, "seq", axis=0, tiled=True),
    )
    mix_back, merge_back, expand_pullback, shrink_back = (again[0], again[1], again[2], again[3])
    w_mix, merge_matrix, w_expand, w_shrink = (
        lax.all_gather(mix_back, "dp", axis=0, tiled=True),
        lax.all_gather(merge_back, "dp", axis=0, tiled=True),
        lax.all_gather(expand_pullback, "dp", axis=0, tiled=True),
        lax.all_gather(shrink_back, "dp", axis=1, tiled=True),
    )
    cot_low = cotangent[0]
    grad_out = cot_low.astype(jnp.float32)
    g_b_shrink = jnp.sum(grad_out, axis=0)
    g_shrink = jnp.dot(active.T, cot_low, preferred_element_type=jnp.float32)
    d_active = jnp.dot(cot_low, w_shrink.T, preferred_element_type=jnp.float32)
    d_pre = gelu_back(d_active)[0].astype(jnp.bfloat16)
    g_b_expand = col_sums(d_pre)
    g_expand = jnp.dot(second.T, d_pre, preferred_element_type=jnp.float32)
    d_second = jnp.dot(d_pre, w_expand.T, preferred_element_type=jnp.float32)
    d_mid_norm, g_gain_b, g_shift_b = norm_b_back(d_second)
    d_middle = grad_out + d_mid_norm
    d_branch = d_middle.astype(jnp.bfloat16)
    merge_bias_gradient = col_sums(d_branch)
    g_merge = jnp.dot(attended.T, d_branch, preferred_element_type=jnp.float32)
    d_attended = jnp.dot(d_branch, merge_matrix.T, preferred_element_type=jnp.float32).astype(
        jnp.bfloat16
    )
    d_att_h = d_attended.reshape(rows, HEADS, HEAD_DIM)
    probs = jnp.exp(masked_scores() - log_total)
    weights = probs.astype(jnp.bfloat16)
    d_weights = jnp.einsum("qhd,khd->hqk", d_att_h, values_h, preferred_element_type=jnp.float32)
    centre = jnp.sum(probs * d_weights, axis=-1, keepdims=True)
    d_scores = (probs * (d_weights - centre)).astype(jnp.bfloat16)
    d_query = (
        jnp.einsum("hqk,khd->qhd", d_scores, keys_h, preferred_element_type=jnp.float32) * scale
    )
    d_keys_part = (
        jnp.einsum("hqk,qhd->khd", d_scores, query_h, preferred_element_type=jnp.float32) * scale
    )
    d_values_part = jnp.einsum("hqk,qhd->khd", weights, d_att_h, preferred_element_type=jnp.float32)
    d_keys, d_values = (
        lax.psum_scatter(
            d_keys_part.reshape(length, width).astype(jnp.bfloat16),
            "seq",
            scatter_dimension=0,
            tiled=True,
        ).astype(jnp.float32),
        lax.psum_scatter(
            d_values_part.reshape(length, width).astype(jnp.bfloat16),
            "seq",
            scatter_dimension=0,
            tiled=True,
        ).astype(jnp.float32),
    )
    d_mixed = jnp.concatenate(
        [
            d_query.reshape(rows, width).astype(jnp.bfloat16),
            d_keys.astype(jnp.bfloat16),
            d_values.astype(jnp.bfloat16),
        ],
        axis=1,
    )
    g_mixer = jnp.dot(first.T, d_mixed, preferred_element_type=jnp.float32)
    mixed_sums = col_sums(d_mixed)
    g_b_mix = jnp.concatenate([mixed_sums[:width], mixed_sums[2 * width :]])
    d_first = jnp.dot(d_mixed, w_mix.T, preferred_element_type=jnp.float32)
    d_x_norm, g_gain_a, g_shift_a = norm_a_back(d_first)
    grad_input = (d_middle + d_x_norm)[None]
    partial_sums = (
        lax.psum_scatter(
            g_mixer.astype(jnp.bfloat16), "dp", scatter_dimension=0, tiled=True
        ).astype(jnp.float32),
        lax.psum_scatter(
            g_merge.astype(jnp.bfloat16), "dp", scatter_dimension=0, tiled=True
        ).astype(jnp.float32),
        lax.psum_scatter(
            g_expand.astype(jnp.bfloat16), "dp", scatter_dimension=0, tiled=True
        ).astype(jnp.float32),
        lax.psum_scatter(
            g_shrink.astype(jnp.bfloat16), "dp", scatter_dimension=1, tiled=True
        ).astype(jnp.float32),
    )
    finals = (
        lax.psum_scatter(
            partial_sums[0].astype(jnp.bfloat16), "seq", scatter_dimension=1, tiled=True
        ).astype(jnp.float32),
        lax.psum_scatter(
            partial_sums[1].astype(jnp.bfloat16), "seq", scatter_dimension=1, tiled=True
        ).astype(jnp.float32),
        lax.psum_scatter(
            partial_sums[2].astype(jnp.bfloat16), "seq", scatter_dimension=1, tiled=True
        ).astype(jnp.float32),
        lax.psum_scatter(
            partial_sums[3].astype(jnp.bfloat16), "seq", scatter_dimension=0, tiled=True
        ).astype(jnp.float32),
    )
    vectors = lax.psum(
        (
            g_gain_a,
            g_shift_a,
            g_b_mix,
            merge_bias_gradient,
            g_gain_b,
            g_shift_b,
            g_b_expand,
            g_b_shrink,
        ),
        ("dp", "seq"),
    )
    shards = [own_slice(v, seq_index, seq_count) for v in vectors]
    return (
        hidden_out,
        grad_input,
        shards[0],
        shards[1],
        finals[0],
        shards[2],
        finals[1],
        shards[3],
        shards[4],
        shards[5],
        finals[2],
        shards[6],
        finals[3],
        shards[7],
    )


def solution(mesh):
    return jax.shard_map(
        body,
        mesh=mesh,
        in_specs=(
            P("dp", "seq", None),
            P("dp", "seq", None),
            P("dp", None),
            P("seq"),
            P("seq"),
            P("dp", "seq"),
            P("seq"),
            P("dp", "seq"),
            P("seq"),
            P("seq"),
            P("seq"),
            P("dp", "seq"),
            P("seq"),
            P("seq", "dp"),
            P("seq"),
        ),
        out_specs=(
            P("dp", "seq", None),
            P("dp", "seq", None),
            P("seq"),
            P("seq"),
            P("dp", "seq"),
            P("seq"),
            P("dp", "seq"),
            P("seq"),
            P("seq"),
            P("seq"),
            P("dp", "seq"),
            P("seq"),
            P("seq", "dp"),
            P("seq"),
        ),
        check_vma=False,
    )
```

profile of v0, /device:TPU:1, one launch (start us, length us, event | category | flops | bytes accessed | tf_op | source)
XLA Modules:
  0.0 943.5 jit_solution(11894525032724974994)
XLA Ops:
  7.3 25.8 %all-gather = bf16[8,288,48]{1,2,0:T(8,128)(2,1)S(1)} all-gather(bf16[1,288,48]{1,2,0:T(8,128)(2,1)} %bitcast.143), channel_id=1, replica_groups=mesh['dp'=16,'seq'=8] {'seq'}, dimensions={0}, use_global_device_ids=true | all-gather | bytes 248832 | tf_op jit(solution)/shard_map/all_gather | solution.py:53
  37.8 26.7 %all-reduce.8 = (bf16[1536]{0:T(1024)(128)(2,1)S(1)}, bf16[768]{0:T(1024)(128)(2,1)S(1)}, bf16[768]{0:T(1024)(128)(2,1)S(1)}, bf16[768]{0:T(1024)(128)(2,1)S(1)}...) all-reduce(bf16[1536]{0:T(1024)(128)(2,1)S(1)} %dynamic-update-slic, ...), channel_id=1, replica_groups=mesh['dp'=16,'seq'=8] {'seq'}, use_global_device_ids=true, to_apply=%add.2 | all-reduce | flops 6144 | bytes 24576
  65.0 30.2 %all-gather.10.cloned.1.call-done = bf16[768,2304]{1,0:T(8,128)(2,1)} async-done(((bf16[48,2304]{1,0:T(8,128)(2,1)}), bf16[768,2304]{1,0:T(8,128)(2,1)}) %all-gather.10.cloned.1.call-update) | async-done | bytes 3538960 | tf_op jit(solution)/shard_map/all_gather | solution.py:69
  99.5 23.2 %all-gather.1 = bf16[8,96,48]{1,2,0:T(8,128)(2,1)S(1)} all-gather(bf16[1,96,48]{1,2,0:T(8,128)(2,1)S(1)} %bitcast.145), channel_id=1, replica_groups=mesh['dp'=16,'seq'=8] {'seq'}, dimensions={0}, use_global_device_ids=true | all-gather | bytes 82944 | tf_op jit(solution)/shard_map/all_gather | solution.py:54
  123.6 26.9 %all_gather.74 = bf16[48,3072]{1,0:T(8,128)(2,1)} all-gather(bf16[48,384]{1,0:T(8,128)(2,1)S(1)} %copy-done.23), channel_id=1, replica_groups=mesh['dp'=16,'seq'=8] {'seq'}, dimensions={1}, use_global_device_ids=true | all-gather | bytes 331776 | tf_op jit(solution)/shard_map/all_gather | solution.py:55
  150.6 27.1 %all_gather.77 = bf16[3072,48]{0,1:T(8,128)(2,1)} all-gather(bf16[384,48]{0,1:T(8,128)(2,1)S(1)} %copy-done.24), channel_id=1, replica_groups=mesh['dp'=16,'seq'=8] {'seq'}, dimensions={0}, use_global_device_ids=true | all-gather | bytes 331776 | tf_op jit(solution)/shard_map/all_gather | solution.py:56
  177.8 21.0 %all-gather.2 = bf16[8,1,384]{2,1,0:T(2,128)(2,1)S(1)} all-gather(bf16[1,1,384]{2,1,0:T(2,128)(2,1)S(1)} %reshape.212), channel_id=1, replica_groups=mesh['dp'=16,'seq'=8] {'seq'}, dimensions={0}, use_global_device_ids=true | all-gather | bytes 6912 | tf_op jit(solution)/shard_map/all_gather | solution.py:63
  210.8 30.5 %all-gather.16.cloned.1.call-done = bf16[768,768]{1,0:T(8,128)(2,1)} async-done(((bf16[48,768]{1,0:T(8,128)(2,1)}), bf16[768,768]{1,0:T(8,128)(2,1)}) %all-gather.16.cloned.1.call-update) | async-done | bytes 1179664 | tf_op jit(solution)/shard_map/all_gather | solution.py:70
  243.8 56.5 %all-gather.18.cloned.1.call-done = bf16[768,3072]{1,0:T(8,128)(2,1)} async-done(((bf16[48,3072]{1,0:T(8,128)(2,1)}), bf16[768,3072]{1,0:T(8,128)(2,1)}) %all-gather.18.cloned.1.call-update) | async-done | bytes 4718608 | tf_op jit(solution)/shard_map/all_gather | solution.py:71
  303.6 55.8 %all-gather.20.cloned.1.call-done = bf16[3072,768]{0,1:T(8,128)(2,1)} async-done(((bf16[3072,48]{0,1:T(8,128)(2,1)}), bf16[3072,768]{0,1:T(8,128)(2,1)}) %all-gather.20.cloned.1.call-update) | async-done | bytes 4718608 | tf_op jit(solution)/shard_map/all_gather | solution.py:72
  359.3 5.3 convert_reduce_fusion
  372.9 5.8 convolution_convert_fusion.3
  394.4 4.8 convolution_convert_fusion.1
  399.3 34.9 %reduce-scatter.25.cloned.1.call-done = bf16[48,768]{1,0:T(8,128)(2,1)} async-done(((bf16[768,768]{1,0:T(8,128)(2,1)}), bf16[48,768]{1,0:T(8,128)(2,1)}) %reduce-scatter.25.cloned.1.call-update) | async-done | bytes 73744 | tf_op jit(solution)/shard_map/reduce_scatter | solution.py:204
  436.1 5.0 convolution_convert_fusion
  444.4 34.3 %reduce-scatter.33.cloned.1.call-done = bf16[128,768]{1,0:T(8,128)(2,1)} async-done(((bf16[1024,768]{1,0:T(8,128)(2,1)}), bf16[128,768]{1,0:T(8,128)(2,1)}) %reduce-scatter.33.cloned.1.call-update) | async-done | bytes 196624
  479.9 44.9 %reduce-scatter.31.cloned.1.call-done = bf16[128,768]{1,0:T(8,128)(2,1)} async-done(((bf16[1024,768]{1,0:T(8,128)(2,1)}), bf16[128,768]{1,0:T(8,128)(2,1)}) %reduce-scatter.31.cloned.1.call-update) | async-done | bytes 196624
  530.7 82.7 %reduce-scatter.27.cloned.1.call-done = bf16[48,3072]{1,0:T(8,128)(2,1)} async-done(((bf16[768,3072]{1,0:T(8,128)(2,1)}), bf16[48,3072]{1,0:T(8,128)(2,1)}) %reduce-scatter.27.cloned.1.call-update) | async-done | bytes 294928 | tf_op jit(solution)/shard_map/reduce_scatter | solution.py:207
  616.0 4.8 fusion.15
  620.7 27.2 %reduce-scatter.37.cloned.1.call-done = bf16[96,48]{1,0:T(8,128)(2,1)} async-done(((bf16[768,48]{1,0:T(8,128)(2,1)}), bf16[96,48]{1,0:T(8,128)(2,1)}) %reduce-scatter.37.cloned.1.call-update) | async-done | bytes 9232
  653.0 84.8 %reduce-scatter.29.cloned.1.call-done = bf16[3072,48]{0,1:T(8,128)(2,1)} async-done(((bf16[3072,768]{0,1:T(8,128)(2,1)}), bf16[3072,48]{0,1:T(8,128)(2,1)}) %reduce-scatter.29.cloned.1.call-update) | async-done | bytes 294928 | tf_op jit(solution)/shard_map/reduce_scatter | solution.py:210
  740.4 77.0 %reduce-scatter.23.cloned.1.call-done = bf16[48,2304]{1,0:T(8,128)(2,1)} async-done(((bf16[768,2304]{1,0:T(8,128)(2,1)}), bf16[48,2304]{1,0:T(8,128)(2,1)}) %reduce-scatter.23.cloned.1.call-update) | async-done | bytes 221200 | tf_op jit(solution)/shard_map/reduce_scatter | solution.py:201
  820.5 67.3 %all-reduce.7 = (f32[768]{0:T(1024)S(1)}, f32[768]{0:T(1024)S(1)}, f32[1536]{0:T(1024)S(1)}, f32[768]{0:T(1024)S(1)}, f32[768]{0:T(1024)S(1)}, /*index=5*/f32[76...) all-reduce(f32[768]{0:T(1024)S(1)} %get-tuple-element.16, ...), channel_id=1, replica_groups=mesh['dp'=16,'seq'=8] {'dp','seq'}, use_global_device_ids=true, to_apply=%region_14.15 | all-reduce | flops 9216 | bytes 73728 | tf_op jit(solution)/shard_map/psum | solution.py:228
  897.4 38.0 %reduce-scatter.35.cloned.1.call-done = bf16[288,48]{1,0:T(8,128)(2,1)} async-done(((bf16[2304,48]{1,0:T(8,128)(2,1)}), bf16[288,48]{1,0:T(8,128)(2,1)}) %reduce-scatter.35.cloned.1.call-update) | async-done | bytes 27664
  (240 shorter events, 86.6 us)
Async XLA Ops:
  7.3 87.8 %all-gather.10.cloned.1.call-start = ((), (), s32[]{:S(2)}) async-start(), calls=%async_computation.10 | async-start | bytes 3760128 | tf_op jit(solution)/shard_map/all_gather | solution.py:69
  34.2 166.3 %all-gather.12.cloned.1.call-start = ((), (), s32[]{:S(2)}) async-start(), calls=%async_computation.11 | async-start | bytes 1769472 | tf_op jit(solution)/shard_map/all_gather | solution.py:94
  97.9 101.6 %copy-start.37 = (s32[1,1024]{1,0:T(1,128)S(1)}, s32[1,1024]{1,0:T(1,128)}, u32[]{:S(2)}) copy-start(s32[1,1024]{1,0:T(1,128)} %param.17) | copy-start | bytes 12292
  98.7 103.6 %all-gather.14.cloned.1.call-start = ((), (), s32[]{:S(2)}) async-start(), calls=%async_computation.12 | async-start | bytes 1769472 | tf_op jit(solution)/shard_map/all_gather | solution.py:93
  99.4 141.9 %all-gather.16.cloned.1.call-start = ((), (), s32[]{:S(2)}) async-start(), calls=%async_computation.13 | async-start | bytes 1253376 | tf_op jit(solution)/shard_map/all_gather | solution.py:70
  123.6 176.7 %all-gather.18.cloned.1.call-start = ((), (), s32[]{:S(2)}) async-start(), calls=%async_computation.14 | async-start | bytes 5013504 | tf_op jit(solution)/shard_map/all_gather | solution.py:71
  150.5 208.8 %all-gather.20.cloned.1.call-start = ((), (), s32[]{:S(2)}) async-start(), calls=%async_computation.15 | async-start | bytes 5013504 | tf_op jit(solution)/shard_map/all_gather | solution.py:72
  177.7 256.5 %reduce-scatter.25.cloned.1.call-start = ((), (), s32[]{:S(2)}) async-start(), calls=%async_computation.17 | async-start | bytes 1253376 | tf_op jit(solution)/shard_map/reduce_scatter | solution.py:204
  210.8 89.5 %copy-start.18 = (bf16[12,64,128]{2,1,0:T(8,128)(2,1)}, bf16[12,64,128]{2,1,0:T(8,128)(2,1)S(1)}, u32[]{:S(2)}) copy-start(bf16[12,64,128]{2,1,0:T(8,128)(2,1)S(1)} %convolution_convert_fusion.6) | copy-start | bytes 589828
  370.3 108.5 %reduce-scatter.33.cloned.1.call-start = ((), (), s32[]{:S(2)}) async-start(), calls=%async_computation.21 | async-start | bytes 1769472
  381.4 143.5 %reduce-scatter.31.cloned.1.call-start = ((), (), s32[]{:S(2)}) async-start(), calls=%async_computation.20 | async-start | bytes 1769472
  394.4 219.1 %reduce-scatter.27.cloned.1.call-start = ((), (), s32[]{:S(2)}) async-start(), calls=%async_computation.18 | async-start | bytes 5013504 | tf_op jit(solution)/shard_map/reduce_scatter | solution.py:207
  399.3 248.6 %reduce-scatter.37.cloned.1.call-start = ((), (), s32[]{:S(2)}) async-start(), calls=%async_computation.23 | async-start | bytes 221184
  436.0 301.8 %reduce-scatter.29.cloned.1.call-start = ((), (), s32[]{:S(2)}) async-start(), calls=%async_computation.19 | async-start | bytes 5013504 | tf_op jit(solution)/shard_map/reduce_scatter | solution.py:210
  441.1 84.8 %copy-start.26 = (f32[128]{0:T(128)S(1)}, f32[128]{0:T(128)}, u32[]{:S(2)}) copy-start(f32[128]{0:T(128)} %copy-done.25) | copy-start | bytes 1540
  441.1 84.8 %copy-start.33 = (f32[128]{0:T(128)S(1)}, f32[128]{0:T(128)}, u32[]{:S(2)}) copy-start(f32[128]{0:T(128)} %copy-done.32) | copy-start | bytes 1540
  441.1 376.3 %reduce-scatter.23.cloned.1.call-start = ((), (), s32[]{:S(2)}) async-start(), calls=%async_computation.16 | async-start | bytes 3760128 | tf_op jit(solution)/shard_map/reduce_scatter | solution.py:201
  530.0 85.9 %copy-start.6 = (f32[128,3072]{1,0:T(8,128)S(1)}, f32[128,3072]{1,0:T(8,128)}, u32[]{:S(2)}) copy-start(f32[128,3072]{1,0:T(8,128)} %copy-done.5) | copy-start | bytes 4718596
  530.0 362.5 %reduce-scatter.39.cloned.1.call-start = ((), (), s32[]{:S(2)}) async-start(), calls=%async_computation.24 | async-start | bytes 884736
  615.6 280.1 %reduce-scatter.41.cloned.1.call-start = ((), (), s32[]{:S(2)}) async-start(), calls=%async_computation.25 | async-start | bytes 884736
  653.0 87.0 %copy-start.43 = (f32[128]{0:T(128)S(1)}, f32[128]{0:T(128)}, u32[]{:S(2)}) copy-start(f32[128]{0:T(128)} %copy-done.42) | copy-start | bytes 1540
  739.9 195.4 %reduce-scatter.35.cloned.1.call-start = ((), (), s32[]{:S(2)}) async-start(), calls=%async_computation.22 | async-start | bytes 663552
  740.3 80.2 %copy-start.29 = (f32[768]{0:T(1024)S(1)}, f32[768]{0:T(1024)}, u32[]{:S(2)}) copy-start(f32[768]{0:T(1024)} %get-tuple-element.14) | copy-start | bytes 9220
  740.3 80.2 %copy-start.30 = (f32[768]{0:T(1024)S(1)}, f32[768]{0:T(1024)}, u32[]{:S(2)}) copy-start(f32[768]{0:T(1024)} %get-tuple-element.18) | copy-start | bytes 9220
  (46 other events, 1256.9 us)
Sparse Core Ops, SparseCore 0:
  34.3 60.7 all-gather.9
  98.8 44.1 all-gather.11
  145.3 48.8 all-gather.13
  197.0 44.2 all-gather.15
  243.6 56.6 all-gather.17
  302.6 56.7 all-gather.19
  370.4 63.7 reduce-scatter.24
  436.8 41.9 reduce-scatter.32
  481.3 43.4 reduce-scatter.30
  529.3 84.1 reduce-scatter.26
  615.8 32.0 reduce-scatter.36
  652.4 85.3 reduce-scatter.28
  741.9 75.4 reduce-scatter.22
  819.6 35.1 reduce-scatter.38
  857.2 38.4 reduce-scatter.40
  898.0 37.3 reduce-scatter.34
where the time goes:
time: 949 us; the launch traced here: 944 us
  waiting for transfers between devices  599 us (63%)
  blocking collectives  218 us (23%)
  matrix products  59.6 us (6%)
  local copies, waits for them, and re-layouts  36.6 us (4%)
  between operations  16.1 us (2%)
  other arithmetic  12.5 us (1%)
    unnamed x22, waiting for transfers between devices  147 us
    reduce_scatter x1, waiting for transfers between devices, body(): lax.psum_scatter(g_shrink.astype(jnp.bfloat16), 'dp', scatter_dimension=1...  84.8 us
    reduce_scatter x1, waiting for transfers between devices, body(): lax.psum_scatter(g_expand.astype(jnp.bfloat16), 'dp', scatter_dimension=0...  82.7 us
    reduce_scatter x1, waiting for transfers between devices, body(): lax.psum_scatter(g_mixer.astype(jnp.bfloat16), 'dp', scatter_dimension=0,...  77 us
    psum x1, blocking collectives, body(): lax.psum((g_gain_a, g_shift_a, g_b_mix, merge_bias_gradient, g_gain_b, g_...  67.3 us
    all_gather x1, waiting for transfers between devices, body(): lax.all_gather(expand_part, 'dp', axis=0, tiled=True)  56.5 us
    all_gather x1, waiting for transfers between devices, body(): lax.all_gather(shrink_part, 'dp', axis=1, tiled=True)  55.8 us
    reduce_scatter x1, waiting for transfers between devices, body(): lax.psum_scatter(g_merge.astype(jnp.bfloat16), 'dp', scatter_dimension=0,...  34.9 us
  transfers between devices with their start and end apart: 16, of which 13 were waited for; matrix products, arithmetic and copies ran while one was open for 10% of the time, Pallas kernels for 0%

commit v1 on v0

v1 whole, which is shorter than its diff:
```python
import functools
import types

import jax
import jax.numpy as jnp
from jax import lax
from jax.experimental import pallas as pl
from jax.experimental.pallas import tpu as pltpu
from jax.sharding import PartitionSpec as P


D = 768
HD = 64
TOK = 128
SHARD = 384
EPS = 1e-05
NEG = -1e30
MESH = pl.DeviceIdType.MESH
BF = jnp.bfloat16
F32 = jnp.float32
ORDERS = (("x", "y", "z"), ("y", "z", "x"), ("z", "x", "y"))
FIRST_GAIN, FIRST_SHIFT, MIXER_BIAS, MERGE_BIAS, SECOND_GAIN, SECOND_SHIFT, SHRINK_BIAS, EXPAND_BIAS = 0, 1, 2, 4, 5, 6, 7, 8


def place_of():
    dp, seq = lax.axis_index("dp"), lax.axis_index("seq")
    return types.SimpleNamespace(
        x=lax.rem(lax.div(dp, 2), 4),
        yh=lax.div(dp, 8),
        yl=lax.rem(seq, 2),
        z=lax.div(seq, 2),
        c=lax.rem(dp, 2),
    )


def moved(at, **to):
    new = types.SimpleNamespace(**vars(at))
    for name, value in to.items():
        setattr(new, name, value)
    return new


def shifted(at, axis, d):
    d = d % 4
    if axis == "x":
        return moved(at, x=lax.rem(at.x + d, 4))
    if axis == "z":
        return moved(at, z=lax.rem(at.z + d, 4))
    y = lax.rem(at.yh * 2 + at.yl + d, 4)
    return moved(at, yh=lax.div(y, 2), yl=lax.rem(y, 2))


def device(at):
    return (at.yh * 8 + at.x * 2 + at.c, at.z * 2 + at.yl)


def nn(a, b):
    return jnp.dot(a, b, preferred_element_type=F32)


def nt(a, b):
    return lax.dot_general(a, b, (((1,), (1,)), ((), ())), preferred_element_type=F32)


def remote(src, dst, send, recv, to):
    return pltpu.make_async_remote_copy(
        src_ref=src, dst_ref=dst, send_sem=send, recv_sem=recv, device_id=device(to), device_id_type=MESH
    )


def part(ref, at, t, full, lead, core=True):
    every = slice(None)
    where = [every if "z" in full else at.z]
    where += [every, every] if "y" in full else [at.yl, at.yh]
    where += [every if "x" in full else at.x]
    if core:
        where += [at.c]
    return ref.at[tuple(lead) + tuple(where) + (pl.ds(16 * t, 16), every)]


def norm_parts(v):
    centred = v - jnp.mean(v, axis=-1, keepdims=True)
    rstd = lax.rsqrt(jnp.mean(centred * centred, axis=-1, keepdims=True) + EPS)
    return centred * rstd, rstd


def norm_back(dy, gain, normed, rstd):
    dn = dy * gain
    return rstd * (
        dn
        - jnp.mean(dn, axis=-1, keepdims=True)
        - normed * jnp.mean(dn * normed, axis=-1, keepdims=True)
    )


def col_sums(v):
    return jnp.sum(v.astype(F32), axis=0, keepdims=True)


def kernel(
    x_ref, cot_ref, seg_ref, wsh_ref, vec_ref,
    hidden_ref, gin_ref, gmix_ref, gmerge_ref, gexp_ref, gshr_ref, vout_ref,
    w, g, r0, rb1, rb2, rb3, vecs, segs, first_s, mix_s, q_send, kv_send, q_all, kv_all, kvt, lse_s,
    att_send, att_recv, att_s, mid_s, n2_s, sect_s, cott_s, mlp_s, dsec_s, dbr_s, fat_s,
    do_send, do_recv, dkv_s, dkv_sib, dkv_got, dq_send, dq_recv, dkv_send, dkv_recv, dmix_s, dfirst_s,
    vg, vr, vsum, vx,
    ag_ss, ag_rs, sib_ss, sib_rs, vec_ss, vec_rs, one_ss, one_rs, a2a_ss, a2a_rs, kvs_ss, kvs_rs,
    back_ss, back_rs, rs0_ss, rs0_rs, rs_ss, rs_rs, vred_ss, vred_rs, vx_ss, vx_rs, loc,
):
    me = place_of()
    sib = moved(me, c=1 - me.c)
    swap = moved(me, yl=me.c, c=me.yl)
    here = me.yl == me.c
    peers = [shifted(me, a, d) for a in "xyz" for d in (1, 2, 3)] + [sib]
    peers += [moved(shifted(me, "z", d), yl=1 - me.yl) for d in (1, 2, 3)]
    peers += [moved(shifted(me, "z", d), yl=1 - me.yl, c=1 - me.c) for d in range(4)]
    barrier = pltpu.get_barrier_semaphore()
    for p in peers:
        pl.semaphore_signal(barrier, inc=1, device_id=device(p), device_id_type=MESH)
    pl.semaphore_wait(barrier, len(peers))

    pending = []

    def start(copy):
        copy.start()
        pending.append(copy)

    GROUPS = ((0, 1), (1, 2))

    def lead(group):
        first, count = GROUPS[group]
        return (pl.ds(first, count),)

    def ag(group, t, stage, d):
        order = ORDERS[t]
        at = part(w, me, t, order[:stage], lead(group))
        sems = (ag_ss.at[group, t, stage, d - 1], ag_rs.at[group, t, stage, d - 1])
        return remote(at, at, *sems, shifted(me, order[stage], d))

    def ag_wait(group, t, stage, d):
        order = ORDERS[t]
        at = part(w, shifted(me, order[stage], -d), t, order[:stage], lead(group))
        sems = (ag_ss.at[group, t, stage, d - 1], ag_rs.at[group, t, stage, d - 1])
        remote(at, at, *sems, shifted(me, order[stage], d)).wait_recv()

    def hand(group, t, d, mine):
        order = ORDERS[t]
        at = shifted(me if mine else sib, order[2], -d)
        view = part(w, at, t, order[:2], lead(group))
        return remote(view, view, sib_ss.at[group, t, d], sib_rs.at[group, t, d], sib)

    def ag_start(group):
        for d in (1, 3, 2):
            for t in range(3):
                start(ag(group, t, 0, d))

    def ag_next(group, stage):
        for t in range(3):
            for d in (1, 3, 2):
                ag_wait(group, t, stage - 1, d)
            for d in (1, 3, 2):
                start(ag(group, t, stage, d))
            if stage == 2:
                start(hand(group, t, 0, True))

    def ag_finish(group):
        for d in (1, 3, 2):
            for t in range(3):
                ag_wait(group, t, 2, d)
                start(hand(group, t, d, True))
        for d in (0, 1, 3, 2):
            for t in range(3):
                hand(group, t, d, False).wait_recv()

    for a in range(3):
        w[a, me.z, me.yl, me.yh, me.x, me.c] = wsh_ref[a]
    ag_start(0)
    seq = me.z * 2 + me.yl
    vecs[seq] = vec_ref[...]
    seg_own = seg_ref[...].astype(F32)
    segs[0] = seg_own
    start(remote(segs.at[0], segs.at[1], one_ss.at[0], one_rs.at[0], sib))

    def seq_peer(k):
        at = shifted(me, "z", k // 2)
        return moved(at, yl=1 - me.yl) if k % 2 else at

    def seq_from(k):
        at = shifted(me, "z", -(k // 2))
        return moved(at, yl=1 - me.yl) if k % 2 else at

    for k in range(1, 8):
        start(remote(vecs.at[seq], vecs.at[seq], vec_ss.at[k - 1], vec_rs.at[k - 1], seq_peer(k)))
    for k in range(1, 8):
        src = seq_from(k)
        at = vecs.at[src.z * 2 + src.yl]
        remote(at, at, vec_ss.at[k - 1], vec_rs.at[k - 1], seq_peer(k)).wait_recv()

    def whole(row):
        return jnp.concatenate([vecs[s, row : row + 1, 0:96] for s in range(8)], axis=1).astype(F32)

    x_rows = x_ref[...].astype(F32)
    n1, rstd1 = norm_parts(x_rows)
    first = (n1 * whole(FIRST_GAIN) + whole(FIRST_SHIFT)).astype(BF)
    first_s[...] = first
    fat_s[:, 0:TOK] = first.astype(F32).T.astype(BF)
    cott_s[...] = cot_ref[...].astype(F32).T.astype(BF)
    ag_next(0, 1)
    ag_next(0, 2)
    ag_start(1)
    ag_finish(0)
    ag_next(1, 1)

    def unit_bias(u):
        if 8 <= u < 16:
            return jnp.zeros((1, 96), F32)
        j = u if u < 8 else u - 8
        row = MIXER_BIAS + j % 2
        return vecs[j // 2, row : row + 1, 0:96].astype(F32)

    for s in range(8):
        bias = jnp.concatenate([unit_bias(3 * s + k) for k in range(3)], axis=1)
        res = nn(first_s[...], w[0, s // 2, s % 2].reshape(D, SHARD))
        mix_s[:, 288 * s : 288 * s + 288] = (res[:, :288] + bias).astype(BF)
    for h in range(4):
        q = mix_s[:, 192 * h : 192 * h + 192] * jnp.asarray(0.125, BF)
        q_send[h] = jnp.concatenate([q, jnp.zeros((TOK, 64), BF)], axis=1)
        k = mix_s[:, D + 192 * h : D + 192 * h + 192]
        v = mix_s[:, 2 * D + 192 * h : 2 * D + 192 * h + 192]
        kv_send[h] = jnp.concatenate([k, v[:, 128:192], v[:, 0:128]], axis=1)

    def exchange(src_of, dst_of, kind, ss, rs, order=(1, 3, 2, 0)):
        for d in order:
            to = shifted(swap, "z", d)
            src, dst = src_of(to.z), dst_of(me.z)
            if d:
                start(remote(src, dst, ss.at[kind, d], rs.at[kind, d], to))
            else:
                exchange_one(src, dst, kind, ss, rs, to)

    def exchange_one(src, dst, kind, ss, rs, to):
        @pl.when(here)
        def _():
            pltpu.make_async_copy(src, dst, rs.at[kind, 0]).start()

        @pl.when(jnp.logical_not(here))
        def _():
            remote(src, dst, ss.at[kind, 0], rs.at[kind, 0], to).start()

    def exchange_wait(src_of, dst_of, kind, ss, rs, d):
        frm = shifted(me, "z", -d)
        to = shifted(swap, "z", d)
        src, dst = src_of(to.z), dst_of(frm.z)
        if d:
            remote(src, dst, ss.at[kind, d], rs.at[kind, d], to).wait_recv()
        else:

            @pl.when(here)
            def _():
                pltpu.make_async_copy(src, dst, rs.at[kind, 0]).wait()

            @pl.when(jnp.logical_not(here))
            def _():
                remote(src, dst, ss.at[kind, 0], rs.at[kind, 0], to).wait()

    def kv_src(z):
        return kv_send.at[z]

    def kv_dst(z):
        return kv_all.at[z, me.c]

    def kv_there(z):
        return kv_all.at[z, me.yl]

    def q_src(z):
        return q_send.at[z]

    def q_dst(z):
        return q_all.at[z]

    exchange(kv_src, kv_there, 0, a2a_ss, a2a_rs)
    exchange(q_src, q_dst, 1, a2a_ss, a2a_rs)
    kvs = []
    for d in (1, 3, 2, 0):
        exchange_wait(kv_src, kv_dst, 0, a2a_ss, a2a_rs, d)
        z = shifted(me, "z", -d).z
        copy = remote(kv_all.at[z, me.c], kv_all.at[z, me.c], kvs_ss.at[d], kvs_rs.at[d], sib)
        start(copy)
    for d in (1, 3, 2, 0):
        exchange_wait(q_src, q_dst, 1, a2a_ss, a2a_rs, d)
    for d in (1, 3, 2, 0):
        z = shifted(me, "z", -d).z
        at = kv_all.at[z, 1 - me.c]
        remote(at, at, kvs_ss.at[d], kvs_rs.at[d], sib).wait_recv()
    remote(segs.at[0], segs.at[1], one_ss.at[0], one_rs.at[0], sib).wait_recv()
    ag_next(1, 2)

    for b in range(8):
        kvt[:, TOK * b : TOK * b + TOK] = kv_all[b // 2, b % 2].astype(F32).T.astype(BF)
    seg = jnp.where(here, segs[0], segs[1])
    ones = (1, 1)
    begin1 = jnp.sum(jnp.where(seg < 0.5, 1.0, 0.0), axis=(0, 1), keepdims=True).astype(jnp.int32).reshape(ones)
    begin2 = jnp.sum(jnp.where(seg < 1.5, 1.0, 0.0), axis=(0, 1), keepdims=True).astype(jnp.int32).reshape(ones)
    lane = lax.broadcasted_iota(jnp.int32, (TOK, TOK), 1)

    def allowed_of(b):
        n = 256 * (b + 1)
        qpos = 256 * b + TOK * me.c + lax.broadcasted_iota(jnp.int32, (1, TOK), 1)
        low = jnp.where(qpos < begin1, 0, jnp.where(qpos < begin2, begin1, begin2))
        kpos = lax.broadcasted_iota(jnp.int32, (n, TOK), 0)
        return (kpos <= qpos) & (kpos >= low)

    def keys_of(b, h):
        n = 256 * (b + 1)
        at = slice(0, 128) if h < 2 else slice(128, 256)
        return kv_all[0 : b + 1, :, :, at].reshape(n, TOK)

    def values_of(b, h):
        n = 256 * (b + 1)
        at = slice(256, 384) if h < 2 else slice(128, 256)
        return kv_all[0 : b + 1, :, :, at].reshape(n, TOK)

    K_ROWS = (0, 64, 128)
    V_ROWS = (256, 320, 192)

    def half(v, upper):
        keep = lane >= 64 if upper else lane < 64
        return jnp.where(keep, v, jnp.zeros_like(v))

    def query_of(b, h):
        tile = q_all[b, :, 0:128] if h < 2 else q_all[b, :, 128:256]
        return half(tile, h == 1)

    def att_src(z):
        return att_send.at[z]

    def att_dst(z):
        return att_recv.at[z]

    for b in (3, 2, 1, 0):
        n = 256 * (b + 1)
        allowed = allowed_of(b)
        outs = []
        for h in range(3):
            scores = jnp.where(allowed, nt(keys_of(b, h), query_of(b, h)), NEG)
            top = jnp.max(scores, axis=0, keepdims=True)
            expo = jnp.exp(scores - top)
            total = jnp.sum(expo, axis=0, keepdims=True)
            lse_s[b, h : h + 1, :] = top + jnp.log(total)
            weights = (expo * (1.0 / total)).astype(BF)
            outs.append(nn(kvt[V_ROWS[h] : V_ROWS[h] + 64, 0:n], weights))
        outs.append(jnp.zeros((64, TOK), F32))
        both = jnp.concatenate(outs, axis=0)
        att_send[b] = both.T.astype(BF)
    exchange(att_src, att_dst, 0, back_ss, back_rs)
    for d in (1, 3, 2, 0):
        exchange_wait(att_src, att_dst, 0, back_ss, back_rs, d)
    for h in range(4):
        att_s[:, 192 * h : 192 * h + 192] = att_recv[h, :, 0:192]

    def merge_tile(s):
        return w[0, s // 2, s % 2, :, :, :, :, 256:384].reshape(D, TOK)

    branch = jnp.concatenate([nn(att_s[...], merge_tile(s))[:, 32:128] for s in range(8)], axis=1)
    middle = x_ref[...].astype(F32) + branch + whole(MERGE_BIAS)
    mid_s[...] = middle
    n2, rstd2 = norm_parts(middle)
    n2_s[...] = n2
    second = (n2 * whole(SECOND_GAIN) + whole(SECOND_SHIFT)).astype(BF)
    first_s[...] = second
    sect_s[...] = second.astype(F32).T.astype(BF)
    fat_s[:, TOK : 2 * TOK] = att_s[...].astype(F32).T.astype(BF)
    mlp_s[...] = jnp.zeros_like(mlp_s)
    dsec_s[...] = jnp.zeros_like(dsec_s)
    ag_finish(1)

    def rs0(a, z, yl):
        src = g.at[a, z, yl, :, :, 1 - me.c]
        s = z * 2 + yl
        return remote(src, r0.at[a, z, yl], rs0_ss.at[a, s], rs0_rs.at[a, s], sib)

    def units(s, _):
        z, yl = lax.div(s, 2), lax.rem(s, 2)
        rows = vecs[s].astype(F32)
        bias = jnp.concatenate([rows[EXPAND_BIAS + k : EXPAND_BIAS + k + 1] for k in range(3)], axis=1)
        expand = w[1, z, yl].reshape(D, SHARD)
        shrink = w[2, z, yl].reshape(D, SHARD)
        pre = nn(first_s[...], expand) + bias
        square = pre * pre
        tanh = jnp.tanh(0.7978845608028654 * (pre + 0.044715 * square * pre))
        active = (0.5 * pre * (1.0 + tanh)).astype(BF)
        slope = 0.5 * (1.0 + tanh) + 0.5 * pre * (1.0 - tanh * tanh) * (
            0.7978845608028654 * (1.0 + 0.134145 * square)
        )
        d_pre = (nn(cot_ref[...], shrink) * slope).astype(BF)
        mlp_s[...] += nt(active, shrink)
        dsec_s[...] += nt(d_pre, expand)
        sums = col_sums(d_pre)
        for k in range(3):
            vg[s, EXPAND_BIAS + k : EXPAND_BIAS + k + 1, :] = sums[:, TOK * k : TOK * k + TOK]
        blocks = (2, 4, 2, 48, SHARD)
        g[2, z, yl] = nn(cott_s[...], active).astype(BF).reshape(blocks)
        rs0(2, z, yl).start()
        g[1, z, yl] = nn(sect_s[...], d_pre).astype(BF).reshape(blocks)
        rs0(1, z, yl).start()
        return 0

    lax.fori_loop(0, 8, units, 0)
    hidden_ref[...] = (mid_s[...] + mlp_s[...] + whole(SHRINK_BIAS)).astype(BF)

    d_second = dsec_s[...]
    cot = cot_ref[...].astype(F32)
    d_middle = cot + norm_back(d_second, whole(SECOND_GAIN), n2_s[...], rstd2)
    mid_s[...] = d_middle
    d_branch = d_middle.astype(BF)
    dbr_s[...] = d_branch
    g_gain_b = col_sums(d_second * n2_s[...])
    g_shift_b = col_sums(d_second)
    g_b_shrink = col_sums(cot)
    g_b_merge = col_sums(d_branch)
    zeros32 = jnp.zeros((TOK, 32), BF)
    d_att = jnp.zeros((TOK, D), F32)
    for s in range(8):
        d_att += nt(jnp.concatenate([zeros32, dbr_s[:, 96 * s : 96 * s + 96]], axis=1), merge_tile(s))
    d_att = d_att.astype(BF)
    for h in range(4):
        o = d_att[:, 192 * h : 192 * h + 192]
        do_send[h] = jnp.concatenate([o[:, 0:128], jnp.zeros((TOK, 64), BF), o[:, 128:192]], axis=1)

    def do_src(z):
        return do_send.at[z]

    def do_dst(z):
        return do_recv.at[z]

    exchange(do_src, do_dst, 1, back_ss, back_rs)

    def rs0_add(a):
        def step(s, _):
            z, yl = lax.div(s, 2), lax.rem(s, 2)
            rs0(a, z, yl).wait()
            mine = g[a, z, yl, :, :, me.c].astype(F32)
            r0[a, z, yl] = (r0[a, z, yl].astype(F32) + mine).astype(BF)
            return 0

        lax.fori_loop(0, 8, step, 0)

    rbs = (rb1, rb2, rb3)

    def rs_copy(group, t, stage, d):
        order = ORDERS[t][::-1]
        to = shifted(me, order[stage], d)
        src = part(r0, to, t, order[stage + 1 :], lead(group), core=False)
        at = rbs[stage][t].at[(d - 1,) + lead(group)]
        return remote(src, at, rs_ss.at[group, t, stage, d - 1], rs_rs.at[group, t, stage, d - 1], to)

    def rs_start(group, stage):
        for d in (1, 3, 2):
            for t in range(3):
                start(rs_copy(group, t, stage, d))

    def rs_sum(group, t, stage):
        order = ORDERS[t][::-1]
        for d in (1, 3, 2):
            rs_copy(group, t, stage, d).wait_recv()
        at = part(r0, me, t, order[stage + 1 :], lead(group), core=False)
        first, count = GROUPS[group]
        got = rbs[stage][t]
        total = at[...].astype(F32)
        for d in range(3):
            total += got[d, first : first + count].astype(F32)
        return at, total

    def rs_next(group, stage):
        for t in range(3):
            at, total = rs_sum(group, t, stage - 1)
            at[...] = total.astype(BF)
            for d in (1, 3, 2):
                start(rs_copy(group, t, stage, d))

    def rs_finish(group, store):
        for t in range(3):
            _, total = rs_sum(group, t, 2)
            store(t, total)

    rs0_add(2)
    rs0_add(1)
    rs_start(1, 0)

    for d in (1, 3, 2, 0):
        exchange_wait(do_src, do_dst, 1, back_ss, back_rs, d)
    dkv_s[...] = jnp.zeros_like(dkv_s)

    def sib_copy(b):
        return remote(dkv_sib.at[b], dkv_got.at[b], kvs_ss.at[4 + b], kvs_rs.at[4 + b], sib)

    for b in (3, 2, 1, 0):
        n = 256 * (b + 1)
        allowed = allowed_of(b)
        dqs, dss, pbs, dos, qs = [], [], [], [], []
        for h in range(3):
            q = query_of(b, h)
            do = half(do_recv[b, :, 0:128] if h < 2 else do_recv[b, :, 128:256], h > 0)
            scores = jnp.where(allowed, nt(keys_of(b, h), q), NEG)
            probs = jnp.exp(scores - lse_s[b, h : h + 1, :])
            dw = nt(values_of(b, h), do)
            centre = jnp.sum(probs * dw, axis=0, keepdims=True)
            ds = (probs * (dw - centre)).astype(BF)
            dqs.append(nn(kvt[K_ROWS[h] : K_ROWS[h] + 64, 0:n], ds))
            dss.append(ds)
            pbs.append(probs.astype(BF))
            dos.append(do)
            qs.append(q)
        dqs.append(jnp.zeros((64, TOK), F32))
        dq_send[b] = (jnp.concatenate(dqs, axis=0) * 0.125).T.astype(BF)

        def pair(l0, l1, r0_, r1_):
            return nn(jnp.concatenate([l0, l1], axis=1), jnp.concatenate([r0_, r1_], axis=0))

        dkv_s[0:n, 0:128] += pair(dss[0], dss[1], qs[0], qs[1])
        dkv_s[0:n, 128:256] += pair(dss[2], pbs[2], qs[2], dos[2])
        dkv_s[0:n, 256:384] += pair(pbs[0], pbs[1], dos[0], dos[1])
        other = pl.multiple_of(256 * b + TOK * (1 - me.c), TOK)
        dkv_sib[b] = dkv_s[pl.ds(other, TOK), :].astype(BF)
        start(sib_copy(b))

    def dq_src(z):
        return dq_send.at[z]

    def dq_dst(z):
        return dq_recv.at[z]

    def dkv_src(z):
        return dkv_send.at[z]

    def dkv_dst(z):
        return dkv_recv.at[z]

    exchange(dq_src, dq_dst, 2, back_ss, back_rs)
    for b in (3, 2, 1, 0):
        sib_copy(b).wait_recv()
        own = pl.multiple_of(256 * b + TOK * me.c, TOK)
        dkv_send[b] = (dkv_s[pl.ds(own, TOK), :] + dkv_got[b].astype(F32)).astype(BF)
    exchange(dkv_src, dkv_dst, 3, back_ss, back_rs)
    rs_next(1, 1)
    for d in (1, 3, 2, 0):
        exchange_wait(dq_src, dq_dst, 2, back_ss, back_rs, d)
    for d in (1, 3, 2, 0):
        exchange_wait(dkv_src, dkv_dst, 3, back_ss, back_rs, d)

    for h in range(4):
        got = dkv_recv[h]
        dmix_s[:, 192 * h : 192 * h + 192] = dq_recv[h, :, 0:192]
        dmix_s[:, D + 192 * h : D + 192 * h + 192] = got[:, 0:192]
        dmix_s[:, 2 * D + 192 * h : 2 * D + 192 * h + 192] = jnp.concatenate(
            [got[:, 256:384], got[:, 192:256]], axis=1
        )
    zeros96, zeros288 = jnp.zeros((TOK, 96), BF), jnp.zeros((TOK, 288), BF)
    d_first = jnp.zeros((TOK, D), F32)
    for s in range(8):
        z, yl = s // 2, s % 2
        left = jnp.concatenate([dmix_s[:, 288 * s : 288 * s + 288], zeros96], axis=1)
        right = jnp.concatenate([zeros288, dbr_s[:, 96 * s : 96 * s + 96]], axis=1)
        grad = nn(fat_s[...], jnp.concatenate([left, right], axis=0))
        g[0, z, yl] = grad.astype(BF).reshape(2, 4, 2, 48, SHARD)
        start(rs0(0, z, yl))
        d_first += nt(left, w[0, z, yl].reshape(D, SHARD))
    d_x = norm_back(d_first, whole(FIRST_GAIN), n1, rstd1)
    gin_ref[...] = mid_s[...] + d_x
    g_gain_a = col_sums(d_first * n1)
    g_shift_a = col_sums(d_first)
    sums = col_sums(dmix_s[...])
    biases = jnp.concatenate([sums[:, 0:D], sums[:, 2 * D : 3 * D]], axis=1)

    rows = [(FIRST_GAIN, g_gain_a), (FIRST_SHIFT, g_shift_a), (MERGE_BIAS, g_b_merge), (SECOND_GAIN, g_gain_b)]
    rows += [(SECOND_SHIFT, g_shift_b), (SHRINK_BIAS, g_b_shrink)]
    for s in range(8):
        for row, value in rows:
            vg[s, row : row + 1, 0:96] = value[:, 96 * s : 96 * s + 96]
        for k in range(2):
            at = 192 * s + 96 * k
            vg[s, MIXER_BIAS + k : MIXER_BIAS + k + 1, 0:96] = biases[:, at : at + 96]

    def vred(k):
        to = seq_peer(k)
        return remote(vg.at[to.z * 2 + to.yl], vr.at[k - 1], vred_ss.at[k - 1], vred_rs.at[k - 1], to)

    for k in range(1, 8):
        start(vred(k))
    for s in range(8):
        pass
    rs0_add_a(rs0, g, r0, me)
    rs_start(0, 0)
    for k in range(1, 8):
        vred(k).wait_recv()
    total = vg[seq]
    for k in range(7):
        total += vr[k]
    vsum[0] = total
    vcopy = remote(vsum.at[0], vsum.at[1], vx_ss.at[0], vx_rs.at[0], sib)
    start(vcopy)

    def store_es(t, total):
        gexp_ref[16 * t : 16 * t + 16, :] = total[0]
        gshr_ref[16 * t : 16 * t + 16, :] = total[1]

    def store_a(t, total):
        gmix_ref[16 * t : 16 * t + 16, :] = total[0, :, 0:288]
        gmerge_ref[16 * t : 16 * t + 16, :] = total[0, :, 288:384]

    rs_next(1, 2)
    vcopy.wait_recv()
    vx[me.x] = vsum[0] + vsum[1]

    def vx_copy(d, back=False):
        at = vx.at[shifted(me, "x", -d).x] if back else vx.at[me.x]
        return remote(at, at, vx_ss.at[d], vx_rs.at[d], shifted(me, "x", d))

    for d in (1, 2, 3):
        start(vx_copy(d))
    rs_next(0, 1)
    for d in (1, 2, 3):
        vx_copy(d, True).wait_recv()
    vsum[2] = vx[0] + vx[1] + vx[2] + vx[3]
    ycopy = remote(vsum.at[2], vsum.at[3], vx_ss.at[4], vx_rs.at[4], shifted(me, "y", 2))
    start(ycopy)
    rs_finish(1, store_es)
    rs_next(0, 2)
    ycopy.wait_recv()
    vout_ref[...] = vsum[2] + vsum[3]
    rs_finish(0, store_a)
    for copy in pending:
        copy.wait_send()


def rs0_add_a(rs0, g, r0, me):
    def step(s, _):
        z, yl = lax.div(s, 2), lax.rem(s, 2)
        rs0(0, z, yl).wait_recv()
        mine = g[0, z, yl, :, :, me.c].astype(F32)
        r0[0, z, yl] = (r0[0, z, yl].astype(F32) + mine).astype(BF)
        return 0

    lax.fori_loop(0, 8, step, 0)


def scratches():
    v, dma = pltpu.VMEM, pltpu.SemaphoreType.DMA
    third = (16, SHARD)
    return [
        v((3, 4, 2, 2, 4, 2, 48, SHARD), BF),
        v((3, 4, 2, 2, 4, 2, 48, SHARD), BF),
        v((3, 4, 2, 2, 4, 48, SHARD), BF),
        [v((3, 3, 2, 2, 4) + third, BF), v((3, 3, 4, 2, 2) + third, BF), v((3, 3, 4, 4) + third, BF)],
        [v((3, 3, 4) + third, BF), v((3, 3, 2, 2) + third, BF), v((3, 3, 4) + third, BF)],
        [v((3, 3) + third, BF) for _ in range(3)],
        v((8, 16, TOK), BF),
        v((2, 8, TOK), F32),
        v((TOK, D), BF),
        v((TOK, 3 * D), BF),
        v((4, TOK, 256), BF),
        v((4, TOK, SHARD), BF),
        v((4, TOK, 256), BF),
        v((4, 2, TOK, SHARD), BF),
        v((SHARD, 8 * TOK), BF),
        v((4, 8, TOK), F32),
        v((4, TOK, 256), BF),
        v((4, TOK, 256), BF),
        v((TOK, D), BF),
        v((TOK, D), F32),
        v((TOK, D), F32),
        v((D, TOK), BF),
        v((D, TOK), BF),
        v((TOK, D), F32),
        v((TOK, D), F32),
        v((TOK, D), BF),
        v((D, 2 * TOK), BF),
        v((4, TOK, 256), BF),
        v((4, TOK, 256), BF),
        v((8 * TOK, SHARD), F32),
        v((4, TOK, SHARD), BF),
        v((4, TOK, SHARD), BF),
        v((4, TOK, 256), BF),
        v((4, TOK, 256), BF),
        v((4, TOK, SHARD), BF),
        v((4, TOK, SHARD), BF),
        v((TOK, 3 * D), BF),
        v((TOK, D), F32),
        v((8, 16, TOK), F32),
        v((7, 16, TOK), F32),
        v((4, 16, TOK), F32),
        v((4, 16, TOK), F32),
        dma((2, 3, 3, 3)), dma((2, 3, 3, 3)),
        dma((2, 3, 4)), dma((2, 3, 4)),
        dma((7,)), dma((7,)),
        dma((1,)), dma((1,)),
        dma((2, 4)), dma((2, 4)),
        dma((8,)), dma((8,)),
        dma((4, 4)), dma((4, 4)),
        dma((3, 8)), dma((3, 8)),
        dma((2, 3, 3, 3)), dma((2, 3, 3, 3)),
        dma((7,)), dma((7,)),
        dma((5,)), dma((5,)),
        dma((1,)),
    ]


def body(
    residual_in, cotangent, segments, first_gain, first_shift, mixer_weight, mixer_bias, merge_weight, merge_bias,
    second_gain, second_shift, expand_weight, expand_bias, shrink_weight, shrink_bias,
):
    weights = jnp.stack([jnp.concatenate([mixer_weight, merge_weight], axis=1), expand_weight, shrink_weight.T])
    small = [first_gain, first_shift, mixer_bias[:96], mixer_bias[96:], merge_bias, second_gain, second_shift, shrink_bias]
    vec = jnp.concatenate(
        [jnp.pad(jnp.stack(small), ((0, 0), (0, 32))), expand_bias.reshape(3, TOK), jnp.zeros((5, TOK), BF)], axis=0
    )
    vmem = pl.BlockSpec(memory_space=pltpu.VMEM)
    shapes = [((TOK, D), BF), ((TOK, D), F32), ((48, 288), F32), ((48, 96), F32), ((48, SHARD), F32), ((48, SHARD), F32)]
    shapes += [((16, TOK), F32)]
    hidden, gin, gmix, gmerge, gexp, gshr, vout = pl.pallas_call(
        kernel,
        out_shape=[jax.ShapeDtypeStruct(*s) for s in shapes],
        in_specs=[vmem] * 5,
        out_specs=[vmem] * 7,
        scratch_shapes=scratches(),
        compiler_params=pltpu.CompilerParams(
            collective_id=0, has_side_effects=True, vmem_limit_bytes=62 * 1024 * 1024
        ),
    )(residual_in[0], cotangent[0], segments.reshape(8, TOK), weights, vec)
    return (
        hidden[None], gin[None], vout[0, :96], vout[1, :96], gmix, vout[2:4, :96].reshape(192), gmerge, vout[4, :96],
        vout[5, :96], vout[6, :96], gexp, vout[8:11].reshape(SHARD), gshr.T, vout[7, :96],
    )


def solution(mesh):
    vector, matrix = P("seq"), P("dp", "seq")
    tokens = P("dp", "seq", None)
    return jax.shard_map(
        body,
        mesh=mesh,
        in_specs=(
            tokens, tokens, P("dp", None), vector, vector, matrix, vector, matrix, vector, vector, vector, matrix, vector,
            P("seq", "dp"), vector,
        ),
        out_specs=(
            tokens, tokens, vector, vector, matrix, vector, matrix, vector, vector, vector, matrix, vector,
            P("seq", "dp"), vector,
        ),
        check_vma=False,
    )
```

time: 949 us -> 161 us (0.17)
  waiting for transfers between devices: 599 us -> 0 us
  blocking collectives: 218 us -> 0 us
  Pallas kernels: 0 us -> 145 us
  matrix products: 59.6 us -> 0 us
  local copies, waits for them, and re-layouts: 36.6 us -> 11.1 us
  between operations: 16.1 us -> 0.69 us
  other arithmetic: 12.5 us -> 2.8 us
    reduce_scatter x4 -> x0, waiting for transfers between devices: 279 us -> none  [the longest x1 84.8 us: body(): lax.psum_scatter(g_shrink.astype(jnp.bfloat16), 'dp', scatter_dimension=1...]
    all_gather x6 -> x0, waiting for transfers between devices: 173 us -> none  [the longest x1 56.5 us: body(): lax.all_gather(expand_part, 'dp', axis=0, tiled=True)]
    unnamed x22 -> x0, waiting for transfers between devices: 147 us -> none
    pallas_call x0 -> x1, Pallas kernels: none -> 145 us  [body(): pl.pallas_call(kernel, out_shape=[jax.ShapeDtypeStruct(*s) for s in shape...]
    all_gather x5 -> x0, blocking collectives: 124 us -> none  [the longest x1 27.1 us: body(): lax.all_gather(shrink_weight, 'seq', axis=0, tiled=True)]
    psum x1 -> x0, blocking collectives: 67.3 us -> none  [body(): lax.psum((g_gain_a, g_shift_a, g_b_mix, merge_bias_gradient, g_gain_b, g_...]
    dot_general x18 -> x0, matrix products: 59.6 us -> none  [the longest x1 5.8 us: body(): jnp.einsum('hqk,qhd->khd', weights, d_att_h, preferred_element_type=jnp.f...]
    unnamed x1 -> x0, blocking collectives: 26.7 us -> none
  transfers between devices with their start and end apart: 16 -> 0, of which waited for: 13 -> 0; matrix products, arithmetic and copies ran while one was open for 10% -> 0% of each run, Pallas kernels for 0% -> 0%
where the time goes in v1:
time: 161 us; the launch traced here: 159 us
  Pallas kernels  145 us (90%)
  local copies, waits for them, and re-layouts  11.1 us (7%)
  other arithmetic  2.8 us (2%)
    pallas_call x1, Pallas kernels, body(): pl.pallas_call(kernel, out_shape=[jax.ShapeDtypeStruct(*s) for s in shape...  145 us
    unnamed x22, local copies, waits for them, and re-layouts  5.45 us

profile of v1, /device:TPU:1, one launch (start us, length us, event | category | flops | bytes accessed | tf_op | source)
XLA Modules:
  0.0 159.1 jit_solution(15304389329767564716)
XLA Ops:
  0.6 0.0 copy-start.6
  0.7 0.8 slice_bitcast_fusion.7
  1.5 0.8 stack.51
  2.2 0.1 pad.7.clone
  2.3 1.3 fusion.2.vec_ref
  3.6 0.0 copy-done.6
  3.7 0.8 maximum_bitcast_fusion
  4.5 0.0 copy-done.5
  4.5 0.7 pad_maximum_fusion.wsh_ref
  5.1 144.5 %shard_map.254 = (bf16[128,768]{1,0:T(8,128)(2,1)}, f32[128,768]{1,0:T(8,128)}, f32[48,288]{1,0:T(8,128)}, f32[48,96]{1,0:T(8,128)}, f32[48,384]{1,0:T(8,128)}, /*index=5*/f32[48,384]{1,0:T(8,128)}, f32[16,128]{1,0:T(8,128)}) custom-call(bf16[128,768]{1,0:T(8,128)(2,1)} %bitcast.39, bf16[128,768]{1,0:T(8,128)(2,1)} %bitcast.40, s32[8,128]{1,0:T(8,128)} %bitcast.44, ...), custom_call_target="tpu_custom_call" | custom-call | tf_op jit(solution)/shard_map/pallas_call | solution.py:720
  149.7 1.4 slice_bitcast_fusion.1
  151.1 0.7 slice.34
  151.8 0.6 reshape.42
  152.4 1.3 slice_bitcast_fusion
  153.7 1.6 %copy.35 = bf16[1,128,768]{2,1,0:T(8,128)(2,1)} copy(bf16[1,128,768]{2,1,0:T(8,128)(2,1)} %bitcast.38) | data formatting | bytes 393216
  155.3 0.0 copy-done
  155.3 0.7 copy.36
  156.0 0.2 copy-done.3
  156.2 0.6 copy.37
  156.8 0.1 copy-done.7
  157.0 0.6 copy.38
  157.6 0.6 copy.39
  158.2 0.3 copy-done.1
  158.5 0.6 copy.40
  (10 shorter events, 0.0 us)
Async XLA Ops:
  0.6 3.0 %copy-start.6 = (bf16[48,288]{1,0:T(8,128)(2,1)S(1)}, bf16[48,288]{1,0:T(8,128)(2,1)}, u32[]{:S(2)}) copy-start(bf16[48,288]{1,0:T(8,128)(2,1)} %param.20) | copy-start | bytes 82948
  3.7 0.8 copy-start.4
  3.7 0.8 copy-start.5
  149.6 5.6 %copy-start = (f32[128,768]{1,0:T(8,128)S(1)}, f32[128,768]{1,0:T(8,128)}, u32[]{:S(2)}) copy-start(f32[128,768]{1,0:T(8,128)} %get-tuple-element.22) | copy-start | bytes 1179652
  155.3 0.9 copy-start.3
  156.2 0.7 copy-start.7
  156.2 1.3 copy-start.2
  157.6 0.9 copy-start.1

commit v2 on v1

v2 whole, which is shorter than its diff:
```python
import functools
import types

import jax
import jax.numpy as jnp
from jax import lax
from jax.experimental import pallas as pl
from jax.experimental.pallas import tpu as pltpu
from jax.sharding import PartitionSpec as P


D = 768
HD = 64
TOK = 128
SHARD = 384
WIDE = 896
MERGE = 768
EPS = 1e-05
NEG = -1e30
MESH = pl.DeviceIdType.MESH
BF = jnp.bfloat16
F32 = jnp.float32
ORDERS = (("x", "y", "z"), ("y", "z", "x"), ("z", "x", "y"))
FIRST_GAIN, FIRST_SHIFT, MIXER_BIAS, MERGE_BIAS, SECOND_GAIN, SECOND_SHIFT, SHRINK_BIAS, EXPAND_BIAS = 0, 1, 2, 4, 5, 6, 7, 8


def place_of():
    dp, seq = lax.axis_index("dp"), lax.axis_index("seq")
    return types.SimpleNamespace(
        x=lax.rem(lax.div(dp, 2), 4),
        yh=lax.div(dp, 8),
        yl=lax.rem(seq, 2),
        z=lax.div(seq, 2),
        c=lax.rem(dp, 2),
    )


def moved(at, **to):
    new = types.SimpleNamespace(**vars(at))
    for name, value in to.items():
        setattr(new, name, value)
    return new


def shifted(at, axis, d):
    d = d % 4
    if axis == "x":
        return moved(at, x=lax.rem(at.x + d, 4))
    if axis == "z":
        return moved(at, z=lax.rem(at.z + d, 4))
    y = lax.rem(at.yh * 2 + at.yl + d, 4)
    return moved(at, yh=lax.div(y, 2), yl=lax.rem(y, 2))


def device(at):
    return (at.yh * 8 + at.x * 2 + at.c, at.z * 2 + at.yl)


def nn(a, b):
    return jnp.dot(a, b, preferred_element_type=F32)


def nt(a, b):
    return lax.dot_general(a, b, (((1,), (1,)), ((), ())), preferred_element_type=F32)


def remote(src, dst, send, recv, to):
    return pltpu.make_async_remote_copy(
        src_ref=src, dst_ref=dst, send_sem=send, recv_sem=recv, device_id=device(to), device_id_type=MESH
    )


def part(ref, at, t, full, core=True):
    every = slice(None)
    where = [every if "z" in full else at.z]
    where += [every, every] if "y" in full else [at.yl, at.yh]
    where += [every if "x" in full else at.x]
    if core:
        where += [at.c]
    return ref.at[tuple(where) + (pl.ds(16 * t, 16), every)]


def norm_parts(v):
    centred = v - jnp.mean(v, axis=-1, keepdims=True)
    rstd = lax.rsqrt(jnp.mean(centred * centred, axis=-1, keepdims=True) + EPS)
    return centred * rstd, rstd


def norm_back(dy, gain, normed, rstd):
    dn = dy * gain
    return rstd * (
        dn
        - jnp.mean(dn, axis=-1, keepdims=True)
        - normed * jnp.mean(dn * normed, axis=-1, keepdims=True)
    )


def col_sums(v):
    return jnp.sum(v.astype(F32), axis=0, keepdims=True)


def turned(v):
    return v.astype(F32).T.astype(BF)


def lanes(*pieces):
    return jnp.concatenate(pieces, axis=1)


def tile(k):
    return pl.ds(pl.multiple_of(k * TOK, TOK), TOK)


IN = (
    "x_in", "cot_in", "seg_in", "mixer_in", "merge_in", "expand_in", "shrink_in", "fgain_in", "fshift_in", "mixb_in",
    "mergeb_in", "sgain_in", "sshift_in", "expandb_in", "shrinkb_in",
)
OUT = ("hidden", "gin", "gmix", "gmerge", "gexp", "gshr", "vout")


def kernel(names, *refs):
    r = types.SimpleNamespace(**dict(zip(names, refs, strict=True)))
    me = place_of()
    sib = moved(me, c=1 - me.c)
    swap = moved(me, yl=me.c, c=me.yl)
    here = me.yl == me.c
    seq = me.z * 2 + me.yl
    ypos = me.yh * 2 + me.yl
    pending = []

    def post(copy):
        copy.start()
        pending.append(copy.wait_send)

    def post_unless(alone, src, dst, send, recv, to):
        @pl.when(alone)
        def _():
            pltpu.make_async_copy(src, dst, recv).start()

        @pl.when(jnp.logical_not(alone))
        def _():
            remote(src, dst, send, recv, to).start()

        def finish():
            @pl.when(jnp.logical_not(alone))
            def _():
                remote(src, dst, send, recv, to).wait_send()

        pending.append(finish)

    def arrived(at, send, recv):
        remote(at, at, send, recv, sib).wait_recv()

    zero32 = jnp.zeros((48, 32), BF)
    for i in range(3):
        r.units[i] = lanes(r.mixer_in[:, 96 * i : 96 * i + 96], zero32)
    own = (me.z, me.yl, me.yh, me.x, me.c)
    r.w[own] = lanes(r.expand_in[...], r.shrink_in[...], r.merge_in[...], zero32)
    mixb = r.mixb_in[...].astype(F32).reshape(1, 192)
    small = [(FIRST_GAIN, r.fgain_in), (FIRST_SHIFT, r.fshift_in), (MERGE_BIAS, r.mergeb_in)]
    small += [(SECOND_GAIN, r.sgain_in), (SECOND_SHIFT, r.sshift_in), (SHRINK_BIAS, r.shrinkb_in)]
    for row, ref in small:
        r.vecs[seq, row : row + 1, 0:96] = ref[...].astype(F32).reshape(1, 96)
    expb = r.expandb_in[...].astype(F32).reshape(1, SHARD)
    for k in range(2):
        r.vecs[seq, MIXER_BIAS + k : MIXER_BIAS + k + 1, 0:96] = mixb[:, 96 * k : 96 * k + 96]
    for k in range(3):
        r.vecs[seq, EXPAND_BIAS + k : EXPAND_BIAS + k + 1, :] = expb[:, TOK * k : TOK * k + TOK]
    r.segs[0] = r.seg_in[...].astype(F32)

    peers = [shifted(shifted(me, "z", dz), "y", dy) for dz in range(4) for dy in range(4) if dz or dy]
    peers += [shifted(me, "x", d) for d in (1, 2, 3)] + [sib, shifted(sib, "y", 2)]
    peers += [moved(shifted(me, "z", d), yl=1 - me.yl, c=1 - me.c) for d in range(4)]
    barrier = pltpu.get_barrier_semaphore()
    for p in peers:
        pl.semaphore_signal(barrier, inc=1, device_id=device(p), device_id_type=MESH)
    pl.semaphore_wait(barrier, len(peers))

    def send_block(kind, b, src, dst):
        to = moved(swap, z=b)
        post_unless(here & (me.z == b), src, dst, r.ex_ss.at[kind, b], r.ex_rs.at[kind, me.z], to)

    def take_block(kind, z, dst):
        arrived(dst, r.ex_ss.at[kind, z], r.ex_rs.at[kind, z])

    X, ATT, DO, DF = range(4)
    for b in range(4):
        send_block(X, b, r.x_in, r.xall.at[me.z])
    for i in range(3):
        u = 3 * seq + i
        for dy in range(4):
            y = lax.rem(ypos + dy, 4)
            to = moved(me, z=lax.div(lax.rem(u, 8), 2), yh=lax.div(y, 2), yl=lax.rem(y, 2))
            half = lax.rem(u, 2)
            kind = lax.div(u, 8)
            dst = r.wm.at[half, me.yh, me.x, me.c, :, tile(kind)]
            sems = (r.wm1_ss.at[i, dy], r.wm1_rs.at[half, me.yh, kind])
            if dy:
                post(remote(r.units.at[i], dst, *sems, to))
            else:
                post_unless(to.z == me.z, r.units.at[i], dst, *sems, to)

    def seq_peer(k):
        at = shifted(me, "z", k // 2)
        return moved(at, yl=1 - me.yl) if k % 2 else at

    def seq_from(k):
        at = shifted(me, "z", -(k // 2))
        return moved(at, yl=1 - me.yl) if k % 2 else at

    for k in range(1, 8):
        post(remote(r.vecs.at[seq], r.vecs.at[seq], r.vec_ss.at[k - 1], r.vec_rs.at[k - 1], seq_peer(k)))
    post(remote(r.segs.at[0], r.segs.at[1], r.one_ss.at[0], r.one_rs.at[0], sib))

    def ag(t, stage, d):
        order = ORDERS[t]
        at = part(r.w, me, t, order[:stage])
        return remote(
            at, at, r.ag_ss.at[t, stage, d - 1], r.ag_rs.at[t, stage, d - 1], shifted(me, order[stage], d)
        )

    def ag_wait(t, stage, d):
        order = ORDERS[t]
        at = part(r.w, shifted(me, order[stage], -d), t, order[:stage])
        arrived(at, r.ag_ss.at[t, stage, d - 1], r.ag_rs.at[t, stage, d - 1])

    def hand(t, d, mine):
        order = ORDERS[t]
        at = shifted(me if mine else sib, order[2], -d)
        view = part(r.w, at, t, order[:2])
        return remote(view, view, r.hand_ss.at[t, d], r.hand_rs.at[t, d], sib)

    def ag_start():
        for d in (1, 3, 2):
            for t in range(3):
                post(ag(t, 0, d))

    def ag_next(stage):
        for t in range(3):
            for d in (1, 3, 2):
                ag_wait(t, stage - 1, d)
            for d in (1, 3, 2):
                post(ag(t, stage, d))
            if stage == 2:
                post(hand(t, 0, True))

    def ag_finish():
        for d in (1, 3, 2):
            for t in range(3):
                ag_wait(t, 2, d)
                post(hand(t, d, True))
        for d in (0, 1, 3, 2):
            for t in range(3):
                hand(t, d, False).wait_recv()

    ag_start()
    for half in range(2):
        for yh in range(2):
            for kind in range(3):
                at = r.wm.at[half, yh, me.x, me.c, :, pl.ds(TOK * kind, TOK)]
                arrived(at, r.wm1_ss.at[0, 0], r.wm1_rs.at[half, yh, kind])

    def wm_view(d, core):
        return r.wm.at[:, :, lax.rem(me.x + 4 - d, 4), core]

    for d in (1, 3, 2):
        post(
            remote(
                wm_view(0, me.c), wm_view(0, me.c), r.wm2_ss.at[d], r.wm2_rs.at[d], shifted(me, "x", d)
            )
        )
    post(remote(wm_view(0, me.c), wm_view(0, me.c), r.wms_ss.at[0], r.wms_rs.at[0], sib))
    for k in range(1, 8):
        src = seq_from(k)
        arrived(r.vecs.at[src.z * 2 + src.yl], r.vec_ss.at[k - 1], r.vec_rs.at[k - 1])

    def whole(row):
        return jnp.concatenate([r.vecs[s, row : row + 1, 0:96] for s in range(8)], axis=1)

    r.cott[...] = turned(r.cot_in[...])
    n1, rstd1 = norm_parts(r.x_in[...].astype(F32))
    r.n1[...] = n1
    gain1, shift1 = whole(FIRST_GAIN), whole(FIRST_SHIFT)
    for b in range(4):
        take_block(X, b, r.xall.at[b])
        normed, _ = norm_parts(r.xall[b].astype(F32))
        r.n1all[b] = normed
        first = normed * gain1 + shift1
        r.fall[b] = first.astype(BF)
        r.fallt[:, TOK * b : TOK * b + TOK] = first.astype(BF).astype(F32).T.astype(BF)
    ag_next(1)
    for d in (1, 3, 2):
        arrived(wm_view(d, me.c), r.wm2_ss.at[d], r.wm2_rs.at[d])
        post(remote(wm_view(d, me.c), wm_view(d, me.c), r.wms_ss.at[d], r.wms_rs.at[d], sib))
    ag_next(2)
    for d in (0, 1, 3, 2):
        arrived(wm_view(d, 1 - me.c), r.wms_ss.at[d], r.wms_rs.at[d])

    def mixer(half, first, count):
        at = slice(TOK * first, TOK * (first + count))
        return r.wm[half, :, :, :, :, at].reshape(D, TOK * count)

    first = r.fall[...].reshape(4 * TOK, D)

    def mixer_bias(at, half):
        row = MIXER_BIAS + half
        return r.vecs[at, row : row + 1, 0:96]

    kv0, kv1 = nn(first, mixer(0, 1, 2)), nn(first, mixer(1, 1, 2))
    keys = lanes(kv0[:, 0:96], kv1[:, 0:96]).astype(BF)
    vbias = lanes(mixer_bias(4 + me.z, 0), mixer_bias(4 + me.z, 1))
    values = (lanes(kv0[:, 128:224], kv1[:, 128:224]) + vbias).astype(BF)
    packed = lanes(keys, values[:, 128:192], values[:, 0:128])
    for b in range(4):
        r.kv_all[b, me.c] = packed[TOK * b : TOK * b + TOK]
    at = r.kv_all.at[:, me.c]
    post(remote(at, at, r.kvs_ss.at[4], r.kvs_rs.at[4], sib))
    qbias = lanes(mixer_bias(me.z, 0), mixer_bias(me.z, 1))
    q = lanes(nn(first, mixer(0, 0, 1))[:, 0:96], nn(first, mixer(1, 0, 1))[:, 0:96])
    q = (q + qbias).astype(BF) * jnp.asarray(0.125, BF)
    q = lanes(q, jnp.zeros((4 * TOK, 64), BF))
    for b in range(4):
        r.q_all[b] = q[TOK * b : TOK * b + TOK]
        r.kvt[:, tile(2 * b + me.c)] = turned(packed[TOK * b : TOK * b + TOK])
    arrived(r.segs.at[1], r.one_ss.at[0], r.one_rs.at[0])
    arrived(r.kv_all.at[:, 1 - me.c], r.kvs_ss.at[4], r.kvs_rs.at[4])
    for b in range(4):
        r.kvt[:, tile(2 * b + 1 - me.c)] = turned(r.kv_all[b, 1 - me.c])

    seg = jnp.where(here, r.segs[0], r.segs[1])

    def starts(bound):
        return jnp.sum(jnp.where(seg < bound, 1.0, 0.0), axis=(0, 1), keepdims=True).astype(jnp.int32)

    begin1, begin2 = starts(0.5), starts(1.5)
    lane = lax.broadcasted_iota(jnp.int32, (TOK, TOK), 1)

    def allowed_of(b):
        n = 256 * (b + 1)
        qpos = 256 * b + TOK * me.c + lax.broadcasted_iota(jnp.int32, (1, TOK), 1)
        low = jnp.where(qpos < begin1, 0, jnp.where(qpos < begin2, begin1, begin2))
        kpos = lax.broadcasted_iota(jnp.int32, (n, TOK), 0)
        return (kpos <= qpos) & (kpos >= low)

    def keys_of(b, h):
        at = slice(0, 128) if h < 2 else slice(128, 256)
        return r.kv_all[0 : b + 1, :, :, at].reshape(256 * (b + 1), TOK)

    def values_of(b, h):
        at = slice(256, 384) if h < 2 else slice(128, 256)
        return r.kv_all[0 : b + 1, :, :, at].reshape(256 * (b + 1), TOK)

    K_ROWS = (0, 64, 128)
    V_ROWS = (256, 320, 192)

    def one_head(v, upper):
        keep = lane >= 64 if upper else lane < 64
        return jnp.where(keep, v, jnp.zeros_like(v))

    def query_of(b, h):
        return one_head(r.q_all[b, :, 0:128] if h < 2 else r.q_all[b, :, 128:256], h == 1)

    for b in (3, 2, 1, 0):
        n = 256 * (b + 1)
        allowed = allowed_of(b)
        outs = []
        for h in range(3):
            scores = jnp.where(allowed, nt(keys_of(b, h), query_of(b, h)), NEG)
            top = jnp.max(scores, axis=0, keepdims=True)
            expo = jnp.exp(scores - top)
            total = jnp.sum(expo, axis=0, keepdims=True)
            r.lse[b, h : h + 1, :] = top + jnp.log(total)
            weights = (expo * (1.0 / total)).astype(BF)
            outs.append(nn(r.kvt[V_ROWS[h] : V_ROWS[h] + 64, 0:n], weights))
        outs.append(jnp.zeros((64, TOK), F32))
        r.att_send[b] = jnp.concatenate(outs, axis=0).T.astype(BF)
        send_block(ATT, b, r.att_send.at[b], r.att_recv.at[me.z])
    for b in range(4):
        take_block(ATT, b, r.att_recv.at[b])
        r.att[:, 192 * b : 192 * b + 192] = r.att_recv[b, :, 0:192]
    ag_finish()

    def merge_tile(s):
        return r.w[s // 2, s % 2, :, :, :, :, MERGE:WIDE].reshape(D, TOK)

    branch = lanes(*[nn(r.att[...], merge_tile(s))[:, 0:96] for s in range(8)])
    middle = r.x_in[...].astype(F32) + branch + whole(MERGE_BIAS)
    r.mid[...] = middle
    n2, rstd2 = norm_parts(middle)
    r.n2[...] = n2
    second = (n2 * whole(SECOND_GAIN) + whole(SECOND_SHIFT)).astype(BF)
    r.second[...] = second
    r.secondt[...] = turned(second)
    r.attt[...] = turned(r.att[...])
    r.mlp[...] = jnp.zeros((TOK, D), F32)
    r.dsec[...] = jnp.zeros((TOK, D), F32)

    def rs0(z, yl):
        src = r.g.at[z, yl, :, :, 1 - me.c, :, pl.ds(0, MERGE)]
        s = z * 2 + yl
        return remote(src, r.r0.at[z, yl, :, :, :, pl.ds(0, MERGE)], r.rs0_ss.at[s], r.rs0_rs.at[s], sib)

    def rs0_merge():
        src = r.g.at[:, :, :, :, 1 - me.c, :, pl.ds(MERGE, TOK)]
        dst = r.r0.at[:, :, :, :, :, pl.ds(MERGE, TOK)]
        return remote(src, dst, r.rs0_ss.at[8], r.rs0_rs.at[8], sib)

    def units(s, _):
        z, yl = lax.div(s, 2), lax.rem(s, 2)
        rows = r.vecs[s]
        bias = lanes(*[rows[EXPAND_BIAS + k : EXPAND_BIAS + k + 1] for k in range(3)])
        expand = r.w[z, yl, :, :, :, :, 0:SHARD].reshape(D, SHARD)
        shrink = r.w[z, yl, :, :, :, :, SHARD:MERGE].reshape(D, SHARD)
        pre = nn(r.second[...], expand) + bias
        square = pre * pre
        tanh = jnp.tanh(0.7978845608028654 * (pre + 0.044715 * square * pre))
        active = (0.5 * pre * (1.0 + tanh)).astype(BF)
        slope = 0.5 * (1.0 + tanh) + 0.5 * pre * (1.0 - tanh * tanh) * (
            0.7978845608028654 * (1.0 + 0.134145 * square)
        )
        d_pre = (nn(r.cot_in[...], shrink) * slope).astype(BF)
        r.mlp[...] += nt(active, shrink)
        r.dsec[...] += nt(d_pre, expand)
        sums = col_sums(d_pre)
        for k in range(3):
            r.vg[s, EXPAND_BIAS + k : EXPAND_BIAS + k + 1, :] = sums[:, TOK * k : TOK * k + TOK]
        blocks = (2, 4, 2, 48, SHARD)
        r.g[z, yl, :, :, :, :, 0:SHARD] = nn(r.secondt[...], d_pre).astype(BF).reshape(blocks)
        r.g[z, yl, :, :, :, :, SHARD:MERGE] = nn(r.cott[...], active).astype(BF).reshape(blocks)
        rs0(z, yl).start()
        return 0

    lax.fori_loop(0, 8, units, 0)
    r.hidden[...] = (r.mid[...] + r.mlp[...] + whole(SHRINK_BIAS)).astype(BF)

    d_second = r.dsec[...]
    cot = r.cot_in[...].astype(F32)
    d_middle = cot + norm_back(d_second, whole(SECOND_GAIN), r.n2[...], rstd2)
    r.mid[...] = d_middle
    d_branch = d_middle.astype(BF)
    r.dbr[...] = d_branch
    g_gain_b = col_sums(d_second * r.n2[...])
    g_shift_b = col_sums(d_second)
    g_b_shrink = col_sums(cot)
    g_b_merge = col_sums(d_branch)
    zeros = jnp.zeros((TOK, 32), BF)

    def branch_part(s):
        return lanes(r.dbr[:, 96 * s : 96 * s + 96], zeros)

    d_att = jnp.zeros((TOK, D), F32)
    for s in range(8):
        d_att += nt(branch_part(s), merge_tile(s))
    d_att = d_att.astype(BF)
    for b in range(4):
        o = d_att[:, 192 * b : 192 * b + 192]
        r.do_send[b] = lanes(o[:, 0:128], jnp.zeros((TOK, 64), BF), o[:, 128:192])
        send_block(DO, b, r.do_send.at[b], r.do_recv.at[me.z])

    for s in range(8):
        r.g[s // 2, s % 2, :, :, :, :, MERGE:WIDE] = (
            nn(r.attt[...], branch_part(s)).astype(BF).reshape(2, 4, 2, 48, TOK)
        )
    rs0_merge().start()

    def rs_copy(t, stage, d):
        order = ORDERS[t][::-1]
        to = shifted(me, order[stage], d)
        src = part(r.r0, to, t, order[stage + 1 :], core=False)
        at = (r.rb1, r.rb2, r.rb3)[stage][t].at[d - 1]
        return remote(src, at, r.rs_ss.at[t, stage, d - 1], r.rs_rs.at[t, stage, d - 1], to)

    def rs_start():
        for d in (1, 3, 2):
            for t in range(3):
                post(rs_copy(t, 0, d))

    def rs_sum(t, stage):
        order = ORDERS[t][::-1]
        for d in (1, 3, 2):
            rs_copy(t, stage, d).wait_recv()
        at = part(r.r0, me, t, order[stage + 1 :], core=False)
        got = (r.rb1, r.rb2, r.rb3)[stage][t]
        total = at[...].astype(F32)
        for d in range(3):
            total += got[d].astype(F32)
        return at, total

    def rs_next(stage):
        for t in range(3):
            at, total = rs_sum(t, stage - 1)
            at[...] = total.astype(BF)
            for d in (1, 3, 2):
                post(rs_copy(t, stage, d))

    rs0_merge().wait()

    def add(s, _):
        z, yl = lax.div(s, 2), lax.rem(s, 2)
        rs0(z, yl).wait()
        mine = r.g[z, yl, :, :, me.c].astype(F32)
        r.r0[z, yl] = (r.r0[z, yl].astype(F32) + mine).astype(BF)
        return 0

    lax.fori_loop(0, 8, add, 0)
    rs_start()

    rows = [(MERGE_BIAS, g_b_merge), (SECOND_GAIN, g_gain_b), (SECOND_SHIFT, g_shift_b), (SHRINK_BIAS, g_b_shrink)]
    for s in range(8):
        for row, value in rows:
            r.vg[s, row : row + 1, 0:96] = value[:, 96 * s : 96 * s + 96]
        r.vg[s, MIXER_BIAS : MIXER_BIAS + 2, :] = jnp.zeros((2, TOK), F32)

    r.dkv[...] = jnp.zeros((8 * TOK, SHARD), F32)
    for b in range(4):
        take_block(DO, b, r.do_recv.at[b])

    def sib_copy(b):
        return remote(r.dkv_sib.at[b], r.dkv_got.at[b], r.kvs_ss.at[b], r.kvs_rs.at[b], sib)

    def pair(l0, l1, r0, r1):
        return nn(jnp.concatenate([l0, l1], axis=1), jnp.concatenate([r0, r1], axis=0))

    gain_sum, shift_sum = [], []

    def finish_block(b):
        sib_copy(b).wait_recv()
        own = pl.multiple_of(256 * b + TOK * me.c, TOK)
        dkv = (r.dkv[pl.ds(own, TOK), :] + r.dkv_got[b].astype(F32)).astype(BF)
        dq = r.dq[b]
        dv = lanes(dkv[:, 256:384], dkv[:, 192:256])
        d_first = jnp.zeros((TOK, D), F32)
        for half in range(2):
            at = slice(96 * half, 96 * half + 96)
            padded = lanes(dq[:, at], zeros, dkv[:, at], zeros, dv[:, at], zeros)
            r.dpad[half, TOK * b : TOK * b + TOK, :] = padded
            d_first += nt(padded, mixer(half, 0, 3))
        r.df_send[b] = d_first.astype(BF)
        send_block(DF, b, r.df_send.at[b], r.df_recv.at[me.z])
        gain_sum.append(col_sums(d_first * r.n1all[b]))
        shift_sum.append(col_sums(d_first))

    for b in (3, 2, 1, 0):
        n = 256 * (b + 1)
        allowed = allowed_of(b)
        dqs, dss, pbs, dos, qs = [], [], [], [], []
        for h in range(3):
            q = query_of(b, h)
            do = one_head(r.do_recv[b, :, 0:128] if h < 2 else r.do_recv[b, :, 128:256], h > 0)
            scores = jnp.where(allowed, nt(keys_of(b, h), q), NEG)
            probs = jnp.exp(scores - r.lse[b, h : h + 1, :])
            dw = nt(values_of(b, h), do)
            centre = jnp.sum(probs * dw, axis=0, keepdims=True)
            ds = (probs * (dw - centre)).astype(BF)
            dqs.append(nn(r.kvt[K_ROWS[h] : K_ROWS[h] + 64, 0:n], ds))
            dss.append(ds)
            pbs.append(probs.astype(BF))
            dos.append(do)
            qs.append(q)
        dqs.append(jnp.zeros((64, TOK), F32))
        r.dq[b] = (jnp.concatenate(dqs, axis=0) * 0.125).T.astype(BF)
        r.dkv[0:n, 0:128] += pair(dss[0], dss[1], qs[0], qs[1])
        r.dkv[0:n, 128:256] += pair(dss[2], pbs[2], qs[2], dos[2])
        r.dkv[0:n, 256:384] += pair(pbs[0], pbs[1], dos[0], dos[1])
        other = pl.multiple_of(256 * b + TOK * (1 - me.c), TOK)
        r.dkv_sib[b] = r.dkv[pl.ds(other, TOK), :].astype(BF)
        post(sib_copy(b))
        if b < 3:
            finish_block(b + 1)
    finish_block(0)

    for half in range(2):
        grad = nn(r.fallt[...], r.dpad[half]).astype(BF)
        r.gm[half] = grad.reshape(2, 4, 2, 48, SHARD)
    gm_sib = remote(r.gm.at[:, :, :, 1 - me.c], r.rm0, r.rm0_ss.at[0], r.rm0_rs.at[0], sib)
    post(gm_sib)
    for half in range(2):
        sums = col_sums(r.dpad[half])
        row = MIXER_BIAS + half
        r.vg[me.z, row : row + 1, 0:96] = sums[:, 0:96]
        r.vg[4 + me.z, row : row + 1, 0:96] = sums[:, 256:352]
    gain_a, shift_a = sum(gain_sum), sum(shift_sum)
    for s in range(8):
        r.vg[s, FIRST_GAIN : FIRST_GAIN + 1, 0:96] = gain_a[:, 96 * s : 96 * s + 96]
        r.vg[s, FIRST_SHIFT : FIRST_SHIFT + 1, 0:96] = shift_a[:, 96 * s : 96 * s + 96]

    def vred(k):
        to = seq_peer(k)
        return remote(r.vg.at[to.z * 2 + to.yl], r.vr.at[k - 1], r.vred_ss.at[k - 1], r.vred_rs.at[k - 1], to)

    for k in range(1, 8):
        post(vred(k))
    gm_sib.wait_recv()
    r.rm0[...] = (r.rm0[...].astype(F32) + r.gm[:, :, :, me.c].astype(F32)).astype(BF)

    def rmx_copy(d):
        to = shifted(me, "x", d)
        return remote(r.rm0.at[:, :, to.x], r.rmx.at[d - 1], r.rmx_ss.at[d - 1], r.rmx_rs.at[d - 1], to)

    for d in (1, 3, 2):
        post(rmx_copy(d))
    rs_next(1)
    for k in range(1, 8):
        vred(k).wait_recv()
    total = r.vg[seq]
    for k in range(7):
        total += r.vr[k]
    r.vx[me.x] = total

    def vx_copy(d, back=False):
        at = r.vx.at[shifted(me, "x", -d).x] if back else r.vx.at[me.x]
        return remote(at, at, r.vx_ss.at[d], r.vx_rs.at[d], shifted(me, "x", d))

    for d in (1, 2, 3):
        post(vx_copy(d))
    for d in (1, 3, 2):
        rmx_copy(d).wait_recv()
    summed = r.rm0[:, :, me.x].astype(F32)
    for d in range(3):
        summed += r.rmx[d].astype(F32)
    r.rmy[...] = summed.astype(BF)
    for half in range(2):
        for yh in range(2):
            for kind in range(3):
                u = 8 * kind + 2 * me.z + half
                owner = lax.div(u, 3)
                to = moved(me, yh=yh, z=lax.div(owner, 2), yl=lax.rem(owner, 2))
                slot = (lax.rem(u, 3), ypos)
                alone = (me.yh == yh) & (owner == seq)
                post_unless(
                    alone,
                    r.rmy.at[half, yh, :, pl.ds(TOK * kind, TOK)],
                    r.rmf.at[slot],
                    r.rmf_ss.at[half, yh, kind],
                    r.rmf_rs.at[slot],
                    to,
                )
    for d in (1, 2, 3):
        vx_copy(d, True).wait_recv()
    ours = me.yh * 2 + me.c
    r.vy[ours] = r.vx[0] + r.vx[1] + r.vx[2] + r.vx[3]
    pairs = ((sib, 0), (shifted(me, "y", 2), 1), (shifted(sib, "y", 2), 2))

    def vy_copy(k, back=False):
        to = pairs[k][0]
        at = r.vy.at[to.yh * 2 + to.c] if back else r.vy.at[ours]
        return remote(at, at, r.vy_ss.at[k], r.vy_rs.at[k], to)

    for k in range(3):
        post(vy_copy(k))
    rs_next(2)

    d_first = jnp.zeros((TOK, D), F32)
    for b in range(4):
        take_block(DF, b, r.df_recv.at[b])
        d_first += r.df_recv[b].astype(F32)
    r.gin[...] = r.mid[...] + norm_back(d_first, gain1, r.n1[...], rstd1)

    for t in range(3):
        _, total = rs_sum(t, 2)
        at = slice(16 * t, 16 * t + 16)
        r.gexp[at, :] = total[:, 0:SHARD]
        r.gshr[at, :] = total[:, SHARD:MERGE]
        r.gmerge[at, :] = total[:, MERGE : MERGE + 96]
    for k in range(3):
        vy_copy(k, True).wait_recv()
    r.vout[...] = r.vy[0] + r.vy[1] + r.vy[2] + r.vy[3]
    for i in range(3):
        total = jnp.zeros((48, TOK), F32)
        for y in range(4):
            arrived(r.rmf.at[i, y], r.rmf_ss.at[0, 0, 0], r.rmf_rs.at[i, y])
            total += r.rmf[i, y].astype(F32)
        r.gmix[:, 96 * i : 96 * i + 96] = total[:, 0:96]
    for finish in pending:
        finish()


def scratches():
    v, dma = pltpu.VMEM, pltpu.SemaphoreType.DMA
    third, blocks = (16, WIDE), (2, 4, 2, 48)
    s = {
        "w": v((4, 2) + blocks + (WIDE,), BF),
        "g": v((4, 2) + blocks + (WIDE,), BF),
        "r0": v((4, 2, 2, 4, 48, WIDE), BF),
        "rb1": [v((3, 2, 2, 4) + third, BF), v((3, 4, 2, 2) + third, BF), v((3, 4, 4) + third, BF)],
        "rb2": [v((3, 4) + third, BF), v((3, 2, 2) + third, BF), v((3, 4) + third, BF)],
        "rb3": [v((3,) + third, BF) for _ in range(3)],
        "units": v((3, 48, TOK), BF),
        "wm": v((2,) + blocks + (SHARD,), BF),
        "gm": v((2,) + blocks + (SHARD,), BF),
        "rm0": v((2, 2, 4, 48, SHARD), BF),
        "rmx": v((3, 2, 2, 48, SHARD), BF),
        "rmy": v((2, 2, 48, SHARD), BF),
        "rmf": v((3, 4, 48, TOK), BF),
        "vecs": v((8, 16, TOK), F32),
        "segs": v((2, 8, TOK), F32),
        "xall": v((4, TOK, D), BF),
        "n1all": v((4, TOK, D), F32),
        "fall": v((4, TOK, D), BF),
        "fallt": v((D, 4 * TOK), BF),
        "q_all": v((4, TOK, 256), BF),
        "kv_all": v((4, 2, TOK, SHARD), BF),
        "kvt": v((SHARD, 8 * TOK), BF),
        "lse": v((4, 8, TOK), F32),
        "dkv": v((8 * TOK, SHARD), F32),
        "dkv_sib": v((4, TOK, SHARD), BF),
        "dkv_got": v((4, TOK, SHARD), BF),
        "dq": v((4, TOK, 256), BF),
        "dpad": v((2, 4 * TOK, SHARD), BF),
        "df_send": v((4, TOK, D), BF),
        "df_recv": v((4, TOK, D), BF),
    }
    for name in ("att_send", "att_recv", "do_send", "do_recv"):
        s[name] = v((4, TOK, 256), BF)
    for name in ("mid", "n1", "n2", "mlp", "dsec"):
        s[name] = v((TOK, D), F32)
    for name in ("att", "second", "dbr"):
        s[name] = v((TOK, D), BF)
    for name in ("cott", "secondt", "attt"):
        s[name] = v((D, TOK), BF)
    for name, count in (("vg", 8), ("vr", 7), ("vx", 4), ("vy", 4)):
        s[name] = v((count, 16, TOK), F32)
    sems = {
        "ag": (3, 3, 3), "hand": (3, 4), "ex": (4, 4), "wm1": (3, 4), "wm2": (4,), "wms": (4,), "vec": (7,), "one": (1,),
        "kvs": (5,), "rs0": (9,), "rs": (3, 3, 3), "rm0": (1,), "rmx": (3,), "rmf": (2, 2, 3), "vred": (7,), "vx": (4,),
        "vy": (3,),
    }
    for name, shape in sems.items():
        s[name + "_ss"] = dma(shape)
        s[name + "_rs"] = dma(shape)
    s["wm1_rs"] = dma((2, 2, 3))
    s["rmf_rs"] = dma((3, 4))
    return s


def finish(hidden, gin, gmix, gmerge, gexp, gshr, vout, *outs):
    for ref, out in zip((hidden, gin, gmix, gmerge, gexp, gshr), outs[:6], strict=True):
        out[...] = ref[...]
    v = vout[...]
    rows = (FIRST_GAIN, FIRST_SHIFT, MERGE_BIAS, SECOND_GAIN, SECOND_SHIFT, SHRINK_BIAS)
    for row, out in zip(rows, outs[6:12], strict=True):
        out[...] = v[row : row + 1, 0:96].reshape(96)
    outs[12][...] = lanes(v[MIXER_BIAS : MIXER_BIAS + 1, 0:96], v[MIXER_BIAS + 1 : MIXER_BIAS + 2, 0:96]).reshape(192)
    outs[13][...] = lanes(*[v[EXPAND_BIAS + k : EXPAND_BIAS + k + 1] for k in range(3)]).reshape(SHARD)


def body(
    residual_in, cotangent, segments, first_gain, first_shift, mixer_weight, mixer_bias, merge_weight, merge_bias,
    second_gain, second_shift, expand_weight, expand_bias, shrink_weight, shrink_bias,
):
    vmem = pl.BlockSpec(memory_space=pltpu.VMEM)
    scratch = scratches()
    shapes = [((TOK, D), BF), ((TOK, D), F32), ((48, 288), F32), ((48, 96), F32), ((48, SHARD), F32), ((48, SHARD), F32)]
    held = [jax.ShapeDtypeStruct(*s) for s in shapes]
    parts = pl.pallas_call(
        functools.partial(kernel, IN + OUT + tuple(scratch)),
        out_shape=held + [jax.ShapeDtypeStruct((16, TOK), F32)],
        in_specs=[vmem] * len(IN),
        out_specs=[vmem] * len(OUT),
        scratch_shapes=list(scratch.values()),
        compiler_params=pltpu.CompilerParams(
            collective_id=0, has_side_effects=True, vmem_limit_bytes=62 * 1024 * 1024
        ),
    )(
        residual_in[0], cotangent[0], segments.reshape(8, TOK), mixer_weight, merge_weight, expand_weight,
        shrink_weight.T, first_gain, first_shift, mixer_bias, merge_bias, second_gain, second_shift, expand_bias,
        shrink_bias,
    )
    vectors = [jax.ShapeDtypeStruct((n,), F32) for n in (96, 96, 96, 96, 96, 96, 192, SHARD)]
    hidden, gin, gmix, gmerge, gexp, gshr, fg, fs, mb, sg, ss, sb, xb, eb = pl.pallas_call(
        finish, out_shape=held + vectors, in_specs=[vmem] * 7, out_specs=[vmem] * 14
    )(*parts)
    return hidden[None], gin[None], fg, fs, gmix, xb, gmerge, mb, sg, ss, gexp, eb, gshr.T, sb


def solution(mesh):
    vector, matrix = P("seq"), P("dp", "seq")
    tokens = P("dp", "seq", None)
    return jax.shard_map(
        body,
        mesh=mesh,
        in_specs=(
            tokens, tokens, P("dp", None), vector, vector, matrix, vector, matrix, vector, vector, vector, matrix, vector,
            P("seq", "dp"), vector,
        ),
        out_specs=(
            tokens, tokens, vector, vector, matrix, vector, matrix, vector, vector, vector, matrix, vector,
            P("seq", "dp"), vector,
        ),
        check_vma=False,
    )
```

time: 161 us -> 137 us (0.85)
  local copies, waits for them, and re-layouts: 11.1 us -> 0 us
  Pallas kernels: 145 us -> 135 us
  other arithmetic: 2.8 us -> 0 us
    pallas_call x1 -> x2, Pallas kernels: 145 us -> 135 us  [the longest x1 133 us: body(): pl.pallas_call(functools.partial(kernel, IN + OUT + tuple(scratch)), out_...]
    unnamed x22 -> x0, local copies, waits for them, and re-layouts: 5.45 us -> none
    reshape x2 -> x0, local copies, waits for them, and re-layouts: 1.9 us -> none  [the longest x1 1.25 us: body(): vout[8:11].reshape(SHARD)]
where the time goes in v2:
time: 137 us; the launch traced here: 136 us
  Pallas kernels  135 us (99%)
    pallas_call x1, Pallas kernels, body(): pl.pallas_call(functools.partial(kernel, IN + OUT + tuple(scratch)), out_...  133 us

profile of v2, /device:TPU:1, one launch (start us, length us, event | category | flops | bytes accessed | tf_op | source)
XLA Modules:
  0.0 135.6 jit_solution(10387127300824674547)
XLA Ops:
  0.7 132.6 %shard_map.254 = (bf16[128,768]{1,0:T(8,128)(2,1)}, f32[128,768]{1,0:T(8,128)}, f32[48,288]{1,0:T(8,128)}, f32[48,96]{1,0:T(8,128)}, f32[48,384]{1,0:T(8,128)}, /*index=5*/f32[48,384]{1,0:T(8,128)}, f32[16,128]{1,0:T(8,128)}) custom-call(bf16[128,768]{1,0:T(8,128)(2,1)} %bitcast.7, bf16[128,768]{1,0:T(8,128)(2,1)} %bitcast.8, s32[8,128]{1,0:T(8,128)} %bitcast.10, ...), custom_call_target="tpu_custom_call" | custom-call | tf_op jit(solution)/shard_map/pallas_call | solution.py:755
  133.3 2.1 %shard_map.255 = (bf16[128,768]{1,0:T(8,128)(2,1)}, f32[128,768]{1,0:T(8,128)}, f32[48,288]{1,0:T(8,128)}, f32[48,96]{1,0:T(8,128)}, f32[48,384]{1,0:T(8,128)}, ...) custom-call(bf16[128,768]{1,0:T(8,128)(2,1)} %get-tuple-element.35.h, ...), custom_call_target="tpu_custom_call" | custom-call | tf_op jit(solution)/shard_map/pallas_call | solution.py:770

commit v3 on v2

v3 whole, which is shorter than its diff:
```python
import functools
import types

import jax
import jax.numpy as jnp
from jax import lax
from jax.experimental import pallas as pl
from jax.experimental.pallas import tpu as pltpu
from jax.sharding import PartitionSpec as P


D = 768
HD = 64
TOK = 128
SHARD = 384
WIDE = 768
EPS = 1e-05
NEG = -1e30
MESH = pl.DeviceIdType.MESH
BF = jnp.bfloat16
F32 = jnp.float32
SENDS, RECVS = 45, 46
FIRST_GAIN, FIRST_SHIFT, MIXER_BIAS, MERGE_BIAS, SECOND_GAIN, SECOND_SHIFT, SHRINK_BIAS, EXPAND_BIAS = 0, 1, 2, 4, 5, 6, 7, 8


def place_of():
    dp, seq = lax.axis_index("dp"), lax.axis_index("seq")
    return types.SimpleNamespace(
        x=lax.rem(lax.div(dp, 2), 4),
        yh=lax.div(dp, 8),
        yl=lax.rem(seq, 2),
        z=lax.div(seq, 2),
        c=lax.rem(dp, 2),
    )


def moved(at, **to):
    new = types.SimpleNamespace(**vars(at))
    for name, value in to.items():
        setattr(new, name, value)
    return new


def shifted(at, axis, d):
    d = d % 4
    if axis == "x":
        return moved(at, x=lax.rem(at.x + d, 4))
    if axis == "z":
        return moved(at, z=lax.rem(at.z + d, 4))
    y = lax.rem(at.yh * 2 + at.yl + d, 4)
    return moved(at, yh=lax.div(y, 2), yl=lax.rem(y, 2))


def device(at):
    return (at.yh * 8 + at.x * 2 + at.c, at.z * 2 + at.yl)


def nn(a, b):
    return jnp.dot(a, b, preferred_element_type=F32)


def nt(a, b):
    return lax.dot_general(a, b, (((1,), (1,)), ((), ())), preferred_element_type=F32)


def remote(src, dst, send, recv, to):
    return pltpu.make_async_remote_copy(
        src_ref=src, dst_ref=dst, send_sem=send, recv_sem=recv, device_id=device(to), device_id_type=MESH
    )


def norm_parts(v):
    centred = v - jnp.mean(v, axis=-1, keepdims=True)
    rstd = lax.rsqrt(jnp.mean(centred * centred, axis=-1, keepdims=True) + EPS)
    return centred * rstd, rstd


def norm_back(dy, gain, normed, rstd):
    dn = dy * gain
    return rstd * (
        dn
        - jnp.mean(dn, axis=-1, keepdims=True)
        - normed * jnp.mean(dn * normed, axis=-1, keepdims=True)
    )


def col_sums(v):
    return jnp.sum(v.astype(F32), axis=0, keepdims=True)


def turned(v):
    return v.astype(F32).T.astype(BF)


def lanes(*pieces):
    return jnp.concatenate(pieces, axis=1)


def tile(k):
    return pl.ds(pl.multiple_of(k * TOK, TOK), TOK)


IN = (
    "x_in", "cot_in", "seg_in", "mixer_in", "merge_in", "expand_in", "shrink_in", "fgain_in", "fshift_in", "mixb_in",
    "mergeb_in", "sgain_in", "sshift_in", "expandb_in", "shrinkb_in",
)
OUT = ("hidden", "gin", "gmix", "gmerge", "gexp", "gshr", "vout")


def kernel(names, *refs):
    r = types.SimpleNamespace(**dict(zip(names, refs, strict=True)))
    me = place_of()
    sib = moved(me, c=1 - me.c)
    swap = moved(me, yl=me.c, c=me.yl)
    here = me.yl == me.c
    seq = me.z * 2 + me.yl
    ypos = me.yh * 2 + me.yl
    pending = []
    sends, recvs = {}, {}

    def send_of(*key):
        return r.send.at[sends.setdefault(key, len(sends))]

    def recv_of(*key):
        return r.recv.at[recvs.setdefault(key, len(recvs))]

    def copy_to(to, src, dst, *key, recv=None):
        return remote(src, dst, send_of(*key), recv_of(*(recv or key)), to)

    def arrived(size, *key):
        remote(size, size, r.send.at[0], recv_of(*key), sib).wait_recv()

    def wait_sent(size, *key):
        remote(size, size, send_of(*key), r.recv.at[0], sib).wait_send()

    def sent(size, *key):
        pending.append(lambda: wait_sent(size, *key))

    def sent_unless(alone, size, *key):
        def finish():
            @pl.when(jnp.logical_not(alone))
            def _():
                wait_sent(size, *key)

        pending.append(finish)

    def start_unless(alone, to, src, dst, *key, recv=None):
        @pl.when(alone)
        def _():
            pltpu.make_async_copy(src, dst, recv_of(*(recv or key))).start()

        @pl.when(jnp.logical_not(alone))
        def _():
            copy_to(to, src, dst, *key, recv=recv).start()

    zero32 = jnp.zeros((48, 32), BF)
    for i in range(3):
        r.units[i] = lanes(r.mixer_in[:, 96 * i : 96 * i + 96], zero32)
    own = (me.z, me.yl, me.yh, me.x, me.c)
    r.wz[own[1:]] = lanes(r.expand_in[...], r.shrink_in[...])
    r.m_w[own] = lanes(r.merge_in[...], zero32)
    mixb = r.mixb_in[...].astype(F32).reshape(1, 192)
    small = [(FIRST_GAIN, r.fgain_in), (FIRST_SHIFT, r.fshift_in), (MERGE_BIAS, r.mergeb_in)]
    small += [(SECOND_GAIN, r.sgain_in), (SECOND_SHIFT, r.sshift_in), (SHRINK_BIAS, r.shrinkb_in)]
    for row, ref in small:
        r.vecs[seq, row : row + 1, 0:96] = ref[...].astype(F32).reshape(1, 96)
    expb = r.expandb_in[...].astype(F32).reshape(1, SHARD)
    for k in range(2):
        r.vecs[seq, MIXER_BIAS + k : MIXER_BIAS + k + 1, 0:96] = mixb[:, 96 * k : 96 * k + 96]
    for k in range(3):
        r.vecs[seq, EXPAND_BIAS + k : EXPAND_BIAS + k + 1, :] = expb[:, TOK * k : TOK * k + TOK]
    r.segs[0] = r.seg_in[...].astype(F32)

    peers = [shifted(shifted(me, "z", dz), "y", dy) for dz in range(4) for dy in range(4) if dz or dy]
    peers += [shifted(me, "x", d) for d in (1, 2, 3)] + [sib, shifted(sib, "y", 2)]
    peers += [moved(shifted(me, "z", d), yl=1 - me.yl, c=1 - me.c) for d in range(4)]
    peers += [shifted(shifted(at, "x", d), "y", dy) for d in (1, 2, 3) for at, dy in ((sib, 0), (me, 2), (sib, 2))]
    barrier = pltpu.get_barrier_semaphore()
    for p in peers:
        pl.semaphore_signal(barrier, inc=1, device_id=device(p), device_id_type=MESH)
    pl.semaphore_wait(barrier, len(peers))

    def send_block(b, src):
        start_unless(here & (me.z == b), moved(swap, z=b), src, r.df_recv.at[me.z], "block")

    def take_blocks():
        arrived(r.df_recv, "block")

        def finish():
            @pl.when(here)
            def _():
                wait_sent(r.df_recv.at[0:3], "block")

            @pl.when(jnp.logical_not(here))
            def _():
                wait_sent(r.df_recv, "block")

        pending.append(finish)

    def send_own(name):
        at = getattr(r, name).at[me.z]
        for d in (1, 3, 2):
            copy_to(shifted(me, "z", d), at, at, name).start()

    def send_along(name, src_of, order=(1, 3, 2)):
        for d in order:
            to = shifted(me, "z", d)
            copy_to(to, src_of(to.z), getattr(r, name).at[me.z], name).start()

    def take_along(name):
        arrived(getattr(r, name).at[0:3], name)
        sent(getattr(r, name).at[0:3], name)

    def send_back(src, dst, key):
        start_unless(here, swap, src, dst, key)
        sent_unless(here, src, key)

    for i in range(3):
        u = 3 * seq + i
        group = lax.div(lax.rem(u, 8), 2)
        dst = r.wm.at[lax.rem(u, 2), me.yh, me.x, me.c, :, tile(lax.div(u, 8))]
        for dy in range(4):
            y = lax.rem(ypos + dy, 4)
            to = moved(me, z=group, yh=lax.div(y, 2), yl=lax.rem(y, 2))
            if dy:
                copy_to(to, r.units.at[i], dst, "unit").start()
            else:
                start_unless(group == me.z, to, r.units.at[i], dst, "unit", i, recv=("unit",))
        sent_unless(group == me.z, r.units.at[i], "unit", i)
    sent(r.rmf.at[:, 0:3], "unit")

    send_back(r.x_in, r.xall.at[me.z], "x")

    @pl.when(here)
    def _():
        arrived(r.xall.at[0], "x")
        send_own("xall")

    def seq_peer(k):
        at = shifted(me, "z", k // 2)
        return moved(at, yl=1 - me.yl) if k % 2 else at

    for k in range(1, 8):
        copy_to(seq_peer(k), r.vecs.at[seq], r.vecs.at[seq], "vec").start()
    sent(r.vr, "vec")

    def plane(ref, d):
        return ref.at[(slice(None),) * (len(ref.shape) - 4) + (lax.rem(me.x + 4 - d, 4), me.c)]

    def plane_start(ref, key):
        at = plane(ref, 0)
        for d in (1, 3, 2):
            copy_to(shifted(me, "x", d), at, at, key, recv=(key, d)).start()
        copy_to(sib, at, at, key, "hand").start()
        every = (slice(None),) * (len(ref.shape) - 4)
        sent(ref.at[every + (slice(0, 3), me.c)], key)
        sent(ref.at[every + (slice(0, 4), me.c)], key, "hand")

    def plane_hand(ref, key):
        for d in (1, 3, 2):
            at = plane(ref, d)
            arrived(at, key, d)
            copy_to(sib, at, at, key, "hand").start()

    def plane_finish(ref, key):
        every = (slice(None),) * (len(ref.shape) - 4)
        arrived(ref.at[every + (slice(0, 4), 1 - me.c)], key, "hand")

    def column(d):
        at = shifted(me, "y", -d)
        return r.wz.at[at.yl, at.yh, :, me.c]

    def column_start():
        for d in (1, 3, 2):
            copy_to(shifted(me, "y", d), column(0), column(0), "column", recv=("column", d)).start()
        copy_to(sib, column(0), column(0), "column", "hand").start()
        sent(r.wz.at[0, :, 0:3], "column")
        sent(r.wz.at[:, :, :, me.c], "column", "hand")

    def column_hand():
        for d in (1, 3, 2):
            arrived(column(d), "column", d)
            copy_to(sib, column(d), column(d), "column", "hand").start()

    def column_finish():
        arrived(r.wz.at[:, :, :, 1 - me.c], "column", "hand")

    copy_to(sib, r.segs.at[0], r.segs.at[1], "seg").start()
    sent(r.segs.at[0], "seg")
    own = r.wz.at[me.yl, me.yh, me.x, me.c]
    for d in (1, 3, 2):
        copy_to(shifted(me, "x", d), own, own, "hidden").start()
    sent(r.gy, "hidden")
    around = [(dz, dy) for dz in (1, 3, 0, 2) for dy in (0, 1, 3, 2) if dz or dy]
    at = r.m_w.at[me.z, me.yl, me.yh, me.x, me.c]
    for dz, dy in around:
        copy_to(shifted(shifted(me, "z", dz), "y", dy), at, at, "merge").start()
    sent(r.m_y, "merge")
    send_back(r.cot_in, r.call.at[me.z], "cot")
    arrived(r.wm.at[:, :, me.x, me.c], "unit")

    plane_start(r.wm, "mixer")
    @pl.when(jnp.logical_not(here))
    def _():
        arrived(r.xall.at[0], "x")
        send_own("xall")

    arrived(r.gy, "hidden")
    column_start()
    arrived(r.vr, "vec")

    def whole(row):
        return jnp.concatenate([r.vecs[s, row : row + 1, 0:96] for s in range(8)], axis=1)


    n1, rstd1 = norm_parts(r.x_in[...].astype(F32))
    r.n1[...] = n1
    gain1, shift1 = whole(FIRST_GAIN), whole(FIRST_SHIFT)
    plane_hand(r.wm, "mixer")
    take_along("xall")
    arrived(r.call.at[0], "cot")
    send_own("call")
    for b in range(4):
        normed, _ = norm_parts(r.xall[b].astype(F32))
        r.n1all[b] = normed
        first = normed * gain1 + shift1
        r.fall[b] = first.astype(BF)
        r.fallt[:, :, :, TOK * b : TOK * b + TOK] = turned(first.astype(BF)).reshape(8, 2, 48, TOK)
    plane_finish(r.wm, "mixer")

    at = r.fallt.at[:, 1 - me.c]
    copy_to(sib, at, r.fallt_sib, "first").start()
    sent(r.fallt_sib, "first")
    def mixer(half, first, count):
        at = slice(TOK * first, TOK * (first + count))
        return r.wm[half, :, :, :, :, at].reshape(D, TOK * count)

    first = r.fall[...].reshape(4 * TOK, D)

    def mixer_bias(at, half):
        row = MIXER_BIAS + half
        return r.vecs[at, row : row + 1, 0:96]

    kv0, kv1 = nn(first, mixer(0, 1, 2)), nn(first, mixer(1, 1, 2))
    keys = lanes(kv0[:, 0:96], kv1[:, 0:96]).astype(BF)
    vbias = lanes(mixer_bias(4 + me.z, 0), mixer_bias(4 + me.z, 1))
    values = (lanes(kv0[:, 128:224], kv1[:, 128:224]) + vbias).astype(BF)
    packed = lanes(keys, values[:, 128:192], values[:, 0:128])
    for b in range(4):
        r.kv_all[b, me.c] = packed[TOK * b : TOK * b + TOK]
    at = r.kv_all.at[:, me.c]
    copy_to(sib, at, at, "kv").start()
    sent(at, "kv")
    arrived(r.m_y, "merge")
    plane_start(r.m_w, "merge x")
    qbias = lanes(mixer_bias(me.z, 0), mixer_bias(me.z, 1))
    q = lanes(nn(first, mixer(0, 0, 1))[:, 0:96], nn(first, mixer(1, 0, 1))[:, 0:96])
    q = (q + qbias).astype(BF) * jnp.asarray(0.125, BF)
    q = lanes(q, jnp.zeros((4 * TOK, 64), BF))
    for b in range(4):
        r.q_all[b] = q[TOK * b : TOK * b + TOK]
        r.kvt[:, tile(2 * b + me.c)] = turned(packed[TOK * b : TOK * b + TOK])
    arrived(r.segs.at[1], "seg")
    arrived(r.kv_all.at[:, 1 - me.c], "kv")
    for b in range(4):
        r.kvt[:, tile(2 * b + 1 - me.c)] = turned(r.kv_all[b, 1 - me.c])

    seg = jnp.where(here, r.segs[0], r.segs[1])

    def starts(bound):
        return jnp.sum(jnp.where(seg < bound, 1.0, 0.0), axis=(0, 1), keepdims=True).astype(jnp.int32)

    begin1, begin2 = starts(0.5), starts(1.5)
    lane = lax.broadcasted_iota(jnp.int32, (TOK, TOK), 1)

    def allowed_of(b):
        n = 256 * (b + 1)
        qpos = 256 * b + TOK * me.c + lax.broadcasted_iota(jnp.int32, (1, TOK), 1)
        low = jnp.where(qpos < begin1, 0, jnp.where(qpos < begin2, begin1, begin2))
        kpos = lax.broadcasted_iota(jnp.int32, (n, TOK), 0)
        return (kpos <= qpos) & (kpos >= low)

    def keys_of(b, h):
        at = slice(0, 128) if h < 2 else slice(128, 256)
        return r.kv_all[0 : b + 1, :, :, at].reshape(256 * (b + 1), TOK)

    def values_of(b, h):
        at = slice(256, 384) if h < 2 else slice(128, 256)
        return r.kv_all[0 : b + 1, :, :, at].reshape(256 * (b + 1), TOK)

    K_ROWS = (0, 64, 128)
    V_ROWS = (256, 320, 192)

    def one_head(v, upper):
        keep = lane >= 64 if upper else lane < 64
        return jnp.where(keep, v, jnp.zeros_like(v))

    def query_of(b, h):
        return one_head(r.q_all[b, :, 0:128] if h < 2 else r.q_all[b, :, 128:256], h == 1)

    spare = []
    for b in (3, 2, 1, 0):
        n = 256 * (b + 1)
        allowed = allowed_of(b)
        outs = []
        for h in range(3):
            scores = jnp.where(allowed, nt(keys_of(b, h), query_of(b, h)), NEG)
            top = jnp.max(scores, axis=0, keepdims=True)
            expo = jnp.exp(scores - top)
            total = jnp.sum(expo, axis=0, keepdims=True)
            r.lse[b, h : h + 1, :] = top + jnp.log(total)
            weights = (expo * (1.0 / total)).astype(BF)
            outs.append(nn(r.kvt[V_ROWS[h] : V_ROWS[h] + 64, 0:n], weights))
        r.att_all[me.z, b] = jnp.concatenate(outs[0:2], axis=0).T.astype(BF)
        spare.append(outs[2])
        ready = [b]
        if b % 2 == 0:
            r.att_all[me.z, 4 + b // 2] = jnp.concatenate([spare[-1], spare[-2]], axis=0).T.astype(BF)
            ready.append(4 + b // 2)
        for k in ready:
            for d in (1, 3, 2):
                at = r.att_all.at[me.z, k]
                copy_to(shifted(me, "z", d), at, at, "att", recv=("att", b // 2)).start()
        if b == 1:
            column_hand()
        if b == 0:
            plane_hand(r.m_w, "merge x")
    sent(r.att_all.at[0:3], "att")
    take_along("call")
    for b in range(4):
        r.cott[:, TOK * b : TOK * b + TOK] = turned(r.call[b])
    plane_finish(r.m_w, "merge x")
    for s in range(8):
        r.mc[:, 96 * s : 96 * s + 96] = r.m_w[s // 2, s % 2].reshape(D, TOK)[:, 0:96]

    gain2, shift2 = whole(SECOND_GAIN), whole(SECOND_SHIFT)
    for pair in (1, 0):
        arrived(r.att_all.at[0:3, 0:3], "att", pair)
        for b in (2 * pair + 1, 2 * pair):
            at = slice(64 * (b % 2), 64 * (b % 2) + 64)
            r.att[b] = lanes(*[v for g in range(4) for v in (r.att_all[g, b], r.att_all[g, 4 + pair, :, at])])
        rows = slice(2 * pair, 2 * pair + 2)
        branch = nn(r.att[rows].reshape(2 * TOK, D), r.mc[...])
        middle = r.xall[rows].reshape(2 * TOK, D).astype(F32) + branch + whole(MERGE_BIAS)
        r.mid[rows] = middle.reshape(2, TOK, D)
        n2, _ = norm_parts(middle)
        r.second[rows] = (n2 * gain2 + shift2).astype(BF).reshape(2, TOK, D)
    column_finish()

    def hidden(first):
        return lanes(*[r.wz[yl, :, :, :, :, first : first + SHARD].reshape(D, SHARD) for yl in range(2)])

    bias = lanes(*[r.vecs[2 * me.z + yl, EXPAND_BIAS + k : EXPAND_BIAS + k + 1] for yl in range(2) for k in range(3)])
    for step in range(2):
        blocks = [shifted(me, "z", d).z for d in ((2, 1), (3, 0))[step]]

        def rows_of(ref, blocks=blocks):
            return jnp.concatenate([ref[b] for b in blocks], axis=0)

        pre = nn(rows_of(r.second), hidden(0)) + bias
        square = pre * pre
        tanh = jnp.tanh(0.7978845608028654 * (pre + 0.044715 * square * pre))
        active = (0.5 * pre * (1.0 + tanh)).astype(BF)
        slope = 0.5 * (1.0 + tanh) + 0.5 * pre * (1.0 - tanh * tanh) * (
            0.7978845608028654 * (1.0 + 0.134145 * square)
        )
        d_pre = (nn(rows_of(r.call), hidden(SHARD)) * slope).astype(BF)
        d_second = nt(d_pre, hidden(0)).astype(BF)
        for i, b in enumerate(blocks):
            at = slice(TOK * i, TOK * i + TOK)
            r.active[b] = active[at]
            r.dpre[b] = d_pre[at]
            (r.dsec_send if (step, i) != (1, 1) else r.dsec)[b] = d_second[at]
        send_along("dsec", lambda z: r.dsec_send.at[z], ((2, 1), (3,))[step])

    sums = col_sums(r.dpre[...].reshape(4 * TOK, WIDE))
    r.vg[...] = jnp.zeros((8, 16, TOK), F32)
    for yl in range(2):
        for k in range(3):
            at = TOK * (3 * yl + k)
            r.vg[2 * me.z + yl, EXPAND_BIAS + k : EXPAND_BIAS + k + 1, :] = sums[:, at : at + TOK]
    for b in range(4):
        r.secondt[:, TOK * b : TOK * b + TOK] = turned(r.second[b])
    shape = (2, 4, 2, 48, SHARD)
    for first, left, right in ((0, r.secondt, r.dpre), (SHARD, r.cott, r.active)):
        grad = nn(left[...], right[...].reshape(4 * TOK, WIDE)).astype(BF)
        for yl in range(2):
            r.gz[yl, :, :, :, :, first : first + SHARD] = grad[:, SHARD * yl : SHARD * yl + SHARD].reshape(shape)
    copy_to(sib, r.gz.at[:, :, :, 1 - me.c], r.gz0, "hidden", "pair").start()
    sent(r.gz0, "hidden", "pair")
    result = nt(r.active[...].reshape(4 * TOK, WIDE), hidden(SHARD)).astype(BF)
    for b in range(4):
        r.res_send[b] = result[TOK * b : TOK * b + TOK]
    r.attt[...] = turned(r.att[me.z])

    def pair_sum(ref, own, key):
        arrived(ref, key, "pair")
        every = (slice(None),) * (len(ref.shape) - 2)
        ref[...] = (ref[...].astype(F32) + own[every + (me.c,)].astype(F32)).astype(BF)

    def plane_send(ref, got, key):
        every = (slice(None),) * (len(ref.shape) - 3)
        for d in (1, 3, 2):
            to = shifted(me, "x", d)
            copy_to(to, ref.at[every + (to.x,)], got.at[d - 1], key, "sum").start()
        sent(got, key, "sum")

    def plane_total(ref, got, key):
        arrived(got, key, "sum")
        total = ref[(slice(None),) * (len(ref.shape) - 3) + (me.x,)].astype(F32)
        for d in range(3):
            total += got[d].astype(F32)
        return total.astype(BF)

    pair_sum(r.gz0, r.gz, "hidden")
    for d in (1, 3, 2):
        to = shifted(me, "y", d)
        copy_to(to, r.gz0.at[to.yl, to.yh], r.gzy.at[d - 1], "hidden y").start()
    sent(r.gzy, "hidden y")
    take_along("dsec")

    d_second = sum(r.dsec[b].astype(F32) for b in range(4))
    cot = r.call[me.z].astype(F32)
    n2, rstd2 = norm_parts(r.mid[me.z])
    d_middle = cot + norm_back(d_second, gain2, n2, rstd2)
    d_branch = d_middle.astype(BF)
    r.dbr[...] = d_branch
    zeros = jnp.zeros((TOK, 32), BF)
    d_att = nt(d_branch, r.mc[...]).astype(BF)
    for b in range(4):
        o = d_att[:, 192 * b : 192 * b + 192]
        r.do_send[b] = lanes(o[:, 0:128], jnp.zeros((TOK, 64), BF), o[:, 128:192])
    send_along("do_recv", lambda z: r.do_send.at[z])
    send_along("res_recv", lambda z: r.res_send.at[z])
    r.res_recv[me.z] = r.res_send[me.z]
    r.do_recv[me.z] = r.do_send[me.z]

    r.dmid[...] = d_middle
    send_back(r.dmid, r.dmid_recv, "dmid")

    for s in range(8):
        right = lanes(r.dbr[:, 96 * s : 96 * s + 96], zeros)
        r.m_g[s // 2, s % 2] = nn(r.attt[...], right).astype(BF).reshape(2, 4, 2, 48, TOK)
    copy_to(sib, r.m_g.at[:, :, :, :, 1 - me.c], r.m_r0, "merge", "pair").start()
    sent(r.m_r0, "merge", "pair")

    g_gain_b = col_sums(d_second * n2)
    g_shift_b = col_sums(d_second)
    g_b_shrink = col_sums(cot)
    g_b_merge = col_sums(d_branch)
    rows = [(MERGE_BIAS, g_b_merge), (SECOND_GAIN, g_gain_b), (SECOND_SHIFT, g_shift_b), (SHRINK_BIAS, g_b_shrink)]
    for s in range(8):
        for row, value in rows:
            r.vg[s, row : row + 1, 0:96] = value[:, 96 * s : 96 * s + 96]

    pair_sum(r.m_r0, r.m_g, "merge")
    plane_send(r.m_r0, r.m_x, "merge")

    r.dkv[...] = jnp.zeros((8 * TOK, SHARD), F32)
    take_along("do_recv")
    sent(r.dkv_got, "dkv")

    def pair(l0, l1, r0, r1):
        return nn(jnp.concatenate([l0, l1], axis=1), jnp.concatenate([r0, r1], axis=0))

    gain_sum, shift_sum = [], []

    def finish_block(b):
        arrived(r.dkv_got.at[b], "dkv", b)
        own = pl.multiple_of(256 * b + TOK * me.c, TOK)
        dkv = (r.dkv[pl.ds(own, TOK), :] + r.dkv_got[b].astype(F32)).astype(BF)
        dq = r.dq[b]
        dv = lanes(dkv[:, 256:384], dkv[:, 192:256])
        for half in range(2):
            at = slice(96 * half, 96 * half + 96)
            r.dpad[half, b] = lanes(dq[:, at], zeros, dkv[:, at], zeros, dv[:, at], zeros)
        at = r.dpad.at[:, b]
        copy_to(sib, at, r.dpad_sib.at[:, b], "dpad").start()
        d_first = nt(r.dpad[0, b], mixer(0, 0, 3)) + nt(r.dpad[1, b], mixer(1, 0, 3))
        r.df_send[b] = d_first.astype(BF)
        if b:
            send_block(b, r.df_send.at[b])
        gain_sum.append(col_sums(d_first * r.n1all[b]))
        shift_sum.append(col_sums(d_first))

    for b in (3, 2, 1, 0):
        n = 256 * (b + 1)
        allowed = allowed_of(b)
        dqs, dss, pbs, dos, qs = [], [], [], [], []
        for h in range(3):
            q = query_of(b, h)
            do = one_head(r.do_recv[b, :, 0:128] if h < 2 else r.do_recv[b, :, 128:256], h > 0)
            scores = jnp.where(allowed, nt(keys_of(b, h), q), NEG)
            probs = jnp.exp(scores - r.lse[b, h : h + 1, :])
            dw = nt(values_of(b, h), do)
            centre = jnp.sum(probs * dw, axis=0, keepdims=True)
            ds = (probs * (dw - centre)).astype(BF)
            dqs.append(nn(r.kvt[K_ROWS[h] : K_ROWS[h] + 64, 0:n], ds))
            dss.append(ds)
            pbs.append(probs.astype(BF))
            dos.append(do)
            qs.append(q)
        dqs.append(jnp.zeros((64, TOK), F32))
        r.dq[b] = (jnp.concatenate(dqs, axis=0) * 0.125).T.astype(BF)
        r.dkv[0:n, 0:128] += pair(dss[0], dss[1], qs[0], qs[1])
        r.dkv[0:n, 128:256] += pair(dss[2], pbs[2], qs[2], dos[2])
        r.dkv[0:n, 256:384] += pair(pbs[0], pbs[1], dos[0], dos[1])
        other = pl.multiple_of(256 * b + TOK * (1 - me.c), TOK)
        r.dkv_sib[b] = r.dkv[pl.ds(other, TOK), :].astype(BF)
        copy_to(sib, r.dkv_sib.at[b], r.dkv_got.at[b], "dkv", recv=("dkv", b)).start()
        if b == 1:
            arrived(r.gzy, "hidden y")
            total = r.gz0[me.yl, me.yh].astype(F32)
            for d in range(3):
                total += r.gzy[d].astype(F32)
            r.gzx[...] = total.astype(BF)
            for d in (1, 3, 2):
                to = shifted(me, "x", d)
                copy_to(to, r.gzx.at[to.x], r.gy.at[d - 1], "hidden x").start()
            sent(r.gy, "hidden x")
        if b < 3:
            finish_block(b + 1)
    finish_block(0)
    arrived(r.fallt_sib, "first")
    for half in range(2):
        sums = col_sums(r.dpad[half].reshape(4 * TOK, SHARD))
        row = MIXER_BIAS + half
        r.vg[me.z, row : row + 1, 0:96] = sums[:, 0:96]
        r.vg[4 + me.z, row : row + 1, 0:96] = sums[:, 256:352]
    gain_a, shift_a = sum(gain_sum), sum(shift_sum)
    for s in range(8):
        r.vg[s, FIRST_GAIN : FIRST_GAIN + 1, 0:96] = gain_a[:, 96 * s : 96 * s + 96]
        r.vg[s, FIRST_SHIFT : FIRST_SHIFT + 1, 0:96] = shift_a[:, 96 * s : 96 * s + 96]

    for k in range(1, 8):
        to = seq_peer(k)
        copy_to(to, r.vg.at[to.z * 2 + to.yl], r.vr.at[k - 1], "rows").start()
    sent(r.vr, "rows")
    send_block(0, r.df_send.at[0])

    arrived(r.dpad_sib, "dpad")
    sent(r.dpad, "dpad")
    left = jnp.concatenate([r.fallt[:, me.c].reshape(D // 2, 4 * TOK), r.fallt_sib[...].reshape(D // 2, 4 * TOK)], axis=1)
    for half in range(2):
        right = [ref[half].reshape(4 * TOK, SHARD) for ref in (r.dpad, r.dpad_sib)]
        r.rm0[half] = nn(left, jnp.concatenate(right, axis=0)).astype(BF).reshape(2, 4, 48, SHARD)
    plane_send(r.rm0, r.rmx, "mixer")
    r.m_t[...] = plane_total(r.m_r0, r.m_x, "merge")
    for i, (dz, dy) in enumerate(around):
        to = shifted(shifted(me, "z", dz), "y", dy)
        copy_to(to, r.m_t.at[to.z, to.yl, to.yh], r.m_y.at[i], "merge all").start()
    sent(r.m_y, "merge all")
    take_along("res_recv")
    result = r.mid[me.z] + whole(SHRINK_BIAS)
    for b in range(4):
        result += r.res_recv[b].astype(F32)
    r.hid[...] = result.astype(BF)
    send_back(r.hid, r.hid_recv, "hid")
    arrived(r.vr, "rows")
    total = r.vg[seq]
    for k in range(7):
        total += r.vr[k]
    ours = me.yh * 8 + me.x * 2 + me.c
    r.vx[ours] = total
    others = [(at, dx, dy) for at in (me, sib) for dx in range(4) for dy in (0, 2) if dx or dy or at is sib]
    for at, dx, dy in others:
        copy_to(shifted(shifted(at, "x", dx), "y", dy), r.vx.at[ours], r.vx.at[ours], "rows all").start()
    sent(r.vx.at[0:15], "rows all")
    r.rmy[...] = plane_total(r.rm0, r.rmx, "mixer")
    for dyh in range(2):
        yh = lax.rem(me.yh + dyh, 2)
        for half in range(2):
            for kind in range(3):
                u = 8 * kind + 2 * me.z + half
                owner = lax.div(u, 3)
                to = moved(me, yh=yh, z=lax.div(owner, 2), yl=lax.rem(owner, 2))
                src = r.rmy.at[half, yh, :, pl.ds(TOK * kind, TOK)]
                dst = r.rmf.at[lax.rem(u, 3), ypos]
                if dyh:
                    copy_to(to, src, dst, "piece").start()
                else:
                    start_unless(owner == seq, to, src, dst, "piece", half, kind, recv=("piece",))
                    sent_unless(owner == seq, r.units.at[0], "piece", half, kind)
    sent(r.rmf.at[:, 0:2], "piece")
    d_first = jnp.zeros((TOK, D), F32)
    take_blocks()
    for b in range(4):
        d_first += r.df_recv[b].astype(F32)
    arrived(r.dmid_recv, "dmid")
    r.gin[...] = r.dmid_recv[...] + norm_back(d_first, gain1, r.n1[...], rstd1)

    arrived(r.hid_recv, "hid")
    r.hidden[...] = r.hid_recv[...]
    arrived(r.gy, "hidden x")
    total = r.gzx[me.x].astype(F32)
    for d in range(3):
        total += r.gy[d].astype(F32)
    r.gexp[...] = total[:, 0:SHARD]
    r.gshr[...] = total[:, SHARD:WIDE]
    arrived(r.m_y, "merge all")
    total = r.m_t[me.z, me.yl, me.yh].astype(F32)
    for i in range(15):
        total += r.m_y[i].astype(F32)
    r.gmerge[...] = total[:, 0:96]
    arrived(r.vx.at[0:15], "rows all")
    total = r.vx[0]
    for k in range(1, 16):
        total += r.vx[k]
    r.vout[...] = total
    arrived(r.rmf, "piece")
    for i in range(3):
        total = jnp.zeros((48, TOK), F32)
        for y in range(4):
            total += r.rmf[i, y].astype(F32)
        r.gmix[:, 96 * i : 96 * i + 96] = total[:, 0:96]
    for finish in pending:
        finish()
    if (len(sends), len(recvs)) != (SENDS, RECVS):
        raise ValueError((len(sends), len(recvs)))


def scratches():
    v, dma = pltpu.VMEM, pltpu.SemaphoreType.DMA
    blocks = (2, 4, 2, 48)
    s = dict(
        m_w=v((4, 2) + blocks + (TOK,), BF),
        m_g=v((4, 2) + blocks + (TOK,), BF),
        m_r0=v((4, 2, 2, 4, 48, TOK), BF),
        m_x=v((3, 4, 2, 2, 48, TOK), BF),
        m_t=v((4, 2, 2, 48, TOK), BF),
        m_y=v((15, 48, TOK), BF),
        mc=v((D, D), BF),
        wz=v((2,) + blocks + (WIDE,), BF),
        gz=v((2,) + blocks + (WIDE,), BF),
        gz0=v((2, 2, 4, 48, WIDE), BF),
        gzx=v((4, 48, WIDE), BF),
        gzy=v((3, 4, 48, WIDE), BF),
        gy=v((3, 48, WIDE), BF),
        units=v((3, 48, TOK), BF),
        wm=v((2,) + blocks + (SHARD,), BF),
        rm0=v((2, 2, 4, 48, SHARD), BF),
        rmx=v((3, 2, 2, 48, SHARD), BF),
        rmy=v((2, 2, 48, SHARD), BF),
        rmf=v((3, 4, 48, TOK), BF),
        vecs=v((8, 16, TOK), F32),
        segs=v((2, 8, TOK), F32),
        fallt=v((8, 2, 48, 4 * TOK), BF),
        fallt_sib=v((8, 48, 4 * TOK), BF),
        cott=v((D, 4 * TOK), BF),
        secondt=v((D, 4 * TOK), BF),
        attt=v((D, TOK), BF),
        q_all=v((4, TOK, 256), BF),
        kv_all=v((4, 2, TOK, SHARD), BF),
        kvt=v((SHARD, 8 * TOK), BF),
        lse=v((4, 8, TOK), F32),
        att_all=v((4, 6, TOK, TOK), BF),
        dkv=v((8 * TOK, SHARD), F32),
        dkv_sib=v((4, TOK, SHARD), BF),
        dkv_got=v((4, TOK, SHARD), BF),
        dq=v((4, TOK, 256), BF),
        dpad=v((2, 4, TOK, SHARD), BF),
        dpad_sib=v((2, 4, TOK, SHARD), BF),
        do_send=v((4, TOK, 256), BF),
        do_recv=v((4, TOK, 256), BF),
        n1all=v((4, TOK, D), F32),
        mid=v((4, TOK, D), F32),
    )
    for name in ("xall", "call", "fall", "att", "second", "dsec_send", "dsec", "res_send", "res_recv", "df_send", "df_recv"):
        s[name] = v((4, TOK, D), BF)
    for name in ("active", "dpre"):
        s[name] = v((4, TOK, WIDE), BF)
    for name in ("n1", "dmid", "dmid_recv"):
        s[name] = v((TOK, D), F32)
    for name in ("dbr", "hid", "hid_recv"):
        s[name] = v((TOK, D), BF)
    for name, count in (("vg", 8), ("vr", 7), ("vx", 16)):
        s[name] = v((count, 16, TOK), F32)
    s["send"], s["recv"] = dma((SENDS,)), dma((RECVS,))
    return s


def finish(hidden, gin, gmix, gmerge, gexp, gshr, vout, *outs):
    for ref, out in zip((hidden, gin, gmix, gmerge, gexp, gshr), outs[:6], strict=True):
        out[...] = ref[...]
    v = vout[...]
    rows = (FIRST_GAIN, FIRST_SHIFT, MERGE_BIAS, SECOND_GAIN, SECOND_SHIFT, SHRINK_BIAS)
    for row, out in zip(rows, outs[6:12], strict=True):
        out[...] = v[row : row + 1, 0:96].reshape(96)
    outs[12][...] = lanes(v[MIXER_BIAS : MIXER_BIAS + 1, 0:96], v[MIXER_BIAS + 1 : MIXER_BIAS + 2, 0:96]).reshape(192)
    outs[13][...] = lanes(*[v[EXPAND_BIAS + k : EXPAND_BIAS + k + 1] for k in range(3)]).reshape(SHARD)


def body(
    residual_in, cotangent, segments, first_gain, first_shift, mixer_weight, mixer_bias, merge_weight, merge_bias,
    second_gain, second_shift, expand_weight, expand_bias, shrink_weight, shrink_bias,
):
    vmem = pl.BlockSpec(memory_space=pltpu.VMEM)
    scratch = scratches()
    shapes = [((TOK, D), BF), ((TOK, D), F32), ((48, 288), F32), ((48, 96), F32), ((48, SHARD), F32), ((48, SHARD), F32)]
    held = [jax.ShapeDtypeStruct(*s) for s in shapes]
    parts = pl.pallas_call(
        functools.partial(kernel, IN + OUT + tuple(scratch)),
        out_shape=held + [jax.ShapeDtypeStruct((16, TOK), F32)],
        in_specs=[vmem] * len(IN),
        out_specs=[vmem] * len(OUT),
        scratch_shapes=list(scratch.values()),
        compiler_params=pltpu.CompilerParams(
            collective_id=0, has_side_effects=True, vmem_limit_bytes=62 * 1024 * 1024
        ),
    )(
        residual_in[0], cotangent[0], segments.reshape(8, TOK), mixer_weight, merge_weight, expand_weight,
        shrink_weight.T, first_gain, first_shift, mixer_bias, merge_bias, second_gain, second_shift, expand_bias,
        shrink_bias,
    )
    vectors = [jax.ShapeDtypeStruct((n,), F32) for n in (96, 96, 96, 96, 96, 96, 192, SHARD)]
    hidden, gin, gmix, gmerge, gexp, gshr, fg, fs, mb, sg, ss, sb, xb, eb = pl.pallas_call(
        finish, out_shape=held + vectors, in_specs=[vmem] * 7, out_specs=[vmem] * 14
    )(*parts)
    return hidden[None], gin[None], fg, fs, gmix, xb, gmerge, mb, sg, ss, gexp, eb, gshr.T, sb


def solution(mesh):
    vector, matrix = P("seq"), P("dp", "seq")
    tokens = P("dp", "seq", None)
    return jax.shard_map(
        body,
        mesh=mesh,
        in_specs=(
            tokens, tokens, P("dp", None), vector, vector, matrix, vector, matrix, vector, vector, vector, matrix, vector,
            P("seq", "dp"), vector,
        ),
        out_specs=(
            tokens, tokens, vector, vector, matrix, vector, matrix, vector, vector, vector, matrix, vector,
            P("seq", "dp"), vector,
        ),
        check_vma=False,
    )
```

time: 137 us -> 95.1 us (0.69)
  Pallas kernels: 135 us -> 94.1 us
    pallas_call x1, Pallas kernels: 133 us -> 92 us  [body(): pl.pallas_call(functools.partial(kernel, IN + OUT + tuple(scratch)), out_...]
where the time goes in v3:
time: 95.1 us; the launch traced here: 94.9 us
  Pallas kernels  94.1 us (99%)
    pallas_call x1, Pallas kernels, body(): pl.pallas_call(functools.partial(kernel, IN + OUT + tuple(scratch)), out_...  92 us
    pallas_call x1, Pallas kernels, body(): pl.pallas_call(finish, out_shape=held + vectors, in_specs=[vmem] * 7, out...  2.13 us

profile of v3, /device:TPU:1, one launch (start us, length us, event | category | flops | bytes accessed | tf_op | source)
XLA Modules:
  0.0 94.9 jit_solution(15785650590261339100)
XLA Ops:
  0.7 92.0 %shard_map.254 = (bf16[128,768]{1,0:T(8,128)(2,1)}, f32[128,768]{1,0:T(8,128)}, f32[48,288]{1,0:T(8,128)}, f32[48,96]{1,0:T(8,128)}, f32[48,384]{1,0:T(8,128)}, /*index=5*/f32[48,384]{1,0:T(8,128)}, f32[16,128]{1,0:T(8,128)}) custom-call(bf16[128,768]{1,0:T(8,128)(2,1)} %bitcast.7, bf16[128,768]{1,0:T(8,128)(2,1)} %bitcast.8, s32[8,128]{1,0:T(8,128)} %bitcast.10, ...), custom_call_target="tpu_custom_call" | custom-call | tf_op jit(solution)/shard_map/pallas_call | solution.py:801
  92.6 2.1 %shard_map.255 = (bf16[128,768]{1,0:T(8,128)(2,1)}, f32[128,768]{1,0:T(8,128)}, f32[48,288]{1,0:T(8,128)}, f32[48,96]{1,0:T(8,128)}, f32[48,384]{1,0:T(8,128)}, ...) custom-call(bf16[128,768]{1,0:T(8,128)(2,1)} %get-tuple-element.35.h, ...), custom_call_target="tpu_custom_call" | custom-call | tf_op jit(solution)/shard_map/pallas_call | solution.py:816

commit v4 on v3

--- a/solution.py
+++ b/solution.py
@@ -19,7 +19,7 @@
 MESH = pl.DeviceIdType.MESH
 BF = jnp.bfloat16
 F32 = jnp.float32
-SENDS, RECVS = 45, 46
+SENDS, RECVS = 47, 49
 FIRST_GAIN, FIRST_SHIFT, MIXER_BIAS, MERGE_BIAS, SECOND_GAIN, SECOND_SHIFT, SHRINK_BIAS, EXPAND_BIAS = 0, 1, 2, 4, 5, 6, 7, 8
 
 
@@ -158,7 +158,7 @@
         r.units[i] = lanes(r.mixer_in[:, 96 * i : 96 * i + 96], zero32)
     own = (me.z, me.yl, me.yh, me.x, me.c)
     r.wz[own[1:]] = lanes(r.expand_in[...], r.shrink_in[...])
-    r.m_w[own] = lanes(r.merge_in[...], zero32)
+    r.m_w[own[0:3]] = lanes(r.merge_in[...], zero32)
     mixb = r.mixb_in[...].astype(F32).reshape(1, 192)
     small = [(FIRST_GAIN, r.fgain_in), (FIRST_SHIFT, r.fshift_in), (MERGE_BIAS, r.mergeb_in)]
     small += [(SECOND_GAIN, r.sgain_in), (SECOND_SHIFT, r.sshift_in), (SHRINK_BIAS, r.shrinkb_in)]
@@ -179,23 +179,6 @@
     for p in peers:
         pl.semaphore_signal(barrier, inc=1, device_id=device(p), device_id_type=MESH)
     pl.semaphore_wait(barrier, len(peers))
-
-    def send_block(b, src):
-        start_unless(here & (me.z == b), moved(swap, z=b), src, r.df_recv.at[me.z], "block")
-
-    def take_blocks():
-        arrived(r.df_recv, "block")
-
-        def finish():
-            @pl.when(here)
-            def _():
-                wait_sent(r.df_recv.at[0:3], "block")
-
-            @pl.when(jnp.logical_not(here))
-            def _():
-                wait_sent(r.df_recv, "block")
-
-        pending.append(finish)
 
     def send_own(name):
         at = getattr(r, name).at[me.z]
@@ -292,7 +275,7 @@
         copy_to(shifted(me, "x", d), own, own, "hidden").start()
     sent(r.gy, "hidden")
     around = [(dz, dy) for dz in (1, 3, 0, 2) for dy in (0, 1, 3, 2) if dz or dy]
-    at = r.m_w.at[me.z, me.yl, me.yh, me.x, me.c]
+    at = r.m_w.at[me.z, me.yl, me.yh]
     for dz, dy in around:
         copy_to(shifted(shifted(me, "z", dz), "y", dy), at, at, "merge").start()
     sent(r.m_y, "merge")
@@ -313,16 +296,20 @@
         return jnp.concatenate([r.vecs[s, row : row + 1, 0:96] for s in range(8)], axis=1)
 
 
-    n1, rstd1 = norm_parts(r.x_in[...].astype(F32))
-    r.n1[...] = n1
     gain1, shift1 = whole(FIRST_GAIN), whole(FIRST_SHIFT)
     plane_hand(r.wm, "mixer")
+    arrived(r.m_y, "merge")
+    for yh in range(2):
+        pieces = [r.m_w[s // 2, s % 2, yh, :, 0:96] for s in range(8)]
+        r.mc[yh, me.x, me.c] = lanes(*pieces)
+    plane_start(r.mc, "merge x")
     take_along("xall")
     arrived(r.call.at[0], "cot")
     send_own("call")
     for b in range(4):
-        normed, _ = norm_parts(r.xall[b].astype(F32))
+        normed, rstd = norm_parts(r.xall[b].astype(F32))
         r.n1all[b] = normed
+        r.rstd1[b] = jnp.broadcast_to(rstd, (TOK, TOK))
         first = normed * gain1 + shift1
         r.fall[b] = first.astype(BF)
         r.fallt[:, :, :, TOK * b : TOK * b + TOK] = turned(first.astype(BF)).reshape(8, 2, 48, TOK)
@@ -351,8 +338,6 @@
     at = r.kv_all.at[:, me.c]
     copy_to(sib, at, at, "kv").start()
     sent(at, "kv")
-    arrived(r.m_y, "merge")
-    plane_start(r.m_w, "merge x")
     qbias = lanes(mixer_bias(me.z, 0), mixer_bias(me.z, 1))
     q = lanes(nn(first, mixer(0, 0, 1))[:, 0:96], nn(first, mixer(1, 0, 1))[:, 0:96])
     q = (q + qbias).astype(BF) * jnp.asarray(0.125, BF)
@@ -424,54 +409,74 @@
         if b == 1:
             column_hand()
         if b == 0:
-            plane_hand(r.m_w, "merge x")
+            plane_hand(r.mc, "merge x")
     sent(r.att_all.at[0:3], "att")
     take_along("call")
     for b in range(4):
         r.cott[:, TOK * b : TOK * b + TOK] = turned(r.call[b])
-    plane_finish(r.m_w, "merge x")
-    for s in range(8):
-        r.mc[:, 96 * s : 96 * s + 96] = r.m_w[s // 2, s % 2].reshape(D, TOK)[:, 0:96]
-
-    gain2, shift2 = whole(SECOND_GAIN), whole(SECOND_SHIFT)
+    plane_finish(r.mc, "merge x")
+    merge = r.mc[...].reshape(D, D)
+
+    column_finish()
+    gain2, shift2, b_merge = whole(SECOND_GAIN), whole(SECOND_SHIFT), whole(MERGE_BIAS)
+
+    def hidden(first):
+        return lanes(*[r.wz[yl, :, :, :, :, first : first + SHARD].reshape(D, SHARD) for yl in range(2)])
+
+    bias = lanes(*[r.vecs[2 * me.z + yl, EXPAND_BIAS + k : EXPAND_BIAS + k + 1] for yl in range(2) for k in range(3)])
+    sums2 = []
     for pair in (1, 0):
         arrived(r.att_all.at[0:3, 0:3], "att", pair)
-        for b in (2 * pair + 1, 2 * pair):
+        rows = slice(2 * pair, 2 * pair + 2)
+        for b in (2 * pair, 2 * pair + 1):
             at = slice(64 * (b % 2), 64 * (b % 2) + 64)
             r.att[b] = lanes(*[v for g in range(4) for v in (r.att_all[g, b], r.att_all[g, 4 + pair, :, at])])
-        rows = slice(2 * pair, 2 * pair + 2)
-        branch = nn(r.att[rows].reshape(2 * TOK, D), r.mc[...])
-        middle = r.xall[rows].reshape(2 * TOK, D).astype(F32) + branch + whole(MERGE_BIAS)
+        branch = nn(r.att[rows].reshape(2 * TOK, D), merge)
+        middle = r.xall[rows].reshape(2 * TOK, D).astype(F32) + branch + b_merge
         r.mid[rows] = middle.reshape(2, TOK, D)
-        n2, _ = norm_parts(middle)
-        r.second[rows] = (n2 * gain2 + shift2).astype(BF).reshape(2, TOK, D)
-    column_finish()
-
-    def hidden(first):
-        return lanes(*[r.wz[yl, :, :, :, :, first : first + SHARD].reshape(D, SHARD) for yl in range(2)])
-
-    bias = lanes(*[r.vecs[2 * me.z + yl, EXPAND_BIAS + k : EXPAND_BIAS + k + 1] for yl in range(2) for k in range(3)])
-    for step in range(2):
-        blocks = [shifted(me, "z", d).z for d in ((2, 1), (3, 0))[step]]
-
-        def rows_of(ref, blocks=blocks):
-            return jnp.concatenate([ref[b] for b in blocks], axis=0)
-
-        pre = nn(rows_of(r.second), hidden(0)) + bias
+        n2, rstd2 = norm_parts(middle)
+        second = (n2 * gain2 + shift2).astype(BF)
+        r.second[rows] = second.reshape(2, TOK, D)
+        pre = nn(second, hidden(0)) + bias
         square = pre * pre
         tanh = jnp.tanh(0.7978845608028654 * (pre + 0.044715 * square * pre))
-        active = (0.5 * pre * (1.0 + tanh)).astype(BF)
+        r.active[rows] = (0.5 * pre * (1.0 + tanh)).astype(BF).reshape(2, TOK, WIDE)
         slope = 0.5 * (1.0 + tanh) + 0.5 * pre * (1.0 - tanh * tanh) * (
             0.7978845608028654 * (1.0 + 0.134145 * square)
         )
-        d_pre = (nn(rows_of(r.call), hidden(SHARD)) * slope).astype(BF)
-        d_second = nt(d_pre, hidden(0)).astype(BF)
-        for i, b in enumerate(blocks):
-            at = slice(TOK * i, TOK * i + TOK)
-            r.active[b] = active[at]
-            r.dpre[b] = d_pre[at]
-            (r.dsec_send if (step, i) != (1, 1) else r.dsec)[b] = d_second[at]
-        send_along("dsec", lambda z: r.dsec_send.at[z], ((2, 1), (3,))[step])
+        cot = r.call[rows]
+        d_pre = (nn(cot.reshape(2 * TOK, D), hidden(SHARD)) * slope).astype(BF)
+        r.dpre[rows] = d_pre.reshape(2, TOK, WIDE)
+        d_second = nt(d_pre, hidden(0))
+        sums2.append((col_sums(d_second * n2), col_sums(d_second)))
+        d_middle = norm_back(d_second, gain2, n2, rstd2)
+        d_branch = []
+        for i in range(2):
+            own = jnp.where(me.z == 2 * pair + i, cot[i].astype(F32), 0.0) + d_middle[TOK * i : TOK * i + TOK]
+            r.dmid[2 * pair + i] = own
+            d_branch.append(own.astype(BF))
+            r.dbr[2 * pair + i] = d_branch[-1]
+        d_att = nt(jnp.concatenate(d_branch, axis=0), merge).astype(BF)
+        low, high = d_att[0:TOK], d_att[TOK : 2 * TOK]
+        for z in range(4):
+            at = 192 * z
+            r.do_send[pair, z, 0] = low[:, at : at + 128]
+            r.do_send[pair, z, 1] = high[:, at : at + 128]
+            r.do_send[pair, z, 2] = lanes(low[:, at + 128 : at + 192], high[:, at + 128 : at + 192])
+        for d in (1, 3, 2):
+            to = shifted(me, "z", d)
+            copy_to(to, r.do_send.at[pair, to.z], r.do_recv.at[pair, me.z], "do", recv=("do", pair)).start()
+        r.do_recv[pair, me.z] = r.do_send[pair, me.z]
+    sent(r.do_send.at[:, 0:3], "do")
+
+    zeros = jnp.zeros((TOK, 32), BF)
+
+    for b in range(4):
+        r.attt[:, TOK * b : TOK * b + TOK] = turned(r.att[b])
+    grad = nn(r.attt[...], r.dbr[...].reshape(4 * TOK, D)).astype(BF)
+    r.m_g[...] = grad.reshape(2, 4, 2, 48, D)
+    copy_to(sib, r.m_g.at[:, :, 1 - me.c], r.m_r0, "merge", "pair").start()
+    sent(r.m_r0, "merge", "pair")
 
     sums = col_sums(r.dpre[...].reshape(4 * TOK, WIDE))
     r.vg[...] = jnp.zeros((8, 16, TOK), F32)
@@ -481,20 +486,27 @@
             r.vg[2 * me.z + yl, EXPAND_BIAS + k : EXPAND_BIAS + k + 1, :] = sums[:, at : at + TOK]
     for b in range(4):
         r.secondt[:, TOK * b : TOK * b + TOK] = turned(r.second[b])
-    shape = (2, 4, 2, 48, SHARD)
-    for first, left, right in ((0, r.secondt, r.dpre), (SHARD, r.cott, r.active)):
+    halves = ((r.g_e, r.g_e0), (r.g_s, r.g_s0))
+
+    def hidden_gradient(k, left, right):
+        ref, pair0 = halves[k]
         grad = nn(left[...], right[...].reshape(4 * TOK, WIDE)).astype(BF)
         for yl in range(2):
-            r.gz[yl, :, :, :, :, first : first + SHARD] = grad[:, SHARD * yl : SHARD * yl + SHARD].reshape(shape)
-    copy_to(sib, r.gz.at[:, :, :, 1 - me.c], r.gz0, "hidden", "pair").start()
-    sent(r.gz0, "hidden", "pair")
+            ref[yl] = grad[:, SHARD * yl : SHARD * yl + SHARD].reshape(2, 4, 2, 48, SHARD)
+        copy_to(sib, ref.at[:, :, :, 1 - me.c], pair0, "hidden", k, "pair").start()
+        sent(pair0, "hidden", k, "pair")
+
+    hidden_gradient(0, r.secondt, r.dpre)
+
+    hidden_gradient(1, r.cott, r.active)
     result = nt(r.active[...].reshape(4 * TOK, WIDE), hidden(SHARD)).astype(BF)
     for b in range(4):
         r.res_send[b] = result[TOK * b : TOK * b + TOK]
-    r.attt[...] = turned(r.att[me.z])
+    send_along("res_recv", lambda z: r.res_send.at[z])
+    r.res_recv[me.z] = r.res_send[me.z]
 
     def pair_sum(ref, own, key):
-        arrived(ref, key, "pair")
+        arrived(ref, *key, "pair")
         every = (slice(None),) * (len(ref.shape) - 2)
         ref[...] = (ref[...].astype(F32) + own[every + (me.c,)].astype(F32)).astype(BF)
 
@@ -512,53 +524,32 @@
             total += got[d].astype(F32)
         return total.astype(BF)
 
-    pair_sum(r.gz0, r.gz, "hidden")
-    for d in (1, 3, 2):
-        to = shifted(me, "y", d)
-        copy_to(to, r.gz0.at[to.yl, to.yh], r.gzy.at[d - 1], "hidden y").start()
-    sent(r.gzy, "hidden y")
-    take_along("dsec")
-
-    d_second = sum(r.dsec[b].astype(F32) for b in range(4))
-    cot = r.call[me.z].astype(F32)
-    n2, rstd2 = norm_parts(r.mid[me.z])
-    d_middle = cot + norm_back(d_second, gain2, n2, rstd2)
-    d_branch = d_middle.astype(BF)
-    r.dbr[...] = d_branch
-    zeros = jnp.zeros((TOK, 32), BF)
-    d_att = nt(d_branch, r.mc[...]).astype(BF)
-    for b in range(4):
-        o = d_att[:, 192 * b : 192 * b + 192]
-        r.do_send[b] = lanes(o[:, 0:128], jnp.zeros((TOK, 64), BF), o[:, 128:192])
-    send_along("do_recv", lambda z: r.do_send.at[z])
-    send_along("res_recv", lambda z: r.res_send.at[z])
-    r.res_recv[me.z] = r.res_send[me.z]
-    r.do_recv[me.z] = r.do_send[me.z]
-
-    r.dmid[...] = d_middle
-    send_back(r.dmid, r.dmid_recv, "dmid")
-
-    for s in range(8):
-        right = lanes(r.dbr[:, 96 * s : 96 * s + 96], zeros)
-        r.m_g[s // 2, s % 2] = nn(r.attt[...], right).astype(BF).reshape(2, 4, 2, 48, TOK)
-    copy_to(sib, r.m_g.at[:, :, :, :, 1 - me.c], r.m_r0, "merge", "pair").start()
-    sent(r.m_r0, "merge", "pair")
-
-    g_gain_b = col_sums(d_second * n2)
-    g_shift_b = col_sums(d_second)
-    g_b_shrink = col_sums(cot)
-    g_b_merge = col_sums(d_branch)
-    rows = [(MERGE_BIAS, g_b_merge), (SECOND_GAIN, g_gain_b), (SECOND_SHIFT, g_shift_b), (SHRINK_BIAS, g_b_shrink)]
-    for s in range(8):
-        for row, value in rows:
-            r.vg[s, row : row + 1, 0:96] = value[:, 96 * s : 96 * s + 96]
-
-    pair_sum(r.m_r0, r.m_g, "merge")
+    def expand_sum():
+        pair_sum(r.g_e0, r.g_e, ("hidden", 0))
+        for d in (1, 3, 2):
+            to = shifted(me, "y", d)
+            copy_to(to, r.g_e0.at[to.yl, to.yh], r.g_ey.at[d - 1], "expand y").start()
+        sent(r.g_ey, "expand y")
+
+    def shrink_sum():
+        pair_sum(r.g_s0, r.g_s, ("hidden", 1))
+        plane_send(r.g_s0, r.g_sx, "shrink")
+
+    pair_sum(r.m_r0, r.m_g, ("merge",))
     plane_send(r.m_r0, r.m_x, "merge")
-
+    expand_sum()
     r.dkv[...] = jnp.zeros((8 * TOK, SHARD), F32)
-    take_along("do_recv")
     sent(r.dkv_got, "dkv")
+
+    def take_pair(p):
+        arrived(r.do_recv.at[p, 0:3], "do", p)
+        total = r.do_recv[p, 0].astype(F32)
+        for z in range(1, 4):
+            total += r.do_recv[p, z].astype(F32)
+        r.do_all[2 * p, :, 0:TOK] = total[0].astype(BF)
+        r.do_all[2 * p, :, TOK : 2 * TOK] = lanes(total[2, :, 64:128], total[2, :, 0:64]).astype(BF)
+        r.do_all[2 * p + 1, :, 0:TOK] = total[1].astype(BF)
+        r.do_all[2 * p + 1, :, TOK : 2 * TOK] = total[2].astype(BF)
 
     def pair(l0, l1, r0, r1):
         return nn(jnp.concatenate([l0, l1], axis=1), jnp.concatenate([r0, r1], axis=0))
@@ -576,20 +567,27 @@
             r.dpad[half, b] = lanes(dq[:, at], zeros, dkv[:, at], zeros, dv[:, at], zeros)
         at = r.dpad.at[:, b]
         copy_to(sib, at, r.dpad_sib.at[:, b], "dpad").start()
-        d_first = nt(r.dpad[0, b], mixer(0, 0, 3)) + nt(r.dpad[1, b], mixer(1, 0, 3))
-        r.df_send[b] = d_first.astype(BF)
-        if b:
-            send_block(b, r.df_send.at[b])
-        gain_sum.append(col_sums(d_first * r.n1all[b]))
-        shift_sum.append(col_sums(d_first))
+
+    def first_back(p):
+        rows = slice(2 * p, 2 * p + 2)
+        d_first = nt(r.dpad[0, rows].reshape(2 * TOK, SHARD), mixer(0, 0, 3))
+        d_first += nt(r.dpad[1, rows].reshape(2 * TOK, SHARD), mixer(1, 0, 3))
+        for i in range(2):
+            b = 2 * p + i
+            part, normed = d_first[TOK * i : TOK * i + TOK], r.n1all[b]
+            gain_sum.append(col_sums(part * normed))
+            shift_sum.append(col_sums(part))
+            r.df_send[b] = (r.dmid[b] + norm_back(part, gain1, normed, r.rstd1[b][:, 0:1])).astype(BF)
 
     for b in (3, 2, 1, 0):
+        if b % 2:
+            take_pair(b // 2)
         n = 256 * (b + 1)
         allowed = allowed_of(b)
         dqs, dss, pbs, dos, qs = [], [], [], [], []
         for h in range(3):
             q = query_of(b, h)
-            do = one_head(r.do_recv[b, :, 0:128] if h < 2 else r.do_recv[b, :, 128:256], h > 0)
+            do = one_head(r.do_all[b, :, 0:128] if h < 2 else r.do_all[b, :, 128:256], h > 0)
             scores = jnp.where(allowed, nt(keys_of(b, h), q), NEG)
             probs = jnp.exp(scores - r.lse[b, h : h + 1, :])
             dw = nt(values_of(b, h), do)
@@ -608,19 +606,40 @@
         other = pl.multiple_of(256 * b + TOK * (1 - me.c), TOK)
         r.dkv_sib[b] = r.dkv[pl.ds(other, TOK), :].astype(BF)
         copy_to(sib, r.dkv_sib.at[b], r.dkv_got.at[b], "dkv", recv=("dkv", b)).start()
-        if b == 1:
-            arrived(r.gzy, "hidden y")
-            total = r.gz0[me.yl, me.yh].astype(F32)
-            for d in range(3):
-                total += r.gzy[d].astype(F32)
-            r.gzx[...] = total.astype(BF)
-            for d in (1, 3, 2):
-                to = shifted(me, "x", d)
-                copy_to(to, r.gzx.at[to.x], r.gy.at[d - 1], "hidden x").start()
-            sent(r.gy, "hidden x")
-        if b < 3:
-            finish_block(b + 1)
-    finish_block(0)
+        if b == 3:
+            shrink_sum()
+        if b == 2:
+            finish_block(3)
+        if b == 0:
+            finish_block(1)
+        if b % 2 == 0:
+            finish_block(b)
+            first_back(b // 2)
+    total = plane_total(r.m_r0, r.m_x, "merge")
+    for s in range(8):
+        for yh in range(2):
+            r.m_t[s // 2, s % 2, yh] = lanes(total[yh, :, 96 * s : 96 * s + 96], zero32)
+    for i, (dz, dy) in enumerate(around):
+        to = shifted(shifted(me, "z", dz), "y", dy)
+        copy_to(to, r.m_t.at[to.z, to.yl, to.yh], r.m_y.at[i], "merge all").start()
+    sent(r.m_y, "merge all")
+    arrived(r.g_ey, "expand y")
+    total = r.g_e0[me.yl, me.yh].astype(F32)
+    for d in range(3):
+        total += r.g_ey[d].astype(F32)
+    r.g_ex[...] = total.astype(BF)
+    for d in (1, 3, 2):
+        to = shifted(me, "x", d)
+        copy_to(to, r.g_ex.at[to.x], r.e_got.at[d - 1], "expand x").start()
+    sent(r.e_got, "expand x")
+    g_gain_b, g_shift_b = sums2[0][0] + sums2[1][0], sums2[0][1] + sums2[1][1]
+    g_b_shrink = col_sums(r.call[me.z])
+    g_b_merge = col_sums(r.dbr[...].reshape(4 * TOK, D))
+    rows = [(MERGE_BIAS, g_b_merge), (SECOND_GAIN, g_gain_b), (SECOND_SHIFT, g_shift_b), (SHRINK_BIAS, g_b_shrink)]
+    for s in range(8):
+        for row, value in rows:
+            r.vg[s, row : row + 1, 0:96] = value[:, 96 * s : 96 * s + 96]
+
     arrived(r.fallt_sib, "first")
     for half in range(2):
         sums = col_sums(r.dpad[half].reshape(4 * TOK, SHARD))
@@ -636,7 +655,8 @@
         to = seq_peer(k)
         copy_to(to, r.vg.at[to.z * 2 + to.yl], r.vr.at[k - 1], "rows").start()
     sent(r.vr, "rows")
-    send_block(0, r.df_send.at[0])
+    send_along("df_recv", lambda z: r.df_send.at[z])
+    r.df_recv[me.z] = r.df_send[me.z]
 
     arrived(r.dpad_sib, "dpad")
     sent(r.dpad, "dpad")
@@ -645,11 +665,6 @@
         right = [ref[half].reshape(4 * TOK, SHARD) for ref in (r.dpad, r.dpad_sib)]
         r.rm0[half] = nn(left, jnp.concatenate(right, axis=0)).astype(BF).reshape(2, 4, 48, SHARD)
     plane_send(r.rm0, r.rmx, "mixer")
-    r.m_t[...] = plane_total(r.m_r0, r.m_x, "merge")
-    for i, (dz, dy) in enumerate(around):
-        to = shifted(shifted(me, "z", dz), "y", dy)
-        copy_to(to, r.m_t.at[to.z, to.yl, to.yh], r.m_y.at[i], "merge all").start()
-    sent(r.m_y, "merge all")
     take_along("res_recv")
     result = r.mid[me.z] + whole(SHRINK_BIAS)
     for b in range(4):
@@ -666,6 +681,11 @@
     for at, dx, dy in others:
         copy_to(shifted(shifted(at, "x", dx), "y", dy), r.vx.at[ours], r.vx.at[ours], "rows all").start()
     sent(r.vx.at[0:15], "rows all")
+    r.g_sy[...] = plane_total(r.g_s0, r.g_sx, "shrink")
+    for d in (1, 3, 2):
+        to = shifted(me, "y", d)
+        copy_to(to, r.g_sy.at[to.yl, to.yh], r.s_got.at[d - 1], "shrink y").start()
+    sent(r.s_got, "shrink y")
     r.rmy[...] = plane_total(r.rm0, r.rmx, "mixer")
     for dyh in range(2):
         yh = lax.rem(me.yh + dyh, 2)
@@ -682,26 +702,23 @@
                     start_unless(owner == seq, to, src, dst, "piece", half, kind, recv=("piece",))
                     sent_unless(owner == seq, r.units.at[0], "piece", half, kind)
     sent(r.rmf.at[:, 0:2], "piece")
-    d_first = jnp.zeros((TOK, D), F32)
-    take_blocks()
-    for b in range(4):
-        d_first += r.df_recv[b].astype(F32)
-    arrived(r.dmid_recv, "dmid")
-    r.gin[...] = r.dmid_recv[...] + norm_back(d_first, gain1, r.n1[...], rstd1)
+    take_along("df_recv")
+    r.gin_send[...] = sum(r.df_recv[b].astype(F32) for b in range(4)).astype(BF)
+    send_back(r.gin_send, r.gin_recv, "gin")
 
     arrived(r.hid_recv, "hid")
     r.hidden[...] = r.hid_recv[...]
-    arrived(r.gy, "hidden x")
-    total = r.gzx[me.x].astype(F32)
-    for d in range(3):
-        total += r.gy[d].astype(F32)
-    r.gexp[...] = total[:, 0:SHARD]
-    r.gshr[...] = total[:, SHARD:WIDE]
+    arrived(r.e_got, "expand x")
+    r.gexp[...] = r.g_ex[me.x].astype(F32) + sum(r.e_got[d].astype(F32) for d in range(3))
+    arrived(r.s_got, "shrink y")
+    r.gshr[...] = r.g_sy[me.yl, me.yh].astype(F32) + sum(r.s_got[d].astype(F32) for d in range(3))
     arrived(r.m_y, "merge all")
     total = r.m_t[me.z, me.yl, me.yh].astype(F32)
     for i in range(15):
         total += r.m_y[i].astype(F32)
     r.gmerge[...] = total[:, 0:96]
+    arrived(r.gin_recv, "gin")
+    r.gin[...] = r.gin_recv[...].astype(F32)
     arrived(r.vx.at[0:15], "rows all")
     total = r.vx[0]
     for k in range(1, 16):
@@ -723,18 +740,24 @@
     v, dma = pltpu.VMEM, pltpu.SemaphoreType.DMA
     blocks = (2, 4, 2, 48)
     s = dict(
-        m_w=v((4, 2) + blocks + (TOK,), BF),
-        m_g=v((4, 2) + blocks + (TOK,), BF),
-        m_r0=v((4, 2, 2, 4, 48, TOK), BF),
-        m_x=v((3, 4, 2, 2, 48, TOK), BF),
+        m_w=v((4, 2, 2, 48, TOK), BF),
+        m_g=v(blocks + (D,), BF),
+        m_r0=v((2, 4, 48, D), BF),
+        m_x=v((3, 2, 48, D), BF),
         m_t=v((4, 2, 2, 48, TOK), BF),
         m_y=v((15, 48, TOK), BF),
-        mc=v((D, D), BF),
+        mc=v(blocks + (D,), BF),
         wz=v((2,) + blocks + (WIDE,), BF),
-        gz=v((2,) + blocks + (WIDE,), BF),
-        gz0=v((2, 2, 4, 48, WIDE), BF),
-        gzx=v((4, 48, WIDE), BF),
-        gzy=v((3, 4, 48, WIDE), BF),
+        g_e=v((2,) + blocks + (SHARD,), BF),
+        g_s=v((2,) + blocks + (SHARD,), BF),
+        g_e0=v((2, 2, 4, 48, SHARD), BF),
+        g_s0=v((2, 2, 4, 48, SHARD), BF),
+        g_ey=v((3, 4, 48, SHARD), BF),
+        g_ex=v((4, 48, SHARD), BF),
+        g_sx=v((3, 2, 2, 48, SHARD), BF),
+        g_sy=v((2, 2, 48, SHARD), BF),
+        e_got=v((3, 48, SHARD), BF),
+        s_got=v((3, 48, SHARD), BF),
         gy=v((3, 48, WIDE), BF),
         units=v((3, 48, TOK), BF),
         wm=v((2,) + blocks + (SHARD,), BF),
@@ -748,7 +771,9 @@
         fallt_sib=v((8, 48, 4 * TOK), BF),
         cott=v((D, 4 * TOK), BF),
         secondt=v((D, 4 * TOK), BF),
-        attt=v((D, TOK), BF),
+        attt=v((D, 4 * TOK), BF),
+        rstd1=v((4, TOK, TOK), F32),
+        dmid=v((4, TOK, D), F32),
         q_all=v((4, TOK, 256), BF),
         kv_all=v((4, 2, TOK, SHARD), BF),
         kvt=v((SHARD, 8 * TOK), BF),
@@ -760,18 +785,17 @@
         dq=v((4, TOK, 256), BF),
         dpad=v((2, 4, TOK, SHARD), BF),
         dpad_sib=v((2, 4, TOK, SHARD), BF),
-        do_send=v((4, TOK, 256), BF),
-        do_recv=v((4, TOK, 256), BF),
+        do_send=v((2, 4, 3, TOK, TOK), BF),
+        do_recv=v((2, 4, 3, TOK, TOK), BF),
+        do_all=v((4, TOK, 256), BF),
         n1all=v((4, TOK, D), F32),
         mid=v((4, TOK, D), F32),
     )
-    for name in ("xall", "call", "fall", "att", "second", "dsec_send", "dsec", "res_send", "res_recv", "df_send", "df_recv"):
+    for name in ("xall", "call", "fall", "att", "second", "dbr", "res_send", "res_recv", "df_send", "df_recv"):
         s[name] = v((4, TOK, D), BF)
     for name in ("active", "dpre"):
         s[name] = v((4, TOK, WIDE), BF)
-    for name in ("n1", "dmid", "dmid_recv"):
-        s[name] = v((TOK, D), F32)
-    for name in ("dbr", "hid", "hid_recv"):
+    for name in ("hid", "hid_recv", "gin_send", "gin_recv"):
         s[name] = v((TOK, D), BF)
     for name, count in (("vg", 8), ("vr", 7), ("vx", 16)):
         s[name] = v((count, 16, TOK), F32)

time: 95.1 us -> 85.4 us (0.90)
  Pallas kernels: 94.1 us -> 84.5 us
    pallas_call x1, Pallas kernels: 92 us -> 82.3 us  [body(): pl.pallas_call(functools.partial(kernel, IN + OUT + tuple(scratch)), out_...]
where the time goes in v4:
time: 85.4 us; the launch traced here: 85.3 us
  Pallas kernels  84.5 us (99%)
    pallas_call x1, Pallas kernels, body(): pl.pallas_call(functools.partial(kernel, IN + OUT + tuple(scratch)), out_...  82.3 us
    pallas_call x1, Pallas kernels, body(): pl.pallas_call(finish, out_shape=held + vectors, in_specs=[vmem] * 7, out...  2.13 us

profile of v4, /device:TPU:1, one launch (start us, length us, event | category | flops | bytes accessed | tf_op | source)
XLA Modules:
  0.0 85.3 jit_solution(7954583430520681779)
XLA Ops:
  0.7 82.3 %shard_map.254 = (bf16[128,768]{1,0:T(8,128)(2,1)}, f32[128,768]{1,0:T(8,128)}, f32[48,288]{1,0:T(8,128)}, f32[48,96]{1,0:T(8,128)}, f32[48,384]{1,0:T(8,128)}, /*index=5*/f32[48,384]{1,0:T(8,128)}, f32[16,128]{1,0:T(8,128)}) custom-call(bf16[128,768]{1,0:T(8,128)(2,1)} %bitcast.7, bf16[128,768]{1,0:T(8,128)(2,1)} %bitcast.8, s32[8,128]{1,0:T(8,128)} %bitcast.10, ...), custom_call_target="tpu_custom_call" | custom-call | tf_op jit(solution)/shard_map/pallas_call | solution.py:825
  83.0 2.1 %shard_map.255 = (bf16[128,768]{1,0:T(8,128)(2,1)}, f32[128,768]{1,0:T(8,128)}, f32[48,288]{1,0:T(8,128)}, f32[48,96]{1,0:T(8,128)}, f32[48,384]{1,0:T(8,128)}, ...) custom-call(bf16[128,768]{1,0:T(8,128)(2,1)} %get-tuple-element.35.h, ...), custom_call_target="tpu_custom_call" | custom-call | tf_op jit(solution)/shard_map/pallas_call | solution.py:840

commit v5 on v4

--- a/solution.py
+++ b/solution.py
@@ -13,13 +13,14 @@
 HD = 64
 TOK = 128
 SHARD = 384
+HEADS3 = 640
 WIDE = 768
 EPS = 1e-05
 NEG = -1e30
 MESH = pl.DeviceIdType.MESH
 BF = jnp.bfloat16
 F32 = jnp.float32
-SENDS, RECVS = 47, 49
+SENDS, RECVS = 48, 50
 FIRST_GAIN, FIRST_SHIFT, MIXER_BIAS, MERGE_BIAS, SECOND_GAIN, SECOND_SHIFT, SHRINK_BIAS, EXPAND_BIAS = 0, 1, 2, 4, 5, 6, 7, 8
 
 
@@ -195,13 +196,13 @@
         sent(getattr(r, name).at[0:3], name)
 
     def send_back(src, dst, key):
-        start_unless(here, swap, src, dst, key)
-        sent_unless(here, src, key)
+        start_unless(here, swap, src, dst, *key)
+        sent_unless(here, src, *key)
 
     for i in range(3):
         u = 3 * seq + i
         group = lax.div(lax.rem(u, 8), 2)
-        dst = r.wm.at[lax.rem(u, 2), me.yh, me.x, me.c, :, tile(lax.div(u, 8))]
+        dst = r.wl.at[lax.rem(u, 2), me.yh, lax.div(u, 8)]
         for dy in range(4):
             y = lax.rem(ypos + dy, 4)
             to = moved(me, z=group, yh=lax.div(y, 2), yl=lax.rem(y, 2))
@@ -212,13 +213,6 @@
         sent_unless(group == me.z, r.units.at[i], "unit", i)
     sent(r.rmf.at[:, 0:3], "unit")
 
-    send_back(r.x_in, r.xall.at[me.z], "x")
-
-    @pl.when(here)
-    def _():
-        arrived(r.xall.at[0], "x")
-        send_own("xall")
-
     def seq_peer(k):
         at = shifted(me, "z", k // 2)
         return moved(at, yl=1 - me.yl) if k % 2 else at
@@ -226,6 +220,23 @@
     for k in range(1, 8):
         copy_to(seq_peer(k), r.vecs.at[seq], r.vecs.at[seq], "vec").start()
     sent(r.vr, "vec")
+    def upper(ref, h):
+        return ref.at[pl.ds(64 * h, 64)]
+
+    for h in range(2):
+        send_back(upper(r.x_in, h), upper(r.xall.at[me.z], h), ("x", h))
+
+    def x_along(h):
+        arrived(upper(r.xall.at[0], 0), "x", h)
+        at = upper(r.xall.at[me.z], h)
+        for d in (1, 3, 2):
+            copy_to(shifted(me, "z", d), at, at, "xall").start()
+
+    @pl.when(here)
+    def _():
+        x_along(0)
+        x_along(1)
+
 
     def plane(ref, d):
         return ref.at[(slice(None),) * (len(ref.shape) - 4) + (lax.rem(me.x + 4 - d, 4), me.c)]
@@ -279,14 +290,17 @@
     for dz, dy in around:
         copy_to(shifted(shifted(me, "z", dz), "y", dy), at, at, "merge").start()
     sent(r.m_y, "merge")
-    send_back(r.cot_in, r.call.at[me.z], "cot")
-    arrived(r.wm.at[:, :, me.x, me.c], "unit")
+    send_back(r.cot_in, r.call.at[me.z], ("cot",))
+    arrived(r.wl, "unit")
+    for yh in range(2):
+        pieces = [r.wl[half, yh, kind, :, 0:96] for kind in (1, 2, 0) for half in range(2)]
+        r.wm[yh, me.x, me.c] = lanes(*pieces, jnp.zeros((48, 64), BF))
 
     plane_start(r.wm, "mixer")
     @pl.when(jnp.logical_not(here))
     def _():
-        arrived(r.xall.at[0], "x")
-        send_own("xall")
+        x_along(0)
+        x_along(1)
 
     arrived(r.gy, "hidden")
     column_start()
@@ -318,9 +332,8 @@
     at = r.fallt.at[:, 1 - me.c]
     copy_to(sib, at, r.fallt_sib, "first").start()
     sent(r.fallt_sib, "first")
-    def mixer(half, first, count):
-        at = slice(TOK * first, TOK * (first + count))
-        return r.wm[half, :, :, :, :, at].reshape(D, TOK * count)
+    def mixer(at):
+        return r.wm[:, :, :, :, at].reshape(D, -1)
 
     first = r.fall[...].reshape(4 * TOK, D)
 
@@ -328,10 +341,10 @@
         row = MIXER_BIAS + half
         return r.vecs[at, row : row + 1, 0:96]
 
-    kv0, kv1 = nn(first, mixer(0, 1, 2)), nn(first, mixer(1, 1, 2))
-    keys = lanes(kv0[:, 0:96], kv1[:, 0:96]).astype(BF)
+    kv = nn(first, mixer(slice(0, 384)))
+    keys = kv[:, 0:192].astype(BF)
     vbias = lanes(mixer_bias(4 + me.z, 0), mixer_bias(4 + me.z, 1))
-    values = (lanes(kv0[:, 128:224], kv1[:, 128:224]) + vbias).astype(BF)
+    values = (kv[:, 192:384] + vbias).astype(BF)
     packed = lanes(keys, values[:, 128:192], values[:, 0:128])
     for b in range(4):
         r.kv_all[b, me.c] = packed[TOK * b : TOK * b + TOK]
@@ -339,7 +352,7 @@
     copy_to(sib, at, at, "kv").start()
     sent(at, "kv")
     qbias = lanes(mixer_bias(me.z, 0), mixer_bias(me.z, 1))
-    q = lanes(nn(first, mixer(0, 0, 1))[:, 0:96], nn(first, mixer(1, 0, 1))[:, 0:96])
+    q = nn(first, mixer(slice(384, HEADS3)))[:, 0:192]
     q = (q + qbias).astype(BF) * jnp.asarray(0.125, BF)
     q = lanes(q, jnp.zeros((4 * TOK, 64), BF))
     for b in range(4):
@@ -528,12 +541,40 @@
         pair_sum(r.g_e0, r.g_e, ("hidden", 0))
         for d in (1, 3, 2):
             to = shifted(me, "y", d)
-            copy_to(to, r.g_e0.at[to.yl, to.yh], r.g_ey.at[d - 1], "expand y").start()
-        sent(r.g_ey, "expand y")
+            copy_to(to, r.g_e0.at[to.yl, to.yh], r.g_y.at[d - 1], "expand y").start()
+        sent(r.g_y, "expand y")
+
+    def expand_next():
+        arrived(r.g_y, "expand y")
+        total = r.g_e0[me.yl, me.yh].astype(F32)
+        for d in range(3):
+            total += r.g_y[d].astype(F32)
+        r.g_ex[...] = total.astype(BF)
+        for d in (1, 3, 2):
+            to = shifted(me, "x", d)
+            copy_to(to, r.g_ex.at[to.x], r.g_got.at[0, d - 1], "expand x").start()
+        sent(r.g_got.at[0], "expand x")
 
     def shrink_sum():
         pair_sum(r.g_s0, r.g_s, ("hidden", 1))
-        plane_send(r.g_s0, r.g_sx, "shrink")
+        plane_send(r.g_s0, r.g_x, "shrink")
+
+    def shrink_next():
+        r.g_sy[...] = plane_total(r.g_s0, r.g_x, "shrink")
+        for d in (1, 3, 2):
+            to = shifted(me, "y", d)
+            copy_to(to, r.g_sy.at[to.yl, to.yh], r.g_got.at[1, d - 1], "shrink y").start()
+        sent(r.g_got.at[1], "shrink y")
+
+    def merge_next():
+        total = plane_total(r.m_r0, r.m_x, "merge")
+        for s in range(8):
+            for yh in range(2):
+                r.m_t[s // 2, s % 2, yh] = lanes(total[yh, :, 96 * s : 96 * s + 96], zero32)
+        for i, (dz, dy) in enumerate(around):
+            to = shifted(shifted(me, "z", dz), "y", dy)
+            copy_to(to, r.m_t.at[to.z, to.yl, to.yh], r.m_y.at[i], "merge all").start()
+        sent(r.m_y, "merge all")
 
     pair_sum(r.m_r0, r.m_g, ("merge",))
     plane_send(r.m_r0, r.m_x, "merge")
@@ -561,19 +602,14 @@
         own = pl.multiple_of(256 * b + TOK * me.c, TOK)
         dkv = (r.dkv[pl.ds(own, TOK), :] + r.dkv_got[b].astype(F32)).astype(BF)
         dq = r.dq[b]
-        dv = lanes(dkv[:, 256:384], dkv[:, 192:256])
-        for half in range(2):
-            at = slice(96 * half, 96 * half + 96)
-            r.dpad[half, b] = lanes(dq[:, at], zeros, dkv[:, at], zeros, dv[:, at], zeros)
-        at = r.dpad.at[:, b]
-        copy_to(sib, at, r.dpad_sib.at[:, b], "dpad").start()
-
-    def first_back(p):
-        rows = slice(2 * p, 2 * p + 2)
-        d_first = nt(r.dpad[0, rows].reshape(2 * TOK, SHARD), mixer(0, 0, 3))
-        d_first += nt(r.dpad[1, rows].reshape(2 * TOK, SHARD), mixer(1, 0, 3))
-        for i in range(2):
-            b = 2 * p + i
+        r.dpad[b] = lanes(dkv[:, 0:192], dkv[:, 256:384], dkv[:, 192:256], dq[:, 0:192], jnp.zeros((TOK, 64), BF))
+        at = r.dpad.at[b]
+        copy_to(sib, at, r.dpad_sib.at[b], "dpad").start()
+
+    def first_back(blocks):
+        rows = jnp.concatenate([r.dpad[b] for b in blocks], axis=0)
+        d_first = nt(rows, mixer(slice(0, HEADS3)))
+        for i, b in enumerate(blocks):
             part, normed = d_first[TOK * i : TOK * i + TOK], r.n1all[b]
             gain_sum.append(col_sums(part * normed))
             shift_sum.append(col_sums(part))
@@ -608,30 +644,12 @@
         copy_to(sib, r.dkv_sib.at[b], r.dkv_got.at[b], "dkv", recv=("dkv", b)).start()
         if b == 3:
             shrink_sum()
-        if b == 2:
-            finish_block(3)
-        if b == 0:
-            finish_block(1)
-        if b % 2 == 0:
-            finish_block(b)
-            first_back(b // 2)
-    total = plane_total(r.m_r0, r.m_x, "merge")
-    for s in range(8):
-        for yh in range(2):
-            r.m_t[s // 2, s % 2, yh] = lanes(total[yh, :, 96 * s : 96 * s + 96], zero32)
-    for i, (dz, dy) in enumerate(around):
-        to = shifted(shifted(me, "z", dz), "y", dy)
-        copy_to(to, r.m_t.at[to.z, to.yl, to.yh], r.m_y.at[i], "merge all").start()
-    sent(r.m_y, "merge all")
-    arrived(r.g_ey, "expand y")
-    total = r.g_e0[me.yl, me.yh].astype(F32)
-    for d in range(3):
-        total += r.g_ey[d].astype(F32)
-    r.g_ex[...] = total.astype(BF)
-    for d in (1, 3, 2):
-        to = shifted(me, "x", d)
-        copy_to(to, r.g_ex.at[to.x], r.e_got.at[d - 1], "expand x").start()
-    sent(r.e_got, "expand x")
+        if b in (2, 1):
+            finish_block(b + 1)
+    finish_block(1)
+    first_back((3, 1))
+    finish_block(0)
+    first_back((2, 0))
     g_gain_b, g_shift_b = sums2[0][0] + sums2[1][0], sums2[0][1] + sums2[1][1]
     g_b_shrink = col_sums(r.call[me.z])
     g_b_merge = col_sums(r.dbr[...].reshape(4 * TOK, D))
@@ -641,11 +659,11 @@
             r.vg[s, row : row + 1, 0:96] = value[:, 96 * s : 96 * s + 96]
 
     arrived(r.fallt_sib, "first")
+    sums = col_sums(r.dpad[...].reshape(4 * TOK, HEADS3))
     for half in range(2):
-        sums = col_sums(r.dpad[half].reshape(4 * TOK, SHARD))
         row = MIXER_BIAS + half
-        r.vg[me.z, row : row + 1, 0:96] = sums[:, 0:96]
-        r.vg[4 + me.z, row : row + 1, 0:96] = sums[:, 256:352]
+        r.vg[me.z, row : row + 1, 0:96] = sums[:, 384 + 96 * half : 480 + 96 * half]
+        r.vg[4 + me.z, row : row + 1, 0:96] = sums[:, 192 + 96 * half : 288 + 96 * half]
     gain_a, shift_a = sum(gain_sum), sum(shift_sum)
     for s in range(8):
         r.vg[s, FIRST_GAIN : FIRST_GAIN + 1, 0:96] = gain_a[:, 96 * s : 96 * s + 96]
@@ -661,16 +679,17 @@
     arrived(r.dpad_sib, "dpad")
     sent(r.dpad, "dpad")
     left = jnp.concatenate([r.fallt[:, me.c].reshape(D // 2, 4 * TOK), r.fallt_sib[...].reshape(D // 2, 4 * TOK)], axis=1)
-    for half in range(2):
-        right = [ref[half].reshape(4 * TOK, SHARD) for ref in (r.dpad, r.dpad_sib)]
-        r.rm0[half] = nn(left, jnp.concatenate(right, axis=0)).astype(BF).reshape(2, 4, 48, SHARD)
+    right = jnp.concatenate([ref[...].reshape(4 * TOK, HEADS3) for ref in (r.dpad, r.dpad_sib)], axis=0)
+    r.rm0[...] = nn(left, right).astype(BF).reshape(2, 4, 48, HEADS3)
     plane_send(r.rm0, r.rmx, "mixer")
     take_along("res_recv")
     result = r.mid[me.z] + whole(SHRINK_BIAS)
     for b in range(4):
         result += r.res_recv[b].astype(F32)
     r.hid[...] = result.astype(BF)
-    send_back(r.hid, r.hid_recv, "hid")
+    send_back(r.hid, r.hid_recv, ("hid",))
+    expand_next()
+    merge_next()
     arrived(r.vr, "rows")
     total = r.vg[seq]
     for k in range(7):
@@ -681,12 +700,13 @@
     for at, dx, dy in others:
         copy_to(shifted(shifted(at, "x", dx), "y", dy), r.vx.at[ours], r.vx.at[ours], "rows all").start()
     sent(r.vx.at[0:15], "rows all")
-    r.g_sy[...] = plane_total(r.g_s0, r.g_sx, "shrink")
-    for d in (1, 3, 2):
-        to = shifted(me, "y", d)
-        copy_to(to, r.g_sy.at[to.yl, to.yh], r.s_got.at[d - 1], "shrink y").start()
-    sent(r.s_got, "shrink y")
-    r.rmy[...] = plane_total(r.rm0, r.rmx, "mixer")
+    shrink_next()
+    total = plane_total(r.rm0, r.rmx, "mixer")
+    for half in range(2):
+        for yh in range(2):
+            for kind in range(3):
+                at = (384, 0, 192)[kind] + 96 * half
+                r.rmy[half, yh, kind] = lanes(total[yh, :, at : at + 96], zero32)
     for dyh in range(2):
         yh = lax.rem(me.yh + dyh, 2)
         for half in range(2):
@@ -694,7 +714,7 @@
                 u = 8 * kind + 2 * me.z + half
                 owner = lax.div(u, 3)
                 to = moved(me, yh=yh, z=lax.div(owner, 2), yl=lax.rem(owner, 2))
-                src = r.rmy.at[half, yh, :, pl.ds(TOK * kind, TOK)]
+                src = r.rmy.at[half, yh, kind]
                 dst = r.rmf.at[lax.rem(u, 3), ypos]
                 if dyh:
                     copy_to(to, src, dst, "piece").start()
@@ -704,14 +724,14 @@
     sent(r.rmf.at[:, 0:2], "piece")
     take_along("df_recv")
     r.gin_send[...] = sum(r.df_recv[b].astype(F32) for b in range(4)).astype(BF)
-    send_back(r.gin_send, r.gin_recv, "gin")
+    send_back(r.gin_send, r.gin_recv, ("gin",))
 
     arrived(r.hid_recv, "hid")
     r.hidden[...] = r.hid_recv[...]
-    arrived(r.e_got, "expand x")
-    r.gexp[...] = r.g_ex[me.x].astype(F32) + sum(r.e_got[d].astype(F32) for d in range(3))
-    arrived(r.s_got, "shrink y")
-    r.gshr[...] = r.g_sy[me.yl, me.yh].astype(F32) + sum(r.s_got[d].astype(F32) for d in range(3))
+    arrived(r.g_got.at[0], "expand x")
+    r.gexp[...] = r.g_ex[me.x].astype(F32) + sum(r.g_got[0, d].astype(F32) for d in range(3))
+    arrived(r.g_got.at[1], "shrink y")
+    r.gshr[...] = r.g_sy[me.yl, me.yh].astype(F32) + sum(r.g_got[1, d].astype(F32) for d in range(3))
     arrived(r.m_y, "merge all")
     total = r.m_t[me.z, me.yl, me.yh].astype(F32)
     for i in range(15):
@@ -752,18 +772,18 @@
         g_s=v((2,) + blocks + (SHARD,), BF),
         g_e0=v((2, 2, 4, 48, SHARD), BF),
         g_s0=v((2, 2, 4, 48, SHARD), BF),
-        g_ey=v((3, 4, 48, SHARD), BF),
+        g_y=v((3, 4, 48, SHARD), BF),
+        g_x=v((3, 2, 2, 48, SHARD), BF),
         g_ex=v((4, 48, SHARD), BF),
-        g_sx=v((3, 2, 2, 48, SHARD), BF),
         g_sy=v((2, 2, 48, SHARD), BF),
-        e_got=v((3, 48, SHARD), BF),
-        s_got=v((3, 48, SHARD), BF),
+        g_got=v((2, 3, 48, SHARD), BF),
         gy=v((3, 48, WIDE), BF),
         units=v((3, 48, TOK), BF),
-        wm=v((2,) + blocks + (SHARD,), BF),
-        rm0=v((2, 2, 4, 48, SHARD), BF),
-        rmx=v((3, 2, 2, 48, SHARD), BF),
-        rmy=v((2, 2, 48, SHARD), BF),
+        wl=v((2, 2, 3, 48, TOK), BF),
+        wm=v(blocks + (HEADS3,), BF),
+        rm0=v((2, 4, 48, HEADS3), BF),
+        rmx=v((3, 2, 48, HEADS3), BF),
+        rmy=v((2, 2, 3, 48, TOK), BF),
         rmf=v((3, 4, 48, TOK), BF),
         vecs=v((8, 16, TOK), F32),
         segs=v((2, 8, TOK), F32),
@@ -783,8 +803,8 @@
         dkv_sib=v((4, TOK, SHARD), BF),
         dkv_got=v((4, TOK, SHARD), BF),
         dq=v((4, TOK, 256), BF),
-        dpad=v((2, 4, TOK, SHARD), BF),
-        dpad_sib=v((2, 4, TOK, SHARD), BF),
+        dpad=v((4, TOK, HEADS3), BF),
+        dpad_sib=v((4, TOK, HEADS3), BF),
         do_send=v((2, 4, 3, TOK, TOK), BF),
         do_recv=v((2, 4, 3, TOK, TOK), BF),
         do_all=v((4, TOK, 256), BF),

time: 85.4 us -> 84.2 us (0.986); the launches traced: 85.3 us -> 83.1 us
  Pallas kernels: 84.5 us -> 82.3 us
    pallas_call x1, Pallas kernels: 82.3 us -> 80.2 us  [body(): pl.pallas_call(functools.partial(kernel, IN + OUT + tuple(scratch)), out_...]
where the time goes in v5:
time: 84.2 us; the launch traced here: 83.1 us
  Pallas kernels  82.3 us (98%)
    pallas_call x1, Pallas kernels, body(): pl.pallas_call(functools.partial(kernel, IN + OUT + tuple(scratch)), out_...  80.2 us
    pallas_call x1, Pallas kernels, body(): pl.pallas_call(finish, out_shape=held + vectors, in_specs=[vmem] * 7, out...  2.13 us

profile of v5, /device:TPU:1, one launch (start us, length us, event | category | flops | bytes accessed | tf_op | source)
XLA Modules:
  0.0 83.1 jit_solution(9923553441135350253)
XLA Ops:
  0.7 80.2 %shard_map.254 = (bf16[128,768]{1,0:T(8,128)(2,1)}, f32[128,768]{1,0:T(8,128)}, f32[48,288]{1,0:T(8,128)}, f32[48,96]{1,0:T(8,128)}, f32[48,384]{1,0:T(8,128)}, /*index=5*/f32[48,384]{1,0:T(8,128)}, f32[16,128]{1,0:T(8,128)}) custom-call(bf16[128,768]{1,0:T(8,128)(2,1)} %bitcast.7, bf16[128,768]{1,0:T(8,128)(2,1)} %bitcast.8, s32[8,128]{1,0:T(8,128)} %bitcast.10, ...), custom_call_target="tpu_custom_call" | custom-call | tf_op jit(solution)/shard_map/pallas_call | solution.py:845
  80.8 2.1 %shard_map.255 = (bf16[128,768]{1,0:T(8,128)(2,1)}, f32[128,768]{1,0:T(8,128)}, f32[48,288]{1,0:T(8,128)}, f32[48,96]{1,0:T(8,128)}, f32[48,384]{1,0:T(8,128)}, ...) custom-call(bf16[128,768]{1,0:T(8,128)(2,1)} %get-tuple-element.35.h, ...), custom_call_target="tpu_custom_call" | custom-call | tf_op jit(solution)/shard_map/pallas_call | solution.py:860

commit v6 on v5

--- a/solution.py
+++ b/solution.py
@@ -20,7 +20,7 @@
 MESH = pl.DeviceIdType.MESH
 BF = jnp.bfloat16
 F32 = jnp.float32
-SENDS, RECVS = 48, 50
+SENDS, RECVS = 49, 51
 FIRST_GAIN, FIRST_SHIFT, MIXER_BIAS, MERGE_BIAS, SECOND_GAIN, SECOND_SHIFT, SHRINK_BIAS, EXPAND_BIAS = 0, 1, 2, 4, 5, 6, 7, 8
 
 
@@ -673,8 +673,13 @@
         to = seq_peer(k)
         copy_to(to, r.vg.at[to.z * 2 + to.yl], r.vr.at[k - 1], "rows").start()
     sent(r.vr, "rows")
-    send_along("df_recv", lambda z: r.df_send.at[z])
-    r.df_recv[me.z] = r.df_send[me.z]
+    for d in (1, 3):
+        to = shifted(me, "z", d)
+        copy_to(to, r.df_send.at[to.z], r.df_recv.at[me.z], "near").start()
+    sent(r.df_recv.at[0:2], "near")
+    to = shifted(swap, "z", 2)
+    copy_to(to, r.df_send.at[to.z], r.gin_far, "far").start()
+    sent(r.gin_far, "far")
 
     arrived(r.dpad_sib, "dpad")
     sent(r.dpad, "dpad")
@@ -722,8 +727,9 @@
                     start_unless(owner == seq, to, src, dst, "piece", half, kind, recv=("piece",))
                     sent_unless(owner == seq, r.units.at[0], "piece", half, kind)
     sent(r.rmf.at[:, 0:2], "piece")
-    take_along("df_recv")
-    r.gin_send[...] = sum(r.df_recv[b].astype(F32) for b in range(4)).astype(BF)
+    arrived(r.df_recv.at[0:2], "near")
+    parts = [r.df_send[me.z]] + [r.df_recv[shifted(me, "z", d).z] for d in (1, 3)]
+    r.gin_send[...] = sum(part.astype(F32) for part in parts).astype(BF)
     send_back(r.gin_send, r.gin_recv, ("gin",))
 
     arrived(r.hid_recv, "hid")
@@ -738,7 +744,8 @@
         total += r.m_y[i].astype(F32)
     r.gmerge[...] = total[:, 0:96]
     arrived(r.gin_recv, "gin")
-    r.gin[...] = r.gin_recv[...].astype(F32)
+    arrived(r.gin_far, "far")
+    r.gin[...] = r.gin_recv[...].astype(F32) + r.gin_far[...].astype(F32)
     arrived(r.vx.at[0:15], "rows all")
     total = r.vx[0]
     for k in range(1, 16):
@@ -815,7 +822,7 @@
         s[name] = v((4, TOK, D), BF)
     for name in ("active", "dpre"):
         s[name] = v((4, TOK, WIDE), BF)
-    for name in ("hid", "hid_recv", "gin_send", "gin_recv"):
+    for name in ("hid", "hid_recv", "gin_send", "gin_recv", "gin_far"):
         s[name] = v((TOK, D), BF)
     for name, count in (("vg", 8), ("vr", 7), ("vx", 16)):
         s[name] = v((count, 16, TOK), F32)

time: 84.2 us -> 83.9 us (level); the launches traced: 83.1 us -> 83.7 us
  no operation moved by 1% of the time
where the time goes in v6:
time: 83.9 us; the launch traced here: 83.7 us
  Pallas kernels  82.9 us (99%)
    pallas_call x1, Pallas kernels, body(): pl.pallas_call(functools.partial(kernel, IN + OUT + tuple(scratch)), out_...  80.8 us
    pallas_call x1, Pallas kernels, body(): pl.pallas_call(finish, out_shape=held + vectors, in_specs=[vmem] * 7, out...  2.13 us

profile of v6, /device:TPU:1, one launch (start us, length us, event | category | flops | bytes accessed | tf_op | source)
XLA Modules:
  0.0 83.7 jit_solution(5003715068143039703)
XLA Ops:
  0.7 80.8 %shard_map.254 = (bf16[128,768]{1,0:T(8,128)(2,1)}, f32[128,768]{1,0:T(8,128)}, f32[48,288]{1,0:T(8,128)}, f32[48,96]{1,0:T(8,128)}, f32[48,384]{1,0:T(8,128)}, /*index=5*/f32[48,384]{1,0:T(8,128)}, f32[16,128]{1,0:T(8,128)}) custom-call(bf16[128,768]{1,0:T(8,128)(2,1)} %bitcast.7, bf16[128,768]{1,0:T(8,128)(2,1)} %bitcast.8, s32[8,128]{1,0:T(8,128)} %bitcast.10, ...), custom_call_target="tpu_custom_call" | custom-call | tf_op jit(solution)/shard_map/pallas_call | solution.py:852
  81.4 2.1 %shard_map.255 = (bf16[128,768]{1,0:T(8,128)(2,1)}, f32[128,768]{1,0:T(8,128)}, f32[48,288]{1,0:T(8,128)}, f32[48,96]{1,0:T(8,128)}, f32[48,384]{1,0:T(8,128)}, ...) custom-call(bf16[128,768]{1,0:T(8,128)(2,1)} %get-tuple-element.35.h, ...), custom_call_target="tpu_custom_call" | custom-call | tf_op jit(solution)/shard_map/pallas_call | solution.py:867

commit v7 on v6

--- a/solution.py
+++ b/solution.py
@@ -694,7 +694,6 @@
     r.hid[...] = result.astype(BF)
     send_back(r.hid, r.hid_recv, ("hid",))
     expand_next()
-    merge_next()
     arrived(r.vr, "rows")
     total = r.vg[seq]
     for k in range(7):
@@ -705,6 +704,7 @@
     for at, dx, dy in others:
         copy_to(shifted(shifted(at, "x", dx), "y", dy), r.vx.at[ours], r.vx.at[ours], "rows all").start()
     sent(r.vx.at[0:15], "rows all")
+    merge_next()
     shrink_next()
     total = plane_total(r.rm0, r.rmx, "mixer")
     for half in range(2):

time: 83.9 us -> 83.2 us (level)
  no operation moved by 1% of the time
where the time goes in v7:
time: 83.2 us; the launch traced here: 83 us
  Pallas kernels  82.2 us (99%)
    pallas_call x1, Pallas kernels, body(): pl.pallas_call(functools.partial(kernel, IN + OUT + tuple(scratch)), out_...  80 us
    pallas_call x1, Pallas kernels, body(): pl.pallas_call(finish, out_shape=held + vectors, in_specs=[vmem] * 7, out...  2.13 us

profile of v7, /device:TPU:1, one launch (start us, length us, event | category | flops | bytes accessed | tf_op | source)
XLA Modules:
  0.0 83.0 jit_solution(15352740034085762737)
XLA Ops:
  0.7 80.0 %shard_map.254 = (bf16[128,768]{1,0:T(8,128)(2,1)}, f32[128,768]{1,0:T(8,128)}, f32[48,288]{1,0:T(8,128)}, f32[48,96]{1,0:T(8,128)}, f32[48,384]{1,0:T(8,128)}, /*index=5*/f32[48,384]{1,0:T(8,128)}, f32[16,128]{1,0:T(8,128)}) custom-call(bf16[128,768]{1,0:T(8,128)(2,1)} %bitcast.7, bf16[128,768]{1,0:T(8,128)(2,1)} %bitcast.8, s32[8,128]{1,0:T(8,128)} %bitcast.10, ...), custom_call_target="tpu_custom_call" | custom-call | tf_op jit(solution)/shard_map/pallas_call | solution.py:852
  80.7 2.1 %shard_map.255 = (bf16[128,768]{1,0:T(8,128)(2,1)}, f32[128,768]{1,0:T(8,128)}, f32[48,288]{1,0:T(8,128)}, f32[48,96]{1,0:T(8,128)}, f32[48,384]{1,0:T(8,128)}, ...) custom-call(bf16[128,768]{1,0:T(8,128)(2,1)} %get-tuple-element.35.h, ...), custom_call_target="tpu_custom_call" | custom-call | tf_op jit(solution)/shard_map/pallas_call | solution.py:867

commit v8 on v7

--- a/solution.py
+++ b/solution.py
@@ -693,7 +693,6 @@
         result += r.res_recv[b].astype(F32)
     r.hid[...] = result.astype(BF)
     send_back(r.hid, r.hid_recv, ("hid",))
-    expand_next()
     arrived(r.vr, "rows")
     total = r.vg[seq]
     for k in range(7):
@@ -704,6 +703,7 @@
     for at, dx, dy in others:
         copy_to(shifted(shifted(at, "x", dx), "y", dy), r.vx.at[ours], r.vx.at[ours], "rows all").start()
     sent(r.vx.at[0:15], "rows all")
+    expand_next()
     merge_next()
     shrink_next()
     total = plane_total(r.rm0, r.rmx, "mixer")

time: 83.2 us -> 83.2 us (level)
  no operation moved by 1% of the time
where the time goes in v8:
time: 83.2 us; the launch traced here: 83 us
  Pallas kernels  82.2 us (99%)
    pallas_call x1, Pallas kernels, body(): pl.pallas_call(functools.partial(kernel, IN + OUT + tuple(scratch)), out_...  80 us
    pallas_call x1, Pallas kernels, body(): pl.pallas_call(finish, out_shape=held + vectors, in_specs=[vmem] * 7, out...  2.13 us

profile of v8, /device:TPU:1, one launch (start us, length us, event | category | flops | bytes accessed | tf_op | source)
XLA Modules:
  0.0 83.0 jit_solution(12982872528866406460)
XLA Ops:
  0.7 80.0 %shard_map.254 = (bf16[128,768]{1,0:T(8,128)(2,1)}, f32[128,768]{1,0:T(8,128)}, f32[48,288]{1,0:T(8,128)}, f32[48,96]{1,0:T(8,128)}, f32[48,384]{1,0:T(8,128)}, /*index=5*/f32[48,384]{1,0:T(8,128)}, f32[16,128]{1,0:T(8,128)}) custom-call(bf16[128,768]{1,0:T(8,128)(2,1)} %bitcast.7, bf16[128,768]{1,0:T(8,128)(2,1)} %bitcast.8, s32[8,128]{1,0:T(8,128)} %bitcast.10, ...), custom_call_target="tpu_custom_call" | custom-call | tf_op jit(solution)/shard_map/pallas_call | solution.py:852
  80.7 2.1 %shard_map.255 = (bf16[128,768]{1,0:T(8,128)(2,1)}, f32[128,768]{1,0:T(8,128)}, f32[48,288]{1,0:T(8,128)}, f32[48,96]{1,0:T(8,128)}, f32[48,384]{1,0:T(8,128)}, ...) custom-call(bf16[128,768]{1,0:T(8,128)(2,1)} %get-tuple-element.35.h, ...), custom_call_target="tpu_custom_call" | custom-call | tf_op jit(solution)/shard_map/pallas_call | solution.py:867
